TPU v7x, 1024 devices: a whole 4x4x32 slice. The times are simulated.
1024 devices in a mesh: gx: 16 (over x, y), gy: 64 (over z, core).
Axes of the slice: x: 4, y: 4, z: 32, core: 2. Of those that a mesh axis runs over, the one named last changes fastest.
Arguments:
- a_tiles: bfloat16 [32, 256, 5, 128, 128], P('gx', 'gy'), may hold values from -0.5 to 0.5
- a_links: int32 [32, 256, 4], P('gx', 'gy'), may hold values 0 or 1
- p_own: bfloat16 [32, 256, 128, 128], P('gx', 'gy'), may hold values from -0.75 to 0.75
- p_side: bfloat16 [32, 64, 2, 128, 128], P('gx', 'gy'), may hold values from -0.75 to 0.75
- p_links: int32 [32, 64, 2], P('gx', 'gy'), may hold values 0 or 1
- coarse_pick: int32 [32, 64], P('gx', 'gy'), may hold values from 0 to 3, as said below
Outputs:
- coarse: float32 [32, 64, 3, 3, 128, 128], P('gx', 'gy')
Inputs may be any that keep to these rules, and one draw needn't show every extreme that they name: `coarse_pick`: within each aligned run of 4 entries along the second dimension, the entries are a permutation of 0 to 3.
All inputs are finite; a program needn't handle non-finite values. No bound on the sum of `a_links` or of `p_links` on one device may be relied on, other than what follows from the above.
Results may differ from a plain program's by a relative error of at most 0.0029.
Values may be sent and summed in bfloat16 or wider, within the bound.
No kernel may reach another device: no remote copies, remote signals or barrier semaphores. Data moves between devices by JAX's collectives and lax.ppermute only.
A program may use at most 32 MiB of HBM per device.

v0:
```python
import jax
import jax.numpy as jnp
from jax import lax
from jax.sharding import PartitionSpec as P

RATIO = 4
GROUP = 4


def extended(block, sides, width):
    for axis, dim in sides:
        count = lax.axis_size(axis)
        forward = [(i, i + 1) for i in range(count - 1)]
        backward = [(target, source) for source, target in forward]
        low = lax.ppermute(
            lax.slice_in_dim(block, block.shape[dim] - width, None, axis=dim), axis, forward
        )
        high = lax.ppermute(lax.slice_in_dim(block, 0, width, axis=dim), axis, backward)
        block = jnp.concatenate([low, block, high], axis=dim)
    return block


def from_partner(array, axis, distance):
    return lax.ppermute(array, axis, [(i, i ^ 1 << distance) for i in range(lax.axis_size(axis))])


def slide_down(blocks, slot_axis):
    head = lax.slice_in_dim(blocks, 1, 3, axis=slot_axis)
    empty = jnp.zeros_like(lax.slice_in_dim(blocks, 0, 1, axis=slot_axis))
    return jnp.concatenate([head, empty], axis=slot_axis)


def slide_up(blocks, slot_axis):
    tail = lax.slice_in_dim(blocks, 0, 2, axis=slot_axis)
    empty = jnp.zeros_like(lax.slice_in_dim(blocks, 0, 1, axis=slot_axis))
    return jnp.concatenate([empty, tail], axis=slot_axis)


def apply_tiles(blocks, panels):
    return jnp.einsum("xjab,xjsbe->xjsae", blocks, panels, preferred_element_type=jnp.float32)


def on_device(a_tiles, a_links, p_own, p_side, p_links, coarse_pick):
    columns = p_own.shape[0]
    fine_rows = p_own.shape[1]
    my_index = lax.axis_index("gy")
    y_count = lax.axis_size("gy")
    edge_keep = jnp.stack([my_index > 0, my_index < y_count - 1]).astype(jnp.int32)
    keep_side = (p_links[:, 0, :] * edge_keep[None, :]).astype(p_side.dtype)
    side_tiles = p_side[:, 0] * keep_side[:, :, None, None]
    filler = jnp.zeros((columns, fine_rows - 1) + p_own.shape[2:], p_own.dtype)
    low_slot = jnp.concatenate([side_tiles[:, 0:1], filler], axis=1)
    high_slot = jnp.concatenate([filler, side_tiles[:, 1:2]], axis=1)
    interp = jnp.stack([low_slot, p_own, high_slot], axis=2)
    rimmed = extended(interp, (("gx", 0), ("gy", 1)), 1)
    middle = rimmed[1:-1, 1:-1]
    west_panel = rimmed[:-2, 1:-1]
    east_panel = rimmed[2:, 1:-1]
    lower_panel = rimmed[1:-1, :-2]
    upper_panel = rimmed[1:-1, 2:]
    fine_index = jnp.arange(fine_rows)
    lower_panel = jnp.where(
        (fine_index % RATIO == 0)[None, :, None, None, None],
        slide_down(lower_panel, 2),
        lower_panel,
    )
    upper_panel = jnp.where(
        (fine_index % RATIO == RATIO - 1)[None, :, None, None, None],
        slide_up(upper_panel, 2),
        upper_panel,
    )
    link_float = a_links.astype(jnp.float32)[:, :, :, None, None, None]
    centre = apply_tiles(a_tiles[:, :, 0], middle)
    centre = centre + link_float[:, :, 2] * apply_tiles(a_tiles[:, :, 3], lower_panel)
    centre = centre + link_float[:, :, 3] * apply_tiles(a_tiles[:, :, 4], upper_panel)
    western = link_float[:, :, 0] * apply_tiles(a_tiles[:, :, 1], west_panel)
    eastern = link_float[:, :, 1] * apply_tiles(a_tiles[:, :, 2], east_panel)
    product = jnp.stack([western, centre, eastern], axis=2).astype(jnp.bfloat16)
    local_terms = jnp.einsum(
        "xjrab,xjdsae->xrdsbe", middle, product, preferred_element_type=jnp.float32
    )
    empty_slot = jnp.zeros_like(local_terms[:, 0, :, :1])
    lower_part = local_terms[:, 0, :, :2]
    upper_part = local_terms[:, 2, :, 1:]
    rim_parts = extended(jnp.stack([lower_part, upper_part], axis=1), (("gy", 1),), 1)
    from_below = jnp.concatenate([rim_parts[:, 0], empty_slot], axis=2)
    from_above = jnp.concatenate([empty_slot, rim_parts[:, 3]], axis=2)
    galerkin = local_terms[:, 1] + from_below + from_above
    bit_order = (0, 1)
    stacked = galerkin[None]
    for bit_number in bit_order:
        partner = from_partner(stacked, "gy", bit_number)
        is_upper = my_index >> bit_number & 1 == 1
        stacked = jnp.where(
            is_upper,
            jnp.concatenate([partner, stacked], axis=0),
            jnp.concatenate([stacked, partner], axis=0),
        )
    picks = coarse_pick[:, 0]
    position = (picks >> bit_order[0] & 1) + 2 * (picks >> bit_order[1] & 1)
    onehot = (position[None, :] == jnp.arange(GROUP)[:, None]).astype(jnp.float32)
    coarse = jnp.sum(onehot[:, :, None, None, None, None] * stacked, axis=0)
    return coarse[:, None]


def solution(mesh):
    return jax.shard_map(
        on_device,
        mesh=mesh,
        in_specs=(
            P("gx", "gy", None, None, None),
            P("gx", "gy", None),
            P("gx", "gy", None, None),
            P("gx", "gy", None, None, None),
            P("gx", "gy", None),
            P("gx", "gy"),
        ),
        out_specs=P("gx", "gy", None, None, None, None),
        check_vma=False,
    )
```

profile of v0, /device:TPU:346, one launch (start us, length us, event | category | flops | bytes accessed | tf_op | source)
XLA Modules:
  0.0 122.2 jit_solution(16202684873095361465)
XLA Ops:
  0.0 1.0 copy.31
  1.1 0.7 multiply_convert_fusion.2
  1.9 1.1 copy.32
  3.3 3.2 %collective-permute-start = (bf16[1,4,3,128,128]{3,4,2,1,0:T(8,128)(2,1)S(1)}, bf16[1,4,3,128,128]{3,4,2,1,0:T(8,128)(2,1)S(1)}, u32[]{:S(2)}, u32[]{:S(2)}) collective-permute-start(bf16[1,4,3,128,128]{3,4,2,1,0:T(8,128)(2,1)S(1)} %get-tuple-element.15), channel_id=1, source_target_pairs={{0,64},{64,128},{128,192},{192,256},{256,320},{320,384},{384,448},... | collective-permute-start | bytes 1179656 | tf_op jit(solution)/shard_map/ppermute | solution.py:15
  6.5 2.8 %collective-permute-start.1 = (bf16[1,4,3,128,128]{3,4,2,1,0:T(8,128)(2,1)S(1)}, bf16[1,4,3,128,128]{3,4,2,1,0:T(8,128)(2,1)S(1)}, u32[]{:S(2)}, u32[]{:S(2)}) collective-permute-start(bf16[1,4,3,128,128]{3,4,2,1,0:T(8,128)(2,1)S(1)} %get-tuple-element.16), channel_id=1, source_target_pairs={{64,0},{128,64},{192,128},{256,192},{320,256},{384,320},{448,384},... | collective-permute-start | bytes 1179656 | tf_op jit(solution)/shard_map/ppermute | solution.py:18
  9.9 6.3 %collective-permute-done = bf16[1,4,3,128,128]{3,4,2,1,0:T(8,128)(2,1)S(1)} collective-permute-done((bf16[1,4,3,128,128]{3,4,2,1,0:T(8,128)(2,1)S(1)}, bf16[1,4,3,128,128]{3,4,2,1,0:T(8,128)(2,1)S(1)}, u32[]{:S(2)}, u32[]{:S(2)}) %collective-permute-start) | collective-permute-done | bytes 393248 | tf_op jit(solution)/shard_map/ppermute | solution.py:15
  16.2 4.9 %collective-permute-done.1 = bf16[1,4,3,128,128]{3,4,2,1,0:T(8,128)(2,1)S(1)} collective-permute-done((bf16[1,4,3,128,128]{3,4,2,1,0:T(8,128)(2,1)S(1)}, bf16[1,4,3,128,128]{3,4,2,1,0:T(8,128)(2,1)S(1)}, u32[]{:S(2)}, u32[]{:S(2)}) %collective-permute-start.1) | collective-permute-done | bytes 393248 | tf_op jit(solution)/shard_map/ppermute | solution.py:18
  21.2 1.9 %collective-permute-start.2 = (bf16[4,1,3,128,128]{3,4,2,1,0:T(8,128)(2,1)S(1)}, bf16[4,1,3,128,128]{3,4,2,1,0:T(8,128)(2,1)S(1)}, u32[]{:S(2)}, u32[]{:S(2)}) collective-permute-start(bf16[4,1,3,128,128]{3,4,2,1,0:T(8,128)(2,1)S(1)} %get-tuple-element.12), channel_id=1, source_target_pairs={{0,1},{1,2},{2,3},{3,4},{4,5},{5,6},{6,7},{7,8},{8,9},{9,10},{10,1... | collective-permute-start | bytes 1179656 | tf_op jit(solution)/shard_map/ppermute | solution.py:15
  23.1 3.6 %collective-permute-start.3 = (bf16[4,1,3,128,128]{3,4,2,1,0:T(8,128)(2,1)S(1)}, bf16[4,1,3,128,128]{3,4,2,1,0:T(8,128)(2,1)S(1)}, u32[]{:S(2)}, u32[]{:S(2)}) collective-permute-start(bf16[4,1,3,128,128]{3,4,2,1,0:T(8,128)(2,1)S(1)} %get-tuple-element.11), channel_id=1, source_target_pairs={{1,0},{2,1},{3,2},{4,3},{5,4},{6,5},{7,6},{8,7},{9,8},{10,9},{11,1... | collective-permute-start | bytes 1179656 | tf_op jit(solution)/shard_map/ppermute | solution.py:18
  27.5 2.8 %collective-permute-done.2 = bf16[4,1,3,128,128]{3,4,2,1,0:T(8,128)(2,1)S(1)} collective-permute-done((bf16[4,1,3,128,128]{3,4,2,1,0:T(8,128)(2,1)S(1)}, bf16[4,1,3,128,128]{3,4,2,1,0:T(8,128)(2,1)S(1)}, u32[]{:S(2)}, u32[]{:S(2)}) %collective-permute-start.2) | collective-permute-done | bytes 393248 | tf_op jit(solution)/shard_map/ppermute | solution.py:15
  30.7 1.3 %collective-permute-done.3 = bf16[4,1,3,128,128]{3,4,2,1,0:T(8,128)(2,1)S(1)} collective-permute-done((bf16[4,1,3,128,128]{3,4,2,1,0:T(8,128)(2,1)S(1)}, bf16[4,1,3,128,128]{3,4,2,1,0:T(8,128)(2,1)S(1)}, u32[]{:S(2)}, u32[]{:S(2)}) %collective-permute-start.3) | collective-permute-done | bytes 393248 | tf_op jit(solution)/shard_map/ppermute | solution.py:18
  32.1 0.8 fusion.20
  32.9 1.4 %fusion.4 = f32[2,3,3,3,128,128]{4,5,1,3,2,0:T(8,128)S(1)} fusion(bf16[2,4,3,128,128,1,1]{3,4,2,1,0,6,5:T(8,128)(2,1)S(1)} %get-tuple-element.13, bf16[2,4,1,3,128,128]{4,5,3,1,0,2:T(8,128)(2,1)S(1)} %fusion.21, bf16[2,4,1,3,128,128]{4,5,3,1,0,2:T(8,128)(2,1)S(1)} %fusion.20, bf16[2,4,1,3,128,128]{4,5,3,1,0,2:T(8,128)(2,1)S(1)} %fusion.19), kind=kOutput, calls=%fused_computation.7 | convolution fusion | flops 908328960 | bytes 6684672 | tf_op jit(solution)/shard_map/xjrab,xjdsae->xrdsbe/dot_general | solution.py:79
  34.5 4.1 %collective-permute-start.4 = (f32[2,1,3,2,128,128]{4,5,3,2,0,1:T(8,128)S(1)}, f32[2,1,3,2,128,128]{4,5,3,2,0,1:T(8,128)S(1)}, u32[]{:S(2)}, u32[]{:S(2)}) collective-permute-start(f32[2,1,3,2,128,128]{4,5,3,2,0,1:T(8,128)S(1)} %get-tuple-element.9), channel_id=1, source_target_pairs={{0,1},{1,2},{2,3},{3,4},{4,5},{5,6},{6,7},{7,8},{8,9},{9,10},{10,1... | collective-permute-start | bytes 2359304 | tf_op jit(solution)/shard_map/ppermute | solution.py:15
  38.6 1.9 %collective-permute-start.5 = (f32[2,1,3,2,128,128]{4,5,1,3,2,0:T(8,128)S(1)}, f32[2,1,3,2,128,128]{4,5,1,3,2,0:T(8,128)S(1)}, u32[]{:S(2)}, u32[]{:S(2)}) collective-permute-start(f32[2,1,3,2,128,128]{4,5,1,3,2,0:T(8,128)S(1)} %get-tuple-element.10), channel_id=1, source_target_pairs={{1,0},{2,1},{3,2},{4,3},{5,4},{6,5},{7,6},{8,7},{9,8},{10,9},{11,1... | collective-permute-start | bytes 2359304 | tf_op jit(solution)/shard_map/ppermute | solution.py:18
  40.5 7.4 %collective-permute-done.4 = f32[2,1,3,2,128,128]{4,5,3,2,0,1:T(8,128)S(1)} collective-permute-done((f32[2,1,3,2,128,128]{4,5,3,2,0,1:T(8,128)S(1)}, f32[2,1,3,2,128,128]{4,5,3,2,0,1:T(8,128)S(1)}, u32[]{:S(2)}, u32[]{:S(2)}) %collective-permute-start.4) | collective-permute-done | bytes 786464 | tf_op jit(solution)/shard_map/ppermute | solution.py:15
  47.9 2.0 %collective-permute-done.5 = f32[2,1,3,2,128,128]{4,5,1,3,2,0:T(8,128)S(1)} collective-permute-done((f32[2,1,3,2,128,128]{4,5,1,3,2,0:T(8,128)S(1)}, f32[2,1,3,2,128,128]{4,5,1,3,2,0:T(8,128)S(1)}, u32[]{:S(2)}, u32[]{:S(2)}) %collective-permute-start.5) | collective-permute-done | bytes 786464 | tf_op jit(solution)/shard_map/ppermute | solution.py:18
  50.2 6.5 %collective-permute-start.6 = (f32[1,2,3,3,128,128]{4,5,3,2,1,0:T(8,128)S(1)}, f32[1,2,3,3,128,128]{4,5,3,2,1,0:T(8,128)}, u32[]{:S(2)}, u32[]{:S(2)}) collective-permute-start(f32[1,2,3,3,128,128]{4,5,3,2,1,0:T(8,128)S(1)} %fusion.24), channel_id=1, source_target_pairs={{0,1},{1,0},{2,3},{3,2},{4,5},{5,4},{6,7},{7,6},{8,9},{9,8},{10,11... | collective-permute-start | bytes 3538952 | tf_op jit(solution)/shard_map/ppermute | solution.py:24
  56.7 2.6 %collective-permute-done.6 = f32[1,2,3,3,128,128]{4,5,3,2,1,0:T(8,128)} collective-permute-done((f32[1,2,3,3,128,128]{4,5,3,2,1,0:T(8,128)S(1)}, f32[1,2,3,3,128,128]{4,5,3,2,1,0:T(8,128)}, u32[]{:S(2)}, u32[]{:S(2)}) %collective-permute-start.6) | collective-permute-done | bytes 1179680 | tf_op jit(solution)/shard_map/ppermute | solution.py:24
  59.3 1.8 %maximum_select_fusion.1 = f32[2,2,3,3,128,128]{4,5,3,2,1,0:T(8,128)S(1)} fusion(f32[1,2,3,3,128,128]{4,5,3,2,1,0:T(8,128)S(1)} %fusion.24, f32[1,2,3,3,128,128]{4,5,3,2,1,0:T(8,128)} %collective-permute-done.6, pred[]{:T(512)S(6)} %eq.44), kind=kLoop, calls=%fused_computation.4 | loop fusion | flops 1769472 | bytes 4718593 | tf_op jit(solution)/shard_map/jit(_where)/select_n | solution.py:94
  61.1 4.8 %collective-permute-start.7 = (f32[2,2,3,3,128,128]{4,5,3,2,1,0:T(8,128)S(1)}, f32[2,2,3,3,128,128]{4,5,3,2,1,0:T(8,128)}, u32[]{:S(2)}, u32[]{:S(2)}) collective-permute-start(f32[2,2,3,3,128,128]{4,5,3,2,1,0:T(8,128)S(1)} %maximum_select_fusion.1), channel_id=1, source_target_pairs={{0,2},{1,3},{2,0},{3,1},{4,6},{5,7},{6,4},{7,5},{8,10},{9,11},{10,... | collective-permute-start | bytes 7077896 | tf_op jit(solution)/shard_map/ppermute | solution.py:24
  65.9 51.8 %collective-permute-done.7 = f32[2,2,3,3,128,128]{4,5,3,2,1,0:T(8,128)} collective-permute-done((f32[2,2,3,3,128,128]{4,5,3,2,1,0:T(8,128)S(1)}, f32[2,2,3,3,128,128]{4,5,3,2,1,0:T(8,128)}, u32[]{:S(2)}, u32[]{:S(2)}) %collective-permute-start.7) | collective-permute-done | bytes 2359328 | tf_op jit(solution)/shard_map/ppermute | solution.py:24
  117.8 3.1 %fusion.1 = f32[2,3,3,128,128]{3,4,2,1,0:T(8,128)S(1)} fusion(f32[2,2,3,3,128,128]{4,5,3,2,1,0:T(8,128)S(1)} %maximum_select_fusion.1, f32[2,2,3,3,128,128]{4,5,3,2,1,0:T(8,128)} %collective-permute-done.7, f32[4,2]{1,0:T(4,128)S(1)} %fusion.96, pred[]{:T(512)S(6)} %eq.43), kind=kLoop, calls=%fused_computation.2 | loop fusion | flops 5603328 | bytes 5898273 | tf_op jit(solution)/shard_map/reduce_sum | solution.py:102
  120.8 1.4 %copy.43 = f32[2,1,3,3,128,128]{5,4,3,2,1,0:T(8,128)} copy(f32[2,1,3,3,128,128]{4,5,3,2,0,1:T(8,128)S(1)} %bitcast.96) | data formatting | bytes 2359296 | tf_op jit(solution)/shard_map/broadcast_in_dim | solution.py:103
  (25 shorter events, 2.6 us)
Async XLA Ops:
  3.1 6.2 %copy-start.1 = (s32[2,4,4]{2,1,0:T(4,128)S(1)}, s32[2,4,4]{2,1,0:T(4,128)}, u32[]{:S(2)}) copy-start(s32[2,4,4]{2,1,0:T(4,128)} %param.7) | copy-start | bytes 388
  3.1 6.4 %copy-start = (bf16[2,4,5,128,128]{4,3,2,1,0:T(8,128)(2,1)S(1)}, bf16[2,4,5,128,128]{4,3,2,1,0:T(8,128)(2,1)}, u32[]{:S(2)}) copy-start(bf16[2,4,5,128,128]{4,3,2,1,0:T(8,128)(2,1)} %param.6) | copy-start | bytes 3932164
  3.3 12.9 %collective-permute-start = (bf16[1,4,3,128,128]{3,4,2,1,0:T(8,128)(2,1)S(1)}, bf16[1,4,3,128,128]{3,4,2,1,0:T(8,128)(2,1)S(1)}, u32[]{:S(2)}, u32[]{:S(2)}) collective-permute-start(bf16[1,4,3,128,128]{3,4,2,1,0:T(8,128)(2,1)S(1)} %get-tuple-element.15), channel_id=1, source_target_pairs={{0,64},{64,128},{128,192},{192,256},{256,320},{320,384},{384,448},... | collective-permute-start | bytes 1179656 | tf_op jit(solution)/shard_map/ppermute | solution.py:15
  6.5 14.6 %collective-permute-start.1 = (bf16[1,4,3,128,128]{3,4,2,1,0:T(8,128)(2,1)S(1)}, bf16[1,4,3,128,128]{3,4,2,1,0:T(8,128)(2,1)S(1)}, u32[]{:S(2)}, u32[]{:S(2)}) collective-permute-start(bf16[1,4,3,128,128]{3,4,2,1,0:T(8,128)(2,1)S(1)} %get-tuple-element.16), channel_id=1, source_target_pairs={{64,0},{128,64},{192,128},{256,192},{320,256},{384,320},{448,384},... | collective-permute-start | bytes 1179656 | tf_op jit(solution)/shard_map/ppermute | solution.py:18
  21.2 9.1 %collective-permute-start.2 = (bf16[4,1,3,128,128]{3,4,2,1,0:T(8,128)(2,1)S(1)}, bf16[4,1,3,128,128]{3,4,2,1,0:T(8,128)(2,1)S(1)}, u32[]{:S(2)}, u32[]{:S(2)}) collective-permute-start(bf16[4,1,3,128,128]{3,4,2,1,0:T(8,128)(2,1)S(1)} %get-tuple-element.12), channel_id=1, source_target_pairs={{0,1},{1,2},{2,3},{3,4},{4,5},{5,6},{6,7},{7,8},{8,9},{9,10},{10,1... | collective-permute-start | bytes 1179656 | tf_op jit(solution)/shard_map/ppermute | solution.py:15
  23.1 8.9 %collective-permute-start.3 = (bf16[4,1,3,128,128]{3,4,2,1,0:T(8,128)(2,1)S(1)}, bf16[4,1,3,128,128]{3,4,2,1,0:T(8,128)(2,1)S(1)}, u32[]{:S(2)}, u32[]{:S(2)}) collective-permute-start(bf16[4,1,3,128,128]{3,4,2,1,0:T(8,128)(2,1)S(1)} %get-tuple-element.11), channel_id=1, source_target_pairs={{1,0},{2,1},{3,2},{4,3},{5,4},{6,5},{7,6},{8,7},{9,8},{10,9},{11,1... | collective-permute-start | bytes 1179656 | tf_op jit(solution)/shard_map/ppermute | solution.py:18
  34.5 13.5 %collective-permute-start.4 = (f32[2,1,3,2,128,128]{4,5,3,2,0,1:T(8,128)S(1)}, f32[2,1,3,2,128,128]{4,5,3,2,0,1:T(8,128)S(1)}, u32[]{:S(2)}, u32[]{:S(2)}) collective-permute-start(f32[2,1,3,2,128,128]{4,5,3,2,0,1:T(8,128)S(1)} %get-tuple-element.9), channel_id=1, source_target_pairs={{0,1},{1,2},{2,3},{3,4},{4,5},{5,6},{6,7},{7,8},{8,9},{9,10},{10,1... | collective-permute-start | bytes 2359304 | tf_op jit(solution)/shard_map/ppermute | solution.py:15
  38.6 11.4 %collective-permute-start.5 = (f32[2,1,3,2,128,128]{4,5,1,3,2,0:T(8,128)S(1)}, f32[2,1,3,2,128,128]{4,5,1,3,2,0:T(8,128)S(1)}, u32[]{:S(2)}, u32[]{:S(2)}) collective-permute-start(f32[2,1,3,2,128,128]{4,5,1,3,2,0:T(8,128)S(1)} %get-tuple-element.10), channel_id=1, source_target_pairs={{1,0},{2,1},{3,2},{4,3},{5,4},{6,5},{7,6},{8,7},{9,8},{10,9},{11,1... | collective-permute-start | bytes 2359304 | tf_op jit(solution)/shard_map/ppermute | solution.py:18
  50.2 9.1 %collective-permute-start.6 = (f32[1,2,3,3,128,128]{4,5,3,2,1,0:T(8,128)S(1)}, f32[1,2,3,3,128,128]{4,5,3,2,1,0:T(8,128)}, u32[]{:S(2)}, u32[]{:S(2)}) collective-permute-start(f32[1,2,3,3,128,128]{4,5,3,2,1,0:T(8,128)S(1)} %fusion.24), channel_id=1, source_target_pairs={{0,1},{1,0},{2,3},{3,2},{4,5},{5,4},{6,7},{7,6},{8,9},{9,8},{10,11... | collective-permute-start | bytes 3538952 | tf_op jit(solution)/shard_map/ppermute | solution.py:24
  56.7 9.2 %copy-start.2 = (s32[2,1]{0,1:T(1,128)S(1)}, s32[2,1]{0,1:T(1,128)}, u32[]{:S(2)}) copy-start(s32[2,1]{0,1:T(1,128)} %param.11) | copy-start | bytes 28
  61.1 56.6 %collective-permute-start.7 = (f32[2,2,3,3,128,128]{4,5,3,2,1,0:T(8,128)S(1)}, f32[2,2,3,3,128,128]{4,5,3,2,1,0:T(8,128)}, u32[]{:S(2)}, u32[]{:S(2)}) collective-permute-start(f32[2,2,3,3,128,128]{4,5,3,2,1,0:T(8,128)S(1)} %maximum_select_fusion.1), channel_id=1, source_target_pairs={{0,2},{1,3},{2,0},{3,1},{4,6},{5,7},{6,4},{7,5},{8,10},{9,11},{10,... | collective-permute-start | bytes 7077896 | tf_op jit(solution)/shard_map/ppermute | solution.py:24
where the time goes:
time: 123 us; the launch traced here: 122 us
  waiting for transfers between devices  79.2 us (64%)
  starting transfers between devices  28.9 us (23%)
  other arithmetic  6.19 us (5%)
  local copies, waits for them, and re-layouts  3.98 us (3%)
  matrix products  3.76 us (3%)
    ppermute x2, waiting for transfers between devices, from_partner(): lax.ppermute(array, axis, [(i, i ^ 1 << distance) for i in range(lax.axis...  54.4 us
    ppermute x3, waiting for transfers between devices, extended(): lax.ppermute(lax.slice_in_dim(block, block.shape[dim] - width, None, axis...  16.5 us
    ppermute x2, starting transfers between devices, from_partner(): lax.ppermute(array, axis, [(i, i ^ 1 << distance) for i in range(lax.axis...  11.3 us
    ppermute x3, starting transfers between devices, extended(): lax.ppermute(lax.slice_in_dim(block, block.shape[dim] - width, None, axis...  9.21 us
    ppermute x3, starting transfers between devices, extended(): lax.ppermute(lax.slice_in_dim(block, 0, width, axis=dim), axis, backward)  8.35 us
    ppermute x3, waiting for transfers between devices, extended(): lax.ppermute(lax.slice_in_dim(block, 0, width, axis=dim), axis, backward)  8.28 us
    reduce_sum x1, other arithmetic, on_device(): coarse = jnp.sum(onehot[:, :, None, None, None, None] * stacked, axis=0)  3.06 us
  transfers between devices with their start and end apart: 8, of which 8 were waited for; matrix products, arithmetic and copies ran while one was open for 1% of the time, Pallas kernels for 0%

commit v1 on v0

v1 whole, which is shorter than its diff:
```python
import jax
import jax.numpy as jnp
from jax import lax
from jax.experimental import pallas as pl
from jax.experimental.pallas import tpu as pltpu
from jax.sharding import PartitionSpec as P

B = 128
PAD = 16
F32 = jnp.float32
BF16 = jnp.bfloat16
SMEM = pl.BlockSpec(memory_space=pltpu.SMEM)
VMEM = pl.BlockSpec(memory_space=pltpu.VMEM)


def call(kernel, in_specs, shapes, *args, vmem=None):
    return pl.pallas_call(
        kernel,
        in_specs=in_specs,
        out_specs=[VMEM] * len(shapes),
        out_shape=[jax.ShapeDtypeStruct(shape, dtype) for shape, dtype in shapes],
        compiler_params=pltpu.CompilerParams(vmem_limit_bytes=32 * 2**20),
    )(*args)


def tile(index):
    return pl.ds(index * B, B)


def pick_rows(first, second):
    rows = lax.broadcasted_iota(jnp.int32, (PAD, B), 0)
    return jnp.where(rows < PAD // 2, first, second)


def pack_kernel(me, links, picks, own, side, east, west, sides, msg_e, msg_o):
    c = me[0]
    core = lax.rem(c, 2)
    keep = [c > 0, c < me[1] - 1]
    for u in range(2):
        for k in range(2):
            factor = jnp.where(keep[k], links[u, 0, k], 0).astype(F32).astype(BF16)
            sides[u, k] = side[u, 0, k] * factor
    for u, message in ((1, east), (0, west)):
        for j in range(4):
            message[j] = own[u, j]
        for k in range(2):
            message[4 + k] = sides[u, k]
    mine = pick_rows(picks[0, 0], picks[1, 0]).astype(F32).astype(BF16)

    def fill(message, up):
        for u in range(2):
            message[tile(2 * u)] = own[u, 3 if up else 0]
            message[tile(2 * u + 1)] = sides[u, 1 if up else 0]
        message[pl.ds(4 * B, PAD)] = mine

    @pl.when(core == 0)
    def _():
        fill(msg_e, True)
        fill(msg_o, False)

    @pl.when(core == 1)
    def _():
        fill(msg_e, False)
        fill(msg_o, True)


def dot(a, b):
    return lax.dot_general(a, b, (((1,), (0,)), ((), ())), preferred_element_type=F32)


def dot_t(a, b):
    return lax.dot_general(a, b, (((0,), (0,)), ((), ())), preferred_element_type=F32)


def cat(parts, axis):
    return jnp.concatenate(parts, axis=axis)


def compute_kernel(me, links, a, own, sides, xw, xe, halo_e, halo_o, row, for_e, for_o):
    core = lax.rem(me[0], 2)
    zero = jnp.zeros((B, B), BF16)
    even = core == 0
    for u in range(2):
        def edge(k):
            from_e, from_o = halo_e[1 - core, tile(2 * u + k)], halo_o[tile(2 * u + k)]
            return jnp.where(even, from_o, from_e), jnp.where(even, from_e, from_o)

        own_down, own_up = edge(0)
        high_down, low_up = edge(1)
        low, high = sides[u, 0], sides[u, 1]
        o = [own[u, j] for j in range(4)]
        west = xw if u == 0 else None
        east = xe if u == 1 else None

        def neighbour(message, other, j, k):
            if message is not None:
                return message[j] if k is None else message[4 + k]
            return own[other, j] if k is None else sides[other, k]

        def weight(j, k, link):
            return a[u, j, k] * links[u, j, link].astype(F32).astype(BF16)

        right = [
            [[low, o[0]], [own_down, high_down], [zero, o[1]]],
            [[zero, o[1]], [low, o[0]], [zero, o[2]]],
            [[o[2], zero], [o[1], zero], [o[3], high]],
            [[o[3], high], [o[2], zero], [low_up, own_up]],
        ]
        centre, western, eastern = [], [], []
        for j in range(4):
            left = cat([a[u, j, 0], weight(j, 3, 2), weight(j, 4, 3)], 1)
            centre.append(dot(left, cat([cat(r, 1) for r in right[j]], 0)).astype(BF16))
            for out, k, link, message in ((western, 1, 0, west), (eastern, 2, 1, east)):
                panel = neighbour(message, 1 - u, j, None)
                if j == 0:
                    panel = cat([neighbour(message, 1 - u, j, 0), panel], 1)
                if j == 3:
                    panel = cat([panel, neighbour(message, 1 - u, j, 1)], 1)
                out.append(dot(weight(j, k, link), panel).astype(BF16))

        def slot(values, j, second):
            return values[j][:, B:] if second else values[j][:, :B]

        middle = [
            cat([western[0][:, B:], slot(centre, 0, True), eastern[0][:, B:]], 1),
            cat([western[1], slot(centre, 1, True), eastern[1]], 1),
            cat([western[2], slot(centre, 2, False), eastern[2]], 1),
            cat([western[3][:, :B], slot(centre, 3, False), eastern[3][:, :B]], 1),
        ]
        first = cat([western[0][:, :B], slot(centre, 0, False), eastern[0][:, :B]], 1)
        last = cat([western[3][:, B:], slot(centre, 3, True), eastern[3][:, B:]], 1)
        result1 = dot_t(cat(o, 0), cat(middle, 0))
        result0 = dot_t(o[0], first)
        result2 = dot_t(o[3], last)
        extra0 = dot_t(o[1], slot(centre, 1, False))
        extra2 = dot_t(o[2], slot(centre, 2, True))
        for d in range(3):
            at = slice(d * B, (d + 1) * B)
            row[u, d, 0] = result0[:, at] + extra0 if d == 1 else result0[:, at]
            row[u, d, 1] = result1[:, at]
            row[u, d, 2] = result2[:, at] + extra2 if d == 1 else result2[:, at]
        down = dot_t(low, cat([first, middle[0]], 1))
        up = dot_t(high, cat([middle[3], last], 1))
        for d in range(3):
            for s in range(2):
                at = slice((s * 3 + d) * B, (s * 3 + d + 1) * B)
                for_e[u, d, s] = jnp.where(even, up[:, at], down[:, at])
                for_o[6 * u + 2 * d + s] = jnp.where(even, down[:, at], up[:, at]).astype(BF16)


def merge_kernel(me, row, for_e, from_o, halo_o, row_out, message):
    core = lax.rem(me[0], 2)
    for u in range(2):
        for d in range(3):
            for t in range(3):
                row_out[u, d, t] = row[u, d, t]
            for s in range(2):
                row_out[u, d, core + s] += from_o[6 * u + 2 * d + s].astype(F32)
            for t in range(3):
                message[tile(15 * u + 3 * d + t)] = row_out[u, d, t].astype(BF16)
            for s in range(2):
                message[tile(15 * u + 9 + 2 * d + s)] = for_e[u, d, s].astype(BF16)
    message[pl.ds(30 * B, PAD)] = halo_o[pl.ds(4 * B, PAD)]


def rows_of_chip(core, row, for_e, message, u, d, t):
    mine = row[u, d, t]
    theirs = message[tile(15 * u + 3 * d + t)].astype(F32)
    if t == 1:
        mine = mine + message[tile(15 * u + 9 + 2 * d + core)].astype(F32)
        theirs = theirs + for_e[u, d, 1 - core]
    else:
        gets = (core == 0) == (t == 2)
        s = 1 if t == 2 else 0
        got = message[tile(15 * u + 9 + 2 * d + s)].astype(F32)
        mine = mine + jnp.where(gets, got, 0.0)
        theirs = theirs + jnp.where(gets, 0.0, for_e[u, d, s])
    return mine, theirs


def choose_kernel(me, picks, row, for_e, message, halo_e, halo_o, out):
    c = me[0]
    core = lax.rem(c, 2)
    position = lax.rem(c, 4)
    chip = position // 2
    outer = jnp.logical_or(position == 0, position == 3)
    tail = pl.ds(4 * B, PAD)
    inferred = 6.0 - pick_rows(picks[0, 0], picks[1, 0]).astype(F32)
    inferred = inferred - halo_e[1 - core, tail].astype(F32) - halo_o[tail].astype(F32)
    wanted = jnp.where(outer, message[pl.ds(30 * B, PAD)].astype(F32), inferred)
    own_code = position.astype(F32)
    other_code = (chip * 2 + 1 - core).astype(F32)
    for u in range(2):
        ask = wanted[u * PAD // 2:u * PAD // 2 + 1]
        use_own = jnp.broadcast_to(ask == own_code, (B, B))
        use_other = jnp.broadcast_to(ask == other_code, (B, B))
        for d in range(3):
            for t in range(3):
                mine, theirs = rows_of_chip(core, row, for_e, message, u, d, t)
                out[9 * u + 3 * d + t] = jnp.where(use_own, mine, jnp.where(use_other, theirs, 0.0)).astype(BF16)


def finish_kernel(me, picks, row, for_e, message, arrived, out):
    c = me[0]
    core = lax.rem(c, 2)
    position = lax.rem(c, 4)
    for u in range(2):
        pick = picks[u, 0]

        @pl.when(pick // 2 == position // 2)
        def _():
            for d in range(3):
                for t in range(3):
                    mine, theirs = rows_of_chip(core, row, for_e, message, u, d, t)
                    out[u, 0, d, t] = jnp.where(pick == position, mine, theirs)

        @pl.when(pick // 2 != position // 2)
        def _():
            for d in range(3):
                for t in range(3):
                    out[u, 0, d, t] = arrived[9 * u + 3 * d + t].astype(F32)


def on_device(a_tiles, a_links, p_own, p_side, p_links, coarse_pick):
    count = lax.axis_size("gy")
    columns = lax.axis_size("gx")
    me = jnp.stack([lax.axis_index("gy").astype(jnp.int32), jnp.int32(count)])
    pairs = [(2 * g, 2 * g + 1) for g in range(count // 2)]
    inside = pairs + [(b, a) for a, b in pairs]
    outside = [(i + 1, i + 2) for i in range(0, count - 2, 2)]
    outside = outside + [(b, a) for a, b in outside]
    across = [(i, i ^ 2) for i in range(count)]
    eastward = [(i, i + 1) for i in range(columns - 1)]
    westward = [(b, a) for a, b in eastward]
    tile_shape = (B, B)

    east, west, sides, msg_e, msg_o = call(
        pack_kernel, [SMEM, SMEM, SMEM, VMEM, VMEM],
        [((6,) + tile_shape, BF16), ((6,) + tile_shape, BF16), ((2, 2) + tile_shape, BF16),
         ((4 * B + PAD, B), BF16), ((4 * B + PAD, B), BF16)],
        me, p_links, coarse_pick, p_own, p_side)
    from_west = lax.ppermute(east, "gx", eastward)
    from_east = lax.ppermute(west, "gx", westward)
    halo_o = lax.ppermute(msg_o, "gy", outside)
    halo_e = lax.all_gather(msg_e, "gy", axis_index_groups=[list(p) for p in pairs])
    row, for_e, for_o = call(
        compute_kernel, [SMEM, SMEM] + [VMEM] * 7,
        [((2, 3, 3) + tile_shape, F32), ((2, 3, 2) + tile_shape, F32), ((12,) + tile_shape, BF16)],
        me, a_links, a_tiles, p_own, sides, from_west, from_east, halo_e, halo_o)
    from_o = lax.ppermute(for_o, "gy", outside)
    row, message = call(
        merge_kernel, [SMEM] + [VMEM] * 4,
        [((2, 3, 3) + tile_shape, F32), ((30 * B + PAD, B), BF16)],
        me, row, for_e, from_o, halo_o)
    message = lax.ppermute(message, "gy", inside)
    (chosen,) = call(
        choose_kernel, [SMEM, SMEM] + [VMEM] * 5, [((18,) + tile_shape, BF16)],
        me, coarse_pick, row, for_e, message, halo_e, halo_o)
    arrived = lax.ppermute(chosen, "gy", across)
    (out,) = call(
        finish_kernel, [SMEM, SMEM] + [VMEM] * 4, [((2, 1, 3, 3) + tile_shape, F32)],
        me, coarse_pick, row, for_e, message, arrived)
    return out


def solution(mesh):
    return jax.shard_map(
        on_device,
        mesh=mesh,
        in_specs=(
            P("gx", "gy", None, None, None),
            P("gx", "gy", None),
            P("gx", "gy", None, None),
            P("gx", "gy", None, None, None),
            P("gx", "gy", None),
            P("gx", "gy"),
        ),
        out_specs=P("gx", "gy", None, None, None, None),
        check_vma=False,
    )
```

time: 123 us -> 62.5 us (0.51)
  the two profiles are of different devices: /device:TPU:346 before, /device:TPU:8 now
where the time goes in v1:
time: 62.5 us; the launch traced here: 62.1 us
  starting transfers between devices  29.8 us (48%)
  waiting for transfers between devices  18 us (29%)
  local copies, waits for them, and re-layouts  6.22 us (10%)
  Pallas kernels  5.89 us (9%)
  blocking collectives  2 us (3%)
    ppermute x1, waiting for transfers between devices, on_device(): arrived = lax.ppermute(chosen, 'gy', across)  15.3 us
    ppermute x1, starting transfers between devices, on_device(): from_east = lax.ppermute(west, 'gx', westward)  12.8 us
    ppermute x1, starting transfers between devices, on_device(): message = lax.ppermute(message, 'gy', inside)  9.97 us
    unnamed x13, local copies, waits for them, and re-layouts  6.22 us
    pallas_call x5, Pallas kernels, call(): pl.pallas_call(kernel, in_specs=in_specs, out_specs=[VMEM] * len(shapes),...  5.89 us
    ppermute x1, starting transfers between devices, on_device(): from_west = lax.ppermute(east, 'gx', eastward)  3.48 us
    ppermute x1, starting transfers between devices, on_device(): arrived = lax.ppermute(chosen, 'gy', across)  2.18 us
    ppermute x1, waiting for transfers between devices, on_device(): message = lax.ppermute(message, 'gy', inside)  2.18 us
  transfers between devices with their start and end apart: 6, of which 3 were waited for; matrix products, arithmetic and copies ran while one was open for 0% of the time, Pallas kernels for 0%

profile of v1, /device:TPU:8, one launch (start us, length us, event | category | flops | bytes accessed | tf_op | source)
XLA Modules:
  0.0 62.1 jit_solution(10036918877731465289)
XLA Ops:
  0.0 0.7 %copy.9.picks = s32[2,1]{1,0:T(2,128)S(1)} copy(s32[2,1]{0,1:T(1,128)} %param.11) | data formatting | bytes 16 | tf_op args[5]
  0.7 0.1 pad_add_fusion.me
  0.8 0.9 %copy-done.1 = bf16[2,4,128,128]{3,2,1,0:T(8,128)(2,1)S(1)} copy-done((bf16[2,4,128,128]{3,2,1,0:T(8,128)(2,1)S(1)}, bf16[2,4,128,128]{3,2,1,0:T(8,128)(2,1)}, u32[]{:S(2)}) %copy-start.1) | copy-done | bytes 262168
  1.8 0.9 %copy-done.3 = bf16[2,1,2,128,128]{4,3,2,1,0:T(8,128)(2,1)S(1)} copy-done((bf16[2,1,2,128,128]{4,3,2,1,0:T(8,128)(2,1)S(1)}, bf16[2,1,2,128,128]{4,3,2,1,0:T(8,128)(2,1)}, u32[]{:S(2)}) %copy-start.3) | copy-done | bytes 131096
  2.7 0.7 %copy-done.5 = s32[2,1,2]{2,1,0:T(1,128)S(1)} copy-done((s32[2,1,2]{2,1,0:T(1,128)S(1)}, s32[2,1,2]{2,1,0:T(1,128)}, u32[]{:S(2)}) %copy-start.5) | copy-done | bytes 40
  3.4 0.6 %shard_map.64 = (bf16[6,128,128]{2,1,0:T(8,128)(2,1)S(1)}, bf16[6,128,128]{2,1,0:T(8,128)(2,1)S(1)}, bf16[2,2,128,128]{3,2,1,0:T(8,128)(2,1)S(1)}, bf16[528,128]{1,0:T(8,128)(2,1)S(1)}, bf16[528,128]{1,0:T(8,128)(2,1)S(1)}) custom-call(s32[2]{0:T(128)S(1)} %pad_add_fusion.me, s32[2,1,2]{2,1,0:T(1,128)S(1)} %copy-done.5, s32[2,1]{1,0:T(2,128)S(1)} %copy.9.picks, ...), custom_call_target="tpu_custom_call" | custom-call | tf_op jit(solution)/shard_map/pallas_call | solution.py:17
  4.0 3.5 %collective-permute-start = (bf16[6,128,128]{2,1,0:T(8,128)(2,1)S(1)}, bf16[6,128,128]{2,1,0:T(8,128)(2,1)S(1)}, u32[]{:S(2)}, u32[]{:S(2)}) collective-permute-start(bf16[6,128,128]{2,1,0:T(8,128)(2,1)S(1)} %get-tuple-element.16), channel_id=1, source_target_pairs={{0,64},{64,128},{128,192},{192,256},{256,320},{320,384},{384,448},... | collective-permute-start | bytes 589832 | tf_op jit(solution)/shard_map/ppermute | solution.py:242
  7.5 12.8 %collective-permute-start.1 = (bf16[6,128,128]{2,1,0:T(8,128)(2,1)S(1)}, bf16[6,128,128]{2,1,0:T(8,128)(2,1)S(1)}, u32[]{:S(2)}, u32[]{:S(2)}) collective-permute-start(bf16[6,128,128]{2,1,0:T(8,128)(2,1)S(1)} %get-tuple-element.17), channel_id=1, source_target_pairs={{64,0},{128,64},{192,128},{256,192},{320,256},{384,320},{448,384},... | collective-permute-start | bytes 589832 | tf_op jit(solution)/shard_map/ppermute | solution.py:243
  20.3 0.7 %collective-permute-start.2 = (bf16[528,128]{1,0:T(8,128)(2,1)S(1)}, bf16[528,128]{1,0:T(8,128)(2,1)S(1)}, u32[]{:S(2)}, u32[]{:S(2)}) collective-permute-start(bf16[528,128]{1,0:T(8,128)(2,1)S(1)} %get-tuple-element.19), channel_id=1, source_target_pairs={{1,2},{3,4},{5,6},{7,8},{9,10},{11,12},{13,14},{15,16},{17,18},{19... | collective-permute-start | bytes 405512 | tf_op jit(solution)/shard_map/ppermute | solution.py:244
  21.0 2.0 %all-gather = bf16[1056,128]{1,0:T(8,128)(2,1)S(1)} all-gather(bf16[528,128]{1,0:T(8,128)(2,1)S(1)} %get-tuple-element.18), channel_id=2, replica_groups={{0,1},{2,3},{4,5},{6,7},{8,9},{10,11},{12,13},{14,15},{16,17},{18,19},{..., dimensions={0}, use_global_device_ids=true | all-gather | bytes 405504 | tf_op jit(solution)/shard_map/all_gather | solution.py:245
  23.0 0.0 collective-permute-done.2.halo_o
  23.0 0.5 collective-permute-done.1.xe
  23.5 1.3 %copy-done = bf16[2,4,5,128,128]{4,3,2,1,0:T(8,128)(2,1)S(1)} copy-done((bf16[2,4,5,128,128]{4,3,2,1,0:T(8,128)(2,1)S(1)}, bf16[2,4,5,128,128]{4,3,2,1,0:T(8,128)(2,1)}, u32[]{:S(2)}) %copy-start) | copy-done | bytes 1310744
  24.8 0.9 %copy-done.2 = bf16[2,4,128,128]{3,2,1,0:T(8,128)(2,1)S(1)} copy-done((bf16[2,4,128,128]{3,2,1,0:T(8,128)(2,1)S(1)}, bf16[2,4,128,128]{3,2,1,0:T(8,128)(2,1)}, u32[]{:S(2)}) %copy-start.2) | copy-done | bytes 262168
  25.8 0.7 %copy-done.4 = s32[2,4,4]{2,1,0:T(4,128)S(1)} copy-done((s32[2,4,4]{2,1,0:T(4,128)S(1)}, s32[2,4,4]{2,1,0:T(4,128)}, u32[]{:S(2)}) %copy-start.4) | copy-done | bytes 152
  26.4 1.9 %shard_map.65 = (f32[2,3,3,128,128]{4,3,2,1,0:T(8,128)S(1)}, f32[2,3,2,128,128]{4,3,2,1,0:T(8,128)S(1)}, bf16[12,128,128]{2,1,0:T(8,128)(2,1)S(1)}) custom-call(s32[2]{0:T(128)S(1)} %pad_add_fusion.me, s32[2,4,4]{2,1,0:T(4,128)S(1)} %copy-done.4, bf16[2,4,5,128,128]{4,3,2,1,0:T(8,128)(2,1)S(1)} %copy-done, bf16[2,4,128,128]{3,2,1,0:T(8,128)(2,1)S(1)} %copy-done.2, ...), custom_call_target="tpu_custom_call" | custom-call | tf_op jit(solution)/shard_map/pallas_call | solution.py:17
  28.4 0.7 %collective-permute-start.3 = (bf16[12,128,128]{2,1,0:T(8,128)(2,1)S(1)}, bf16[12,128,128]{2,1,0:T(8,128)(2,1)S(1)}, u32[]{:S(2)}, u32[]{:S(2)}) collective-permute-start(bf16[12,128,128]{2,1,0:T(8,128)(2,1)S(1)} %get-tuple-element.22), channel_id=1, source_target_pairs={{1,2},{3,4},{5,6},{7,8},{9,10},{11,12},{13,14},{15,16},{17,18},{19... | collective-permute-start | bytes 1179656 | tf_op jit(solution)/shard_map/ppermute | solution.py:250
  29.1 0.8 %shard_map.66 = (f32[2,3,3,128,128]{4,3,2,1,0:T(8,128)S(1)}, bf16[3856,128]{1,0:T(8,128)(2,1)S(1)}) custom-call(s32[2]{0:T(128)S(1)} %pad_add_fusion.me, f32[2,3,3,128,128]{4,3,2,1,0:T(8,128)S(1)} %get-tuple-element.20.row, f32[2,3,2,128,128]{4,3,2,1,0:T(8,128)S(1)} %get-tuple-element.21.for_e, bf16[12,128,128]{2,1,0:T(8,128)(2,1)S(1)} %collective-permute-done.3.from_o, ...), custom_call_target="tpu_custom_call" | custom-call | tf_op jit(solution)/shard_map/pallas_call | solution.py:17
  29.9 10.0 %collective-permute-start.4 = (bf16[3856,128]{1,0:T(8,128)(2,1)S(1)}, bf16[3856,128]{1,0:T(8,128)(2,1)S(1)}, u32[]{:S(2)}, u32[]{:S(2)}) collective-permute-start(bf16[3856,128]{1,0:T(8,128)(2,1)S(1)} %get-tuple-element.24), channel_id=1, source_target_pairs={{0,1},{2,3},{4,5},{6,7},{8,9},{10,11},{12,13},{14,15},{16,17},{18,... | collective-permute-start | bytes 2961416 | tf_op jit(solution)/shard_map/ppermute | solution.py:255
  39.9 2.2 %collective-permute-done.4.message = bf16[3856,128]{1,0:T(8,128)(2,1)S(1)} collective-permute-done((bf16[3856,128]{1,0:T(8,128)(2,1)S(1)}, bf16[3856,128]{1,0:T(8,128)(2,1)S(1)}, u32[]{:S(2)}, u32[]{:S(2)}) %collective-permute-start.4) | collective-permute-done | bytes 987168 | tf_op jit(solution)/shard_map/ppermute | solution.py:255
  42.1 0.8 %shard_map.67 = bf16[18,128,128]{2,1,0:T(8,128)(2,1)S(1)} custom-call(s32[2]{0:T(128)S(1)} %pad_add_fusion.me, s32[2,1]{1,0:T(2,128)S(1)} %copy.9.picks, f32[2,3,3,128,128]{4,3,2,1,0:T(8,128)S(1)} %get-tuple-element.23.row, f32[2,3,2,128,128]{4,3,2,1,0:T(8,128)S(1)} %get-tuple-element.21.for_e, bf16[3856,128]{1,0:T(8,128)(2,1)S(1)} %collective-permute-done.4.message, ...), custom_call_target="tpu_custom_call" | custom-call | tf_op jit(solution)/shard_map/pallas_call | solution.py:17
  42.9 2.2 %collective-permute-start.5 = (bf16[18,128,128]{2,1,0:T(8,128)(2,1)S(1)}, bf16[18,128,128]{2,1,0:T(8,128)(2,1)S(1)}, u32[]{:S(2)}, u32[]{:S(2)}) collective-permute-start(bf16[18,128,128]{2,1,0:T(8,128)(2,1)S(1)} %shard_map.67), channel_id=1, source_target_pairs={{0,2},{1,3},{2,0},{3,1},{4,6},{5,7},{6,4},{7,5},{8,10},{9,11},{10,... | collective-permute-start | bytes 1769480 | tf_op jit(solution)/shard_map/ppermute | solution.py:259
  45.1 15.3 %collective-permute-done.5.arrived = bf16[18,128,128]{2,1,0:T(8,128)(2,1)S(1)} collective-permute-done((bf16[18,128,128]{2,1,0:T(8,128)(2,1)S(1)}, bf16[18,128,128]{2,1,0:T(8,128)(2,1)S(1)}, u32[]{:S(2)}, u32[]{:S(2)}) %collective-permute-start.5) | collective-permute-done | bytes 589856 | tf_op jit(solution)/shard_map/ppermute | solution.py:259
  60.4 1.7 %shard_map.68 = f32[2,1,3,3,128,128]{5,4,3,2,1,0:T(8,128)} custom-call(s32[2]{0:T(128)S(1)} %pad_add_fusion.me, s32[2,1]{1,0:T(2,128)S(1)} %copy.9.picks, f32[2,3,3,128,128]{4,3,2,1,0:T(8,128)S(1)} %get-tuple-element.23.row, f32[2,3,2,128,128]{4,3,2,1,0:T(8,128)S(1)} %get-tuple-element.21.for_e, bf16[3856,128]{1,0:T(8,128)(2,1)S(1)} %collective-permute-done.4.message, ...), custom_call_target="tpu_custom_call" | custom-call | tf_op jit(solution)/shard_map/pallas_call | solution.py:17
  (8 shorter events, 0.0 us)
Async XLA Ops:
  0.8 0.9 %copy-start.1 = (bf16[2,4,128,128]{3,2,1,0:T(8,128)(2,1)S(1)}, bf16[2,4,128,128]{3,2,1,0:T(8,128)(2,1)}, u32[]{:S(2)}) copy-start(bf16[2,4,128,128]{3,2,1,0:T(8,128)(2,1)} %own.3) | copy-start | bytes 786436
  1.8 0.9 %copy-start.3 = (bf16[2,1,2,128,128]{4,3,2,1,0:T(8,128)(2,1)S(1)}, bf16[2,1,2,128,128]{4,3,2,1,0:T(8,128)(2,1)}, u32[]{:S(2)}) copy-start(bf16[2,1,2,128,128]{4,3,2,1,0:T(8,128)(2,1)} %side.1) | copy-start | bytes 393220
  2.7 0.7 %copy-start.5 = (s32[2,1,2]{2,1,0:T(1,128)S(1)}, s32[2,1,2]{2,1,0:T(1,128)}, u32[]{:S(2)}) copy-start(s32[2,1,2]{2,1,0:T(1,128)} %links.2) | copy-start | bytes 52
  4.0 19.0 %collective-permute-start = (bf16[6,128,128]{2,1,0:T(8,128)(2,1)S(1)}, bf16[6,128,128]{2,1,0:T(8,128)(2,1)S(1)}, u32[]{:S(2)}, u32[]{:S(2)}) collective-permute-start(bf16[6,128,128]{2,1,0:T(8,128)(2,1)S(1)} %get-tuple-element.16), channel_id=1, source_target_pairs={{0,64},{64,128},{128,192},{192,256},{256,320},{320,384},{384,448},... | collective-permute-start | bytes 589832 | tf_op jit(solution)/shard_map/ppermute | solution.py:242
  7.5 16.0 %collective-permute-start.1 = (bf16[6,128,128]{2,1,0:T(8,128)(2,1)S(1)}, bf16[6,128,128]{2,1,0:T(8,128)(2,1)S(1)}, u32[]{:S(2)}, u32[]{:S(2)}) collective-permute-start(bf16[6,128,128]{2,1,0:T(8,128)(2,1)S(1)} %get-tuple-element.17), channel_id=1, source_target_pairs={{64,0},{128,64},{192,128},{256,192},{320,256},{384,320},{448,384},... | collective-permute-start | bytes 589832 | tf_op jit(solution)/shard_map/ppermute | solution.py:243
  20.3 2.7 %collective-permute-start.2 = (bf16[528,128]{1,0:T(8,128)(2,1)S(1)}, bf16[528,128]{1,0:T(8,128)(2,1)S(1)}, u32[]{:S(2)}, u32[]{:S(2)}) collective-permute-start(bf16[528,128]{1,0:T(8,128)(2,1)S(1)} %get-tuple-element.19), channel_id=1, source_target_pairs={{1,2},{3,4},{5,6},{7,8},{9,10},{11,12},{13,14},{15,16},{17,18},{19... | collective-permute-start | bytes 405512 | tf_op jit(solution)/shard_map/ppermute | solution.py:244
  23.5 1.3 %copy-start = (bf16[2,4,5,128,128]{4,3,2,1,0:T(8,128)(2,1)S(1)}, bf16[2,4,5,128,128]{4,3,2,1,0:T(8,128)(2,1)}, u32[]{:S(2)}) copy-start(bf16[2,4,5,128,128]{4,3,2,1,0:T(8,128)(2,1)} %a.1) | copy-start | bytes 3932164
  24.8 0.9 %copy-start.2 = (bf16[2,4,128,128]{3,2,1,0:T(8,128)(2,1)S(1)}, bf16[2,4,128,128]{3,2,1,0:T(8,128)(2,1)}, u32[]{:S(2)}) copy-start(bf16[2,4,128,128]{3,2,1,0:T(8,128)(2,1)} %own.3) | copy-start | bytes 786436
  25.8 0.7 %copy-start.4 = (s32[2,4,4]{2,1,0:T(4,128)S(1)}, s32[2,4,4]{2,1,0:T(4,128)}, u32[]{:S(2)}) copy-start(s32[2,4,4]{2,1,0:T(4,128)} %links.3) | copy-start | bytes 388
  28.4 0.7 %collective-permute-start.3 = (bf16[12,128,128]{2,1,0:T(8,128)(2,1)S(1)}, bf16[12,128,128]{2,1,0:T(8,128)(2,1)S(1)}, u32[]{:S(2)}, u32[]{:S(2)}) collective-permute-start(bf16[12,128,128]{2,1,0:T(8,128)(2,1)S(1)} %get-tuple-element.22), channel_id=1, source_target_pairs={{1,2},{3,4},{5,6},{7,8},{9,10},{11,12},{13,14},{15,16},{17,18},{19... | collective-permute-start | bytes 1179656 | tf_op jit(solution)/shard_map/ppermute | solution.py:250
  29.9 12.2 %collective-permute-start.4 = (bf16[3856,128]{1,0:T(8,128)(2,1)S(1)}, bf16[3856,128]{1,0:T(8,128)(2,1)S(1)}, u32[]{:S(2)}, u32[]{:S(2)}) collective-permute-start(bf16[3856,128]{1,0:T(8,128)(2,1)S(1)} %get-tuple-element.24), channel_id=1, source_target_pairs={{0,1},{2,3},{4,5},{6,7},{8,9},{10,11},{12,13},{14,15},{16,17},{18,... | collective-permute-start | bytes 2961416 | tf_op jit(solution)/shard_map/ppermute | solution.py:255
  42.9 17.5 %collective-permute-start.5 = (bf16[18,128,128]{2,1,0:T(8,128)(2,1)S(1)}, bf16[18,128,128]{2,1,0:T(8,128)(2,1)S(1)}, u32[]{:S(2)}, u32[]{:S(2)}) collective-permute-start(bf16[18,128,128]{2,1,0:T(8,128)(2,1)S(1)} %shard_map.67), channel_id=1, source_target_pairs={{0,2},{1,3},{2,0},{3,1},{4,6},{5,7},{6,4},{7,5},{8,10},{9,11},{10,... | collective-permute-start | bytes 1769480 | tf_op jit(solution)/shard_map/ppermute | solution.py:259

commit v2 on v0

v2 whole, which is shorter than its diff:
```python
import jax
import jax.numpy as jnp
from jax import lax
from jax.experimental import pallas as pl
from jax.experimental.pallas import tpu as pltpu
from jax.sharding import PartitionSpec as P

B = 128
PAD = 16
F32 = jnp.float32
BF16 = jnp.bfloat16
VMEM = pl.BlockSpec(memory_space=pltpu.VMEM)
HBM = pl.BlockSpec(memory_space=pltpu.HBM)

NEAR = ((0, 2), (0, 1), (1, 0), (1, 1))
FAR = ((0, 0), (1, 2))
LINK_TILE = {0: 1, 2: 2}


def call(kernel, args, shapes, in_specs=None, out_specs=None, scratch=(), aliases=None, cost=1):
    return pl.pallas_call(
        kernel,
        in_specs=in_specs or [VMEM] * len(args),
        out_specs=out_specs or [VMEM] * len(shapes),
        out_shape=[jax.ShapeDtypeStruct(shape, dtype) for shape, dtype in shapes],
        scratch_shapes=list(scratch),
        input_output_aliases=aliases or {},
        compiler_params=pltpu.CompilerParams(vmem_limit_bytes=32 * 2**20),
        cost_estimate=pl.CostEstimate(flops=cost * 10**9, bytes_accessed=cost * 10**6, transcendentals=0),
    )(*args)


def tile(index):
    return pl.ds(index * B, B)


def dot(a, b):
    return lax.dot_general(a, b, (((1,), (0,)), ((), ())), preferred_element_type=F32)


def dot_t(a, b):
    return lax.dot_general(a, b, (((0,), (0,)), ((), ())), preferred_element_type=F32)


def cat(parts, axis):
    return jnp.concatenate(parts, axis=axis)


def begin_kernel(a_links, p_links, picks, own_in, side_in, a_in,
                 own, a, sides, east, west, msg_o, msg_e, mine,
                 s_links, s_side, s_picks, raw, sems):
    copies = [
        pltpu.make_async_copy(src, dst, sems.at[i])
        for i, (src, dst) in enumerate(((p_links, s_side), (own_in, own), (side_in, raw), (a_links, s_links),
                                        (picks, s_picks), (a_in, a)))
    ]
    for copy in copies:
        copy.start()
    c = lax.axis_index("gy")
    core = lax.rem(c, 2)
    keep = [c > 0, c < lax.axis_size("gy") - 1]
    for copy in copies[:3]:
        copy.wait()
    for u in range(2):
        for k in range(2):
            factor = jnp.where(keep[k], s_side[u, 0, k], 0).astype(F32).astype(BF16)
            sides[u, k] = raw[u, 0, k] * factor
    for u, message in ((1, east), (0, west)):
        for j in range(4):
            message[j] = own[u, j]
        for k in range(2):
            message[4 + k] = sides[u, k]
    for copy in copies[3:5]:
        copy.wait()
    rows = lax.broadcasted_iota(jnp.int32, (PAD, B), 0)
    codes = jnp.where(rows < PAD // 2, s_picks[0, 0], s_picks[0, 1]).astype(F32)
    mine[...] = codes
    msg_o[pl.ds(14 * B, PAD)] = codes.astype(BF16)
    msg_e[pl.ds(4 * B, PAD)] = codes.astype(BF16)
    copies[5].wait()
    for u in range(2):
        for j in range(4):
            for k in range(4):
                a[u, j, k + 1] = a[u, j, k + 1] * s_links[u, j, k].astype(F32).astype(BF16)

    def fill(j_e, k_e, j_o, k_o):
        for u in range(2):
            msg_e[tile(2 * u)] = own[u, j_e]
            msg_e[tile(2 * u + 1)] = sides[u, k_e]
            side, block = sides[u, k_o], own[u, j_o]
            other_side, other_block = sides[1 - u, k_o], own[1 - u, j_o]
            zero = jnp.zeros((B, B), BF16)
            inner = 1 if j_o == 0 else 2
            if j_o == 0:
                right = cat([cat([side, block], 1), cat([zero, own[u, inner]], 1)], 0)
                left = cat([a[u, j_o, 0], a[u, j_o, 4]], 1)
                beyond = a[u, j_o, 3]
                panel = cat([other_side, other_block], 1)
            else:
                right = cat([cat([block, side], 1), cat([own[u, inner], zero], 1)], 0)
                left = cat([a[u, j_o, 0], a[u, j_o, 3]], 1)
                beyond = a[u, j_o, 4]
                panel = cat([other_block, other_side], 1)
            centre = dot(left, right).astype(BF16)
            beside = dot(a[u, j_o, LINK_TILE[NEAR[2 * u][1]]], panel).astype(BF16)
            result = dot_t(side, cat([centre, beyond, beside], 1)).astype(BF16)
            msg_o[tile(7 * u)] = block
            msg_o[tile(7 * u + 1)] = side
            for i in range(5):
                msg_o[tile(7 * u + 2 + i)] = result[:, i * B:(i + 1) * B]

    @pl.when(core == 0)
    def _():
        fill(3, 1, 0, 0)

    @pl.when(core == 1)
    def _():
        fill(0, 0, 3, 1)


def reduce_units(own, u, products, count):
    firsts, middles, lasts = products
    blocks = cat([own[u, j] for j in range(4)], 0)
    slot1 = dot_t(blocks, cat(middles, 0))
    slot0 = dot_t(own[u, 0], firsts)
    slot2 = dot_t(own[u, 3], lasts)
    return [[value[:, i * B:(i + 1) * B] for i in range(count)] for value in (slot0, slot1, slot2)]


def link_products(a, u, d, tiles, side_tiles):
    k = LINK_TILE[d]
    first = dot(a[u, 0, k], cat([side_tiles[0], tiles[0]], 1)).astype(BF16)
    last = dot(a[u, 3, k], cat([tiles[3], side_tiles[1]], 1)).astype(BF16)
    inner = [dot(a[u, j, k], tiles[j]).astype(BF16) for j in (1, 2)]
    return first[:, :B], [first[:, B:], inner[0], inner[1], last[:, :B]], last[:, B:]


def near_kernel(own, a, sides, halo_e, halo_o, from_west, from_east, row, for_e, message):
    del from_west, from_east
    core = lax.rem(lax.axis_index("gy"), 2)
    even = core == 0
    zero = jnp.zeros((B, B), BF16)
    message[pl.ds(20 * B, PAD)] = halo_o[pl.ds(14 * B, PAD)]
    for u in range(2):
        def edge(k):
            from_e, from_o = halo_e[1 - core, tile(2 * u + k)], halo_o[tile(7 * u + k)]
            return jnp.where(even, from_o, from_e), jnp.where(even, from_e, from_o)

        own_down, own_up = edge(0)
        high_down, low_up = edge(1)
        low, high = sides[u, 0], sides[u, 1]
        o = [own[u, j] for j in range(4)]
        right = [
            [[low, o[0]], [own_down, high_down], [zero, o[1]]],
            [[zero, o[1]], [low, o[0]], [zero, o[2]]],
            [[o[2], zero], [o[1], zero], [o[3], high]],
            [[o[3], high], [o[2], zero], [low_up, own_up]],
        ]
        centre = []
        for j in range(4):
            left = cat([a[u, j, 0], a[u, j, 3], a[u, j, 4]], 1)
            centre.append(dot(left, cat([cat(r, 1) for r in right[j]], 0)).astype(BF16))
        left_part = [value[:, :B] for value in centre]
        right_part = [value[:, B:] for value in centre]
        beside = link_products(a, u, NEAR[2 * u][1], [own[1 - u, j] for j in range(4)],
                               [sides[1 - u, k] for k in range(2)])
        first = cat([beside[0], left_part[0]], 1)
        middle = [cat([beside[1][0], right_part[0]], 1), cat([beside[1][1], right_part[1]], 1),
                  cat([beside[1][2], left_part[2]], 1), cat([beside[1][3], left_part[3]], 1)]
        last = cat([beside[2], right_part[3]], 1)
        slots = reduce_units(own, u, (first, middle, last), 2)
        slots[0][1] = slots[0][1] + dot_t(o[1], left_part[1])
        slots[2][1] = slots[2][1] + dot_t(o[2], right_part[2])
        beyond = dot(halo_o[tile(7 * u + 4)], cat([jnp.where(even, low, o[3]), jnp.where(even, o[0], high)], 1))
        given = dot_t(jnp.where(even, high, low),
                      cat([jnp.where(even, middle[3], first), jnp.where(even, last, middle[0])], 1))
        for i in range(2):
            k = 2 * u + i
            for t in range(3):
                row[k, t] = slots[t][i]
            for s in range(2):
                if i == 0:
                    extra = halo_o[tile(7 * u + 5 + s)].astype(F32)
                else:
                    extra = halo_o[tile(7 * u + 2 + s)].astype(F32) + beyond[:, s * B:(s + 1) * B]
                row[k, core + s] += extra
                part = given[:, (2 * s + i) * B:(2 * s + i + 1) * B]
                for_e[k, s] = part
                message[tile(5 * k + 3 + s)] = part.astype(BF16)
            for t in range(3):
                message[tile(5 * k + t)] = row[k, t].astype(BF16)


def far_kernel(own, a, sides, from_west, from_east, row, for_e, for_o):
    even = lax.rem(lax.axis_index("gy"), 2) == 0
    for k, (u, d) in enumerate(FAR):
        arrived = from_west if d == 0 else from_east
        first, middle, last = link_products(a, u, d, [arrived[j] for j in range(4)], [arrived[4], arrived[5]])
        slots = reduce_units(own, u, (first, middle, last), 1)
        for t in range(3):
            row[k, t] = slots[t][0]
        down = dot_t(sides[u, 0], cat([first, middle[0]], 1))
        up = dot_t(sides[u, 1], cat([middle[3], last], 1))
        to_e, to_o = jnp.where(even, up, down), jnp.where(even, down, up)
        for s in range(2):
            for_e[k, s] = to_e[:, s * B:(s + 1) * B]
            for_o[2 * k + s] = to_o[:, s * B:(s + 1) * B].astype(BF16)


def merge_kernel(row, for_e, from_o, row_out, message):
    core = lax.rem(lax.axis_index("gy"), 2)
    for k in range(len(FAR)):
        for t in range(3):
            row_out[k, t] = row[k, t]
        for s in range(2):
            row_out[k, core + s] += from_o[2 * k + s].astype(F32)
            message[tile(5 * k + 3 + s)] = for_e[k, s].astype(BF16)
        for t in range(3):
            message[tile(5 * k + t)] = row_out[k, t].astype(BF16)


def complete(core, row, for_e, message, k, t):
    mine = row[k, t]
    theirs = message(5 * k + t).astype(F32)
    if t == 1:
        mine = mine + message(5 * k + 3 + core).astype(F32)
        theirs = theirs + for_e[k, 1 - core]
    else:
        gets = (core == 0) == (t == 2)
        s = 1 if t == 2 else 0
        mine = mine + jnp.where(gets, message(5 * k + 3 + s).astype(F32), 0.0)
        theirs = theirs + jnp.where(gets, 0.0, for_e[k, s])
    return mine, theirs


def masks(codes, u, position, core):
    code = codes[u * PAD // 2:u * PAD // 2 + 1]
    other = position + 1 - 2 * core
    return (jnp.broadcast_to(code == position.astype(F32), (B, B)),
            jnp.broadcast_to(code == other.astype(F32), (B, B)))


def choose(units, core, position, codes, row, for_e, message, out):
    for k, (u, _) in enumerate(units):
        use_mine, use_theirs = masks(codes, u, position, core)
        for t in range(3):
            mine, theirs = complete(core, row, for_e, message, k, t)
            out[3 * k + t] = jnp.where(use_mine, mine, jnp.where(use_theirs, theirs, 0.0)).astype(BF16)


def choose_near_kernel(mine, row, for_e, message, halo_e, halo_o, out, wanted):
    c = lax.axis_index("gy")
    core, position = lax.rem(c, 2), lax.rem(c, 4)
    outer = jnp.logical_or(position == 0, position == 3)
    inferred = 6.0 - mine[...] - halo_e[1 - core, pl.ds(4 * B, PAD)].astype(F32)
    inferred = inferred - halo_o[pl.ds(14 * B, PAD)].astype(F32)
    codes = jnp.where(outer, message[pl.ds(20 * B, PAD)].astype(F32), inferred)
    wanted[...] = codes
    choose(NEAR, core, position, codes, row, for_e, lambda i: message[tile(i)], out)


def choose_far_kernel(wanted, row, for_e, message, out):
    c = lax.axis_index("gy")
    core, position = lax.rem(c, 2), lax.rem(c, 4)
    choose(FAR, core, position, wanted[...], row, for_e, lambda i: message[1 - core, tile(i)], out)


def finish(units, core, position, codes, row, for_e, message, arrived, out, buffer, sems):
    copies = []
    for k, (u, d) in enumerate(units):
        use_mine, use_theirs = masks(codes, u, position, core)
        for t in range(3):
            mine, theirs = complete(core, row, for_e, message, k, t)
            far = arrived[3 * k + t].astype(F32)
            buffer[k, t] = jnp.where(use_mine, mine, jnp.where(use_theirs, theirs, far))
        copies.append(pltpu.make_async_copy(buffer.at[k], out.at[u, 0, d], sems.at[k]))
        copies[-1].start()
    for copy in copies:
        copy.wait()


def finish_near_kernel(mine, row, for_e, message, arrived, out, buffer, sems):
    c = lax.axis_index("gy")
    core, position = lax.rem(c, 2), lax.rem(c, 4)
    finish(NEAR, core, position, mine[...], row, for_e, lambda i: message[tile(i)], arrived, out, buffer, sems)


def finish_far_kernel(mine, row, for_e, message, arrived, started, out, buffer, sems):
    del started
    c = lax.axis_index("gy")
    core, position = lax.rem(c, 2), lax.rem(c, 4)
    finish(FAR, core, position, mine[...], row, for_e, lambda i: message[1 - core, tile(i)], arrived, out, buffer, sems)


def on_device(a_tiles, a_links, p_own, p_side, p_links, coarse_pick):
    count, columns = lax.axis_size("gy"), lax.axis_size("gx")
    pairs = [(2 * g, 2 * g + 1) for g in range(count // 2)]
    cores = [list(pair) for pair in pairs]
    inside = pairs + [(b, a) for a, b in pairs]
    outside = [(i + 1, i + 2) for i in range(0, count - 2, 2)]
    outside = outside + [(b, a) for a, b in outside]
    across = [(i, i ^ 2) for i in range(count)]
    eastward = [(i, i + 1) for i in range(columns - 1)]
    westward = [(b, a) for a, b in eastward]
    bb = (B, B)
    near, far = len(NEAR), len(FAR)

    own, a, sides, east, west, msg_o, msg_e, mine = call(
        begin_kernel,
        [pltpu.with_memory_space_constraint(x, pltpu.HBM)
         for x in (a_links, p_links, coarse_pick.T, p_own, p_side, a_tiles)],
        [(p_own.shape, BF16), (a_tiles.shape, BF16), ((2, 2) + bb, BF16), ((6,) + bb, BF16), ((6,) + bb, BF16),
         ((14 * B + PAD, B), BF16), ((4 * B + PAD, B), BF16), ((PAD, B), F32)],
        in_specs=[HBM] * 6,
        scratch=[pltpu.SMEM(a_links.shape, jnp.int32), pltpu.SMEM(p_links.shape, jnp.int32),
                 pltpu.SMEM((1, 2), jnp.int32), pltpu.VMEM(p_side.shape, BF16), pltpu.SemaphoreType.DMA((6,))])
    halo_o = lax.ppermute(msg_o, "gy", outside)
    from_west = lax.ppermute(east, "gx", eastward)
    from_east = lax.ppermute(west, "gx", westward)
    halo_e = lax.all_gather(msg_e, "gy", axis_index_groups=cores)
    row_n, for_e_n, message_n = call(
        near_kernel, (own, a, sides, halo_e, halo_o, from_west, from_east),
        [((near, 3) + bb, F32), ((near, 2) + bb, F32), ((5 * near * B + PAD, B), BF16)])
    message_n = lax.ppermute(message_n, "gy", inside)
    row_f, for_e_f, for_o_f = call(
        far_kernel, (own, a, sides, from_west, from_east),
        [((far, 3) + bb, F32), ((far, 2) + bb, F32), ((2 * far,) + bb, BF16)])
    chosen_n, wanted = call(
        choose_near_kernel, (mine, row_n, for_e_n, message_n, halo_e, halo_o),
        [((3 * near,) + bb, BF16), ((PAD, B), F32)])
    for_o_f, chosen_n = lax.optimization_barrier((for_o_f, chosen_n))
    arrived_n = lax.ppermute(chosen_n, "gy", across)
    from_o_f = lax.ppermute(for_o_f, "gy", outside)
    row_f, message_f = call(
        merge_kernel, (row_f, for_e_f, from_o_f), [((far, 3) + bb, F32), ((5 * far * B, B), BF16)])
    message_f = lax.all_gather(message_f, "gy", axis_index_groups=cores)
    (chosen_f,) = call(choose_far_kernel, (wanted, row_f, for_e_f, message_f), [((3 * far,) + bb, BF16)])
    arrived_f = lax.ppermute(chosen_f, "gy", across)
    shape = (2, 1, 3, 3) + bb
    (out,) = call(
        finish_near_kernel, (mine, row_n, for_e_n, message_n, arrived_n), [(shape, F32)], out_specs=[HBM],
        scratch=[pltpu.VMEM((near, 3) + bb, F32), pltpu.SemaphoreType.DMA((near,))])
    (out,) = call(
        finish_far_kernel, (mine, row_f, for_e_f, message_f, arrived_f, out), [(shape, F32)],
        in_specs=[VMEM] * 5 + [HBM], out_specs=[HBM], aliases={5: 0},
        scratch=[pltpu.VMEM((far, 3) + bb, F32), pltpu.SemaphoreType.DMA((far,))])
    return out


def solution(mesh):
    return jax.shard_map(
        on_device,
        mesh=mesh,
        in_specs=(
            P("gx", "gy", None, None, None),
            P("gx", "gy", None),
            P("gx", "gy", None, None),
            P("gx", "gy", None, None, None),
            P("gx", "gy", None),
            P("gx", "gy"),
        ),
        out_specs=P("gx", "gy", None, None, None, None),
        check_vma=False,
    )
```

time: 123 us -> 50.9 us (0.41)
  the two profiles are of different devices: /device:TPU:346 before, /device:TPU:1 now
where the time goes in v2:
time: 50.9 us; the launch traced here: 50.6 us
  starting transfers between devices  21.7 us (43%)
  blocking collectives  11.9 us (23%)
  waiting for transfers between devices  10.5 us (21%)
  Pallas kernels  6.36 us (12%)
    all_gather x1, blocking collectives, on_device(): halo_e = lax.all_gather(msg_e, 'gy', axis_index_groups=cores)  9.64 us
    ppermute x1, starting transfers between devices, on_device(): message_n = lax.ppermute(message_n, 'gy', inside)  6.51 us
    pallas_call x8, Pallas kernels, call(): pl.pallas_call(kernel, in_specs=in_specs or [VMEM] * len(args), out_specs...  6.36 us
    ppermute x1, starting transfers between devices, on_device(): halo_o = lax.ppermute(msg_o, 'gy', outside)  4.93 us
    ppermute x1, waiting for transfers between devices, on_device(): arrived_n = lax.ppermute(chosen_n, 'gy', across)  3.86 us
    ppermute x1, waiting for transfers between devices, on_device(): arrived_f = lax.ppermute(chosen_f, 'gy', across)  3.23 us
    ppermute x1, starting transfers between devices, on_device(): from_west = lax.ppermute(east, 'gx', eastward)  3.21 us
    ppermute x1, waiting for transfers between devices, on_device(): from_o_f = lax.ppermute(for_o_f, 'gy', outside)  2.43 us
  transfers between devices with their start and end apart: 7, of which 4 were waited for; matrix products, arithmetic and copies ran while one was open for 0% of the time, Pallas kernels for 4%

profile of v2, /device:TPU:1, one launch (start us, length us, event | category | flops | bytes accessed | tf_op | source)
XLA Modules:
  0.0 50.6 jit_solution(7259956202475044717)
XLA Ops:
  0.0 2.2 %shard_map.64 = (bf16[2,4,128,128]{3,2,1,0:T(8,128)(2,1)S(1)}, bf16[2,4,5,128,128]{4,3,2,1,0:T(8,128)(2,1)S(1)}, bf16[2,2,128,128]{3,2,1,0:T(8,128)(2,1)S(1)}, b...) custom-call(s32[2,4,4]{2,1,0:T(4,128)} %a_links.1, ...), custom_call_target="tpu_custom_call" | custom-call | flops 1000000000 | bytes 1000000 | tf_op jit(solution)/shard_map/pallas_call | solution.py:21
  2.2 4.9 %collective-permute-start.2 = (bf16[1808,128]{1,0:T(8,128)(2,1)S(1)}, bf16[1808,128]{1,0:T(8,128)(2,1)S(1)}, u32[]{:S(2)}, u32[]{:S(2)}) collective-permute-start(bf16[1808,128]{1,0:T(8,128)(2,1)S(1)} %get-tuple-element.35), channel_id=1, source_target_pairs={{1,2},{3,4},{5,6},{7,8},{9,10},{11,12},{13,14},{15,16},{17,18},{19... | collective-permute-start | bytes 1388552 | tf_op jit(solution)/shard_map/ppermute | solution.py:317
  7.2 3.2 %collective-permute-start = (bf16[6,128,128]{2,1,0:T(8,128)(2,1)S(1)}, bf16[6,128,128]{2,1,0:T(8,128)(2,1)S(1)}, u32[]{:S(2)}, u32[]{:S(2)}) collective-permute-start(bf16[6,128,128]{2,1,0:T(8,128)(2,1)S(1)} %get-tuple-element.29), channel_id=1, source_target_pairs={{0,64},{64,128},{128,192},{192,256},{256,320},{320,384},{384,448},... | collective-permute-start | bytes 589832 | tf_op jit(solution)/shard_map/ppermute | solution.py:318
  10.4 1.3 %collective-permute-start.1 = (bf16[6,128,128]{2,1,0:T(8,128)(2,1)S(1)}, bf16[6,128,128]{2,1,0:T(8,128)(2,1)S(1)}, u32[]{:S(2)}, u32[]{:S(2)}) collective-permute-start(bf16[6,128,128]{2,1,0:T(8,128)(2,1)S(1)} %get-tuple-element.30), channel_id=1, source_target_pairs={{64,0},{128,64},{192,128},{256,192},{320,256},{384,320},{448,384},... | collective-permute-start | bytes 589832 | tf_op jit(solution)/shard_map/ppermute | solution.py:319
  11.7 9.6 %all-gather = bf16[1056,128]{1,0:T(8,128)(2,1)S(1)} all-gather(bf16[528,128]{1,0:T(8,128)(2,1)S(1)} %get-tuple-element.34), channel_id=2, replica_groups={{0,1},{2,3},{4,5},{6,7},{8,9},{10,11},{12,13},{14,15},{16,17},{18,19},{..., dimensions={0}, use_global_device_ids=true | all-gather | bytes 405504 | tf_op jit(solution)/shard_map/all_gather | solution.py:320
  21.3 0.0 collective-permute-done.from_west
  21.3 0.0 collective-permute-done.1.from_east
  21.3 0.0 collective-permute-done.2.halo_o
  21.3 1.2 %shard_map.66 = (f32[4,3,128,128]{3,2,1,0:T(8,128)S(1)}, f32[4,2,128,128]{3,2,1,0:T(8,128)S(1)}, bf16[2576,128]{1,0:T(8,128)(2,1)S(1)}) custom-call(bf16[2,4,128,128]{3,2,1,0:T(8,128)(2,1)S(1)} %get-tuple-element.26.own, bf16[2,4,5,128,128]{4,3,2,1,0:T(8,128)(2,1)S(1)} %get-tuple-element.27.a, bf16[2,2,128,128]{3,2,1,0:T(8,128)(2,1)S(1)} %get-tuple-element.28.sides, ...), custom_call_target="tpu_custom_call" | custom-call | flops 1000000000 | bytes 1000000 | tf_op jit(solution)/shard_map/pallas_call | solution.py:21
  22.6 6.5 %collective-permute-start.3 = (bf16[2576,128]{1,0:T(8,128)(2,1)S(1)}, bf16[2576,128]{1,0:T(8,128)(2,1)S(1)}, u32[]{:S(2)}, u32[]{:S(2)}) collective-permute-start(bf16[2576,128]{1,0:T(8,128)(2,1)S(1)} %get-tuple-element.38), channel_id=1, source_target_pairs={{0,1},{2,3},{4,5},{6,7},{8,9},{10,11},{12,13},{14,15},{16,17},{18,... | collective-permute-start | bytes 1978376 | tf_op jit(solution)/shard_map/ppermute | solution.py:324
  29.1 0.7 %shard_map.65 = (f32[2,3,128,128]{3,2,1,0:T(8,128)S(1)}, f32[2,2,128,128]{3,2,1,0:T(8,128)S(1)}, bf16[4,128,128]{2,1,0:T(8,128)(2,1)S(1)}) custom-call(bf16[2,4,128,128]{3,2,1,0:T(8,128)(2,1)S(1)} %get-tuple-element.26.own, bf16[2,4,5,128,128]{4,3,2,1,0:T(8,128)(2,1)S(1)} %get-tuple-element.27.a, bf16[2,2,128,128]{3,2,1,0:T(8,128)(2,1)S(1)} %get-tuple-element.28.sides, ...), custom_call_target="tpu_custom_call" | custom-call | flops 1000000000 | bytes 1000000 | tf_op jit(solution)/shard_map/pallas_call | solution.py:21
  29.8 1.0 %collective-permute-done.3.message = bf16[2576,128]{1,0:T(8,128)(2,1)S(1)} collective-permute-done((bf16[2576,128]{1,0:T(8,128)(2,1)S(1)}, bf16[2576,128]{1,0:T(8,128)(2,1)S(1)}, u32[]{:S(2)}, u32[]{:S(2)}) %collective-permute-start.3) | collective-permute-done | bytes 659488 | tf_op jit(solution)/shard_map/ppermute | solution.py:324
  30.8 0.2 shard_map.67
  31.0 1.9 %collective-permute-start.4 = (bf16[4,128,128]{2,1,0:T(8,128)(2,1)S(1)}, bf16[4,128,128]{2,1,0:T(8,128)(2,1)S(1)}, u32[]{:S(2)}, u32[]{:S(2)}) collective-permute-start(bf16[4,128,128]{2,1,0:T(8,128)(2,1)S(1)} %get-tuple-element.40), channel_id=1, source_target_pairs={{1,2},{3,4},{5,6},{7,8},{9,10},{11,12},{13,14},{15,16},{17,18},{19... | collective-permute-start | bytes 393224 | tf_op jit(solution)/shard_map/ppermute | solution.py:333
  33.0 1.9 %collective-permute-start.6 = (bf16[12,128,128]{2,1,0:T(8,128)(2,1)S(1)}, bf16[12,128,128]{2,1,0:T(8,128)(2,1)S(1)}, u32[]{:S(2)}, u32[]{:S(2)}) collective-permute-start(bf16[12,128,128]{2,1,0:T(8,128)(2,1)S(1)} %get-tuple-element.44), channel_id=1, source_target_pairs={{0,2},{1,3},{2,0},{3,1},{4,6},{5,7},{6,4},{7,5},{8,10},{9,11},{10,... | collective-permute-start | bytes 1179656 | tf_op jit(solution)/shard_map/ppermute | solution.py:332
  34.9 2.4 %collective-permute-done.4.from_o = bf16[4,128,128]{2,1,0:T(8,128)(2,1)S(1)} collective-permute-done((bf16[4,128,128]{2,1,0:T(8,128)(2,1)S(1)}, bf16[4,128,128]{2,1,0:T(8,128)(2,1)S(1)}, u32[]{:S(2)}, u32[]{:S(2)}) %collective-permute-start.4) | collective-permute-done | bytes 131104 | tf_op jit(solution)/shard_map/ppermute | solution.py:333
  37.3 0.1 shard_map.68
  37.4 2.3 %all-gather.1 = bf16[2560,128]{1,0:T(8,128)(2,1)S(1)} all-gather(bf16[1280,128]{1,0:T(8,128)(2,1)S(1)} %get-tuple-element.42), channel_id=3, replica_groups={{0,1},{2,3},{4,5},{6,7},{8,9},{10,11},{12,13},{14,15},{16,17},{18,19},{..., dimensions={0}, use_global_device_ids=true | all-gather | bytes 983040 | tf_op jit(solution)/shard_map/all_gather | solution.py:336
  39.7 0.1 shard_map.69
  39.8 1.9 %collective-permute-start.5 = (bf16[6,128,128]{2,1,0:T(8,128)(2,1)S(1)}, bf16[6,128,128]{2,1,0:T(8,128)(2,1)S(1)}, u32[]{:S(2)}, u32[]{:S(2)}) collective-permute-start(bf16[6,128,128]{2,1,0:T(8,128)(2,1)S(1)} %shard_map.69), channel_id=1, source_target_pairs={{0,2},{1,3},{2,0},{3,1},{4,6},{5,7},{6,4},{7,5},{8,10},{9,11},{10,... | collective-permute-start | bytes 589832 | tf_op jit(solution)/shard_map/ppermute | solution.py:338
  41.7 3.9 %collective-permute-done.6.arrived = bf16[12,128,128]{2,1,0:T(8,128)(2,1)S(1)} collective-permute-done((bf16[12,128,128]{2,1,0:T(8,128)(2,1)S(1)}, bf16[12,128,128]{2,1,0:T(8,128)(2,1)S(1)}, u32[]{:S(2)}, u32[]{:S(2)}) %collective-permute-start.6) | collective-permute-done | bytes 393248 | tf_op jit(solution)/shard_map/ppermute | solution.py:332
  45.6 1.0 %shard_map.70.started = f32[2,1,3,3,128,128]{5,4,3,2,1,0:T(8,128)} custom-call(f32[16,128]{1,0:T(8,128)S(1)} %get-tuple-element.25.mine, f32[4,3,128,128]{3,2,1,0:T(8,128)S(1)} %get-tuple-element.36.row, f32[4,2,128,128]{3,2,1,0:T(8,128)S(1)} %get-tuple-element.37.for_e, bf16[2576,128]{1,0:T(8,128)(2,1)S(1)} %collective-permute-done.3.message, ...), custom_call_target="tpu_custom_call" | custom-call | flops 1000000000 | bytes 1000000 | tf_op jit(solution)/shard_map/pallas_call | solution.py:21
  46.6 3.2 %collective-permute-done.5.arrived = bf16[6,128,128]{2,1,0:T(8,128)(2,1)S(1)} collective-permute-done((bf16[6,128,128]{2,1,0:T(8,128)(2,1)S(1)}, bf16[6,128,128]{2,1,0:T(8,128)(2,1)S(1)}, u32[]{:S(2)}, u32[]{:S(2)}) %collective-permute-start.5) | collective-permute-done | bytes 196640 | tf_op jit(solution)/shard_map/ppermute | solution.py:338
  49.8 0.8 %shard_map.71 = f32[2,1,3,3,128,128]{5,4,3,2,1,0:T(8,128)} custom-call(f32[16,128]{1,0:T(8,128)S(1)} %get-tuple-element.25.mine, f32[2,3,128,128]{3,2,1,0:T(8,128)S(1)} %get-tuple-element.41.row, f32[2,2,128,128]{3,2,1,0:T(8,128)S(1)} %get-tuple-element.32.for_e, bf16[2,1280,128]{2,1,0:T(8,128)(2,1)S(1)} %bitcast.4, ...), custom_call_target="tpu_custom_call", output_to_operand_aliasing={{}: (5, {})} | custom-call | flops 1000000000 | bytes 1000000 | tf_op jit(solution)/shard_map/pallas_call | solution.py:21
Async XLA Ops:
  2.2 19.1 %collective-permute-start.2 = (bf16[1808,128]{1,0:T(8,128)(2,1)S(1)}, bf16[1808,128]{1,0:T(8,128)(2,1)S(1)}, u32[]{:S(2)}, u32[]{:S(2)}) collective-permute-start(bf16[1808,128]{1,0:T(8,128)(2,1)S(1)} %get-tuple-element.35), channel_id=1, source_target_pairs={{1,2},{3,4},{5,6},{7,8},{9,10},{11,12},{13,14},{15,16},{17,18},{19... | collective-permute-start | bytes 1388552 | tf_op jit(solution)/shard_map/ppermute | solution.py:317
  7.2 14.2 %collective-permute-start = (bf16[6,128,128]{2,1,0:T(8,128)(2,1)S(1)}, bf16[6,128,128]{2,1,0:T(8,128)(2,1)S(1)}, u32[]{:S(2)}, u32[]{:S(2)}) collective-permute-start(bf16[6,128,128]{2,1,0:T(8,128)(2,1)S(1)} %get-tuple-element.29), channel_id=1, source_target_pairs={{0,64},{64,128},{128,192},{192,256},{256,320},{320,384},{384,448},... | collective-permute-start | bytes 589832 | tf_op jit(solution)/shard_map/ppermute | solution.py:318
  10.4 10.9 %collective-permute-start.1 = (bf16[6,128,128]{2,1,0:T(8,128)(2,1)S(1)}, bf16[6,128,128]{2,1,0:T(8,128)(2,1)S(1)}, u32[]{:S(2)}, u32[]{:S(2)}) collective-permute-start(bf16[6,128,128]{2,1,0:T(8,128)(2,1)S(1)} %get-tuple-element.30), channel_id=1, source_target_pairs={{64,0},{128,64},{192,128},{256,192},{320,256},{384,320},{448,384},... | collective-permute-start | bytes 589832 | tf_op jit(solution)/shard_map/ppermute | solution.py:319
  22.6 8.2 %collective-permute-start.3 = (bf16[2576,128]{1,0:T(8,128)(2,1)S(1)}, bf16[2576,128]{1,0:T(8,128)(2,1)S(1)}, u32[]{:S(2)}, u32[]{:S(2)}) collective-permute-start(bf16[2576,128]{1,0:T(8,128)(2,1)S(1)} %get-tuple-element.38), channel_id=1, source_target_pairs={{0,1},{2,3},{4,5},{6,7},{8,9},{10,11},{12,13},{14,15},{16,17},{18,... | collective-permute-start | bytes 1978376 | tf_op jit(solution)/shard_map/ppermute | solution.py:324
  31.0 6.3 %collective-permute-start.4 = (bf16[4,128,128]{2,1,0:T(8,128)(2,1)S(1)}, bf16[4,128,128]{2,1,0:T(8,128)(2,1)S(1)}, u32[]{:S(2)}, u32[]{:S(2)}) collective-permute-start(bf16[4,128,128]{2,1,0:T(8,128)(2,1)S(1)} %get-tuple-element.40), channel_id=1, source_target_pairs={{1,2},{3,4},{5,6},{7,8},{9,10},{11,12},{13,14},{15,16},{17,18},{19... | collective-permute-start | bytes 393224 | tf_op jit(solution)/shard_map/ppermute | solution.py:333
  33.0 12.6 %collective-permute-start.6 = (bf16[12,128,128]{2,1,0:T(8,128)(2,1)S(1)}, bf16[12,128,128]{2,1,0:T(8,128)(2,1)S(1)}, u32[]{:S(2)}, u32[]{:S(2)}) collective-permute-start(bf16[12,128,128]{2,1,0:T(8,128)(2,1)S(1)} %get-tuple-element.44), channel_id=1, source_target_pairs={{0,2},{1,3},{2,0},{3,1},{4,6},{5,7},{6,4},{7,5},{8,10},{9,11},{10,... | collective-permute-start | bytes 1179656 | tf_op jit(solution)/shard_map/ppermute | solution.py:332
  39.8 10.0 %collective-permute-start.5 = (bf16[6,128,128]{2,1,0:T(8,128)(2,1)S(1)}, bf16[6,128,128]{2,1,0:T(8,128)(2,1)S(1)}, u32[]{:S(2)}, u32[]{:S(2)}) collective-permute-start(bf16[6,128,128]{2,1,0:T(8,128)(2,1)S(1)} %shard_map.69), channel_id=1, source_target_pairs={{0,2},{1,3},{2,0},{3,1},{4,6},{5,7},{6,4},{7,5},{8,10},{9,11},{10,... | collective-permute-start | bytes 589832 | tf_op jit(solution)/shard_map/ppermute | solution.py:338

commit v3 on v2

--- a/solution.py
+++ b/solution.py
@@ -17,7 +17,7 @@
 LINK_TILE = {0: 1, 2: 2}
 
 
-def call(kernel, args, shapes, in_specs=None, out_specs=None, scratch=(), aliases=None, cost=1):
+def call(kernel, args, shapes, in_specs=None, out_specs=None, scratch=(), aliases=None, cost=0):
     return pl.pallas_call(
         kernel,
         in_specs=in_specs or [VMEM] * len(args),
@@ -26,7 +26,7 @@
         scratch_shapes=list(scratch),
         input_output_aliases=aliases or {},
         compiler_params=pltpu.CompilerParams(vmem_limit_bytes=32 * 2**20),
-        cost_estimate=pl.CostEstimate(flops=cost * 10**9, bytes_accessed=cost * 10**6, transcendentals=0),
+        cost_estimate=pl.CostEstimate(flops=cost, bytes_accessed=cost, transcendentals=0),
     )(*args)
 
 
@@ -135,8 +135,7 @@
     return first[:, :B], [first[:, B:], inner[0], inner[1], last[:, :B]], last[:, B:]
 
 
-def near_kernel(own, a, sides, halo_e, halo_o, from_west, from_east, row, for_e, message):
-    del from_west, from_east
+def near_kernel(own, a, sides, halo_e, halo_o, row, for_e, message):
     core = lax.rem(lax.axis_index("gy"), 2)
     even = core == 0
     zero = jnp.zeros((B, B), BF16)
@@ -319,8 +318,9 @@
     from_east = lax.ppermute(west, "gx", westward)
     halo_e = lax.all_gather(msg_e, "gy", axis_index_groups=cores)
     row_n, for_e_n, message_n = call(
-        near_kernel, (own, a, sides, halo_e, halo_o, from_west, from_east),
+        near_kernel, (own, a, sides, halo_e, halo_o),
         [((near, 3) + bb, F32), ((near, 2) + bb, F32), ((5 * near * B + PAD, B), BF16)])
+    message_n, from_west, from_east = lax.optimization_barrier((message_n, from_west, from_east))
     message_n = lax.ppermute(message_n, "gy", inside)
     row_f, for_e_f, for_o_f = call(
         far_kernel, (own, a, sides, from_west, from_east),
@@ -328,7 +328,6 @@
     chosen_n, wanted = call(
         choose_near_kernel, (mine, row_n, for_e_n, message_n, halo_e, halo_o),
         [((3 * near,) + bb, BF16), ((PAD, B), F32)])
-    for_o_f, chosen_n = lax.optimization_barrier((for_o_f, chosen_n))
     arrived_n = lax.ppermute(chosen_n, "gy", across)
     from_o_f = lax.ppermute(for_o_f, "gy", outside)
     row_f, message_f = call(

time: 50.9 us -> 48.6 us (0.955)
  starting transfers between devices: 21.7 us -> 20.5 us
  waiting for transfers between devices: 10.5 us -> 9.42 us
    ppermute x1, starting transfers between devices: 6.51 us -> 5.27 us  [on_device(): message_n = lax.ppermute(message_n, 'gy', inside)]
    ppermute x1, waiting for transfers between devices: 1 us -> 0.01 us  [on_device(): message_n = lax.ppermute(message_n, 'gy', inside)]
  transfers between devices with their start and end apart: 7 -> 7, of which waited for: 4 -> 3; matrix products, arithmetic and copies ran while one was open for 0% -> 0% of each run, Pallas kernels for 4% -> 7%
where the time goes in v3:
time: 48.6 us; the launch traced here: 48.3 us
  starting transfers between devices  20.5 us (42%)
  blocking collectives  11.9 us (24%)
  waiting for transfers between devices  9.42 us (19%)
  Pallas kernels  6.35 us (13%)
    all_gather x1, blocking collectives, on_device(): halo_e = lax.all_gather(msg_e, 'gy', axis_index_groups=cores)  9.64 us
    pallas_call x8, Pallas kernels, call(): pl.pallas_call(kernel, in_specs=in_specs or [VMEM] * len(args), out_specs...  6.35 us
    ppermute x1, starting transfers between devices, on_device(): message_n = lax.ppermute(message_n, 'gy', inside)  5.27 us
    ppermute x1, starting transfers between devices, on_device(): halo_o = lax.ppermute(msg_o, 'gy', outside)  4.93 us
    ppermute x1, waiting for transfers between devices, on_device(): arrived_n = lax.ppermute(chosen_n, 'gy', across)  3.96 us
    ppermute x1, waiting for transfers between devices, on_device(): arrived_f = lax.ppermute(chosen_f, 'gy', across)  3.23 us
    ppermute x1, starting transfers between devices, on_device(): from_west = lax.ppermute(east, 'gx', eastward)  3.21 us
    all_gather x1, blocking collectives, on_device(): message_f = lax.all_gather(message_f, 'gy', axis_index_groups=cores)  2.28 us
  transfers between devices with their start and end apart: 7, of which 3 were waited for; matrix products, arithmetic and copies ran while one was open for 0% of the time, Pallas kernels for 7%

profile of v3, /device:TPU:1, one launch (start us, length us, event | category | flops | bytes accessed | tf_op | source)
XLA Modules:
  0.0 48.3 jit_solution(11349610292368641309)
XLA Ops:
  0.0 2.2 %shard_map.64 = (bf16[2,4,128,128]{3,2,1,0:T(8,128)(2,1)S(1)}, bf16[2,4,5,128,128]{4,3,2,1,0:T(8,128)(2,1)S(1)}, bf16[2,2,128,128]{3,2,1,0:T(8,128)(2,1)S(1)}, b...) custom-call(s32[2,4,4]{2,1,0:T(4,128)} %a_links.1, ...), custom_call_target="tpu_custom_call" | custom-call | tf_op jit(solution)/shard_map/pallas_call | solution.py:21
  2.2 4.9 %collective-permute-start = (bf16[1808,128]{1,0:T(8,128)(2,1)S(1)}, bf16[1808,128]{1,0:T(8,128)(2,1)S(1)}, u32[]{:S(2)}, u32[]{:S(2)}) collective-permute-start(bf16[1808,128]{1,0:T(8,128)(2,1)S(1)} %get-tuple-element.31), channel_id=1, source_target_pairs={{1,2},{3,4},{5,6},{7,8},{9,10},{11,12},{13,14},{15,16},{17,18},{19... | collective-permute-start | bytes 1388552 | tf_op jit(solution)/shard_map/ppermute | solution.py:316
  7.2 3.2 %collective-permute-start.1 = (bf16[6,128,128]{2,1,0:T(8,128)(2,1)S(1)}, bf16[6,128,128]{2,1,0:T(8,128)(2,1)S(1)}, u32[]{:S(2)}, u32[]{:S(2)}) collective-permute-start(bf16[6,128,128]{2,1,0:T(8,128)(2,1)S(1)} %get-tuple-element.33), channel_id=1, source_target_pairs={{0,64},{64,128},{128,192},{192,256},{256,320},{320,384},{384,448},... | collective-permute-start | bytes 589832 | tf_op jit(solution)/shard_map/ppermute | solution.py:317
  10.4 1.3 %collective-permute-start.2 = (bf16[6,128,128]{2,1,0:T(8,128)(2,1)S(1)}, bf16[6,128,128]{2,1,0:T(8,128)(2,1)S(1)}, u32[]{:S(2)}, u32[]{:S(2)}) collective-permute-start(bf16[6,128,128]{2,1,0:T(8,128)(2,1)S(1)} %get-tuple-element.34), channel_id=1, source_target_pairs={{64,0},{128,64},{192,128},{256,192},{320,256},{384,320},{448,384},... | collective-permute-start | bytes 589832 | tf_op jit(solution)/shard_map/ppermute | solution.py:318
  11.7 9.6 %all-gather = bf16[1056,128]{1,0:T(8,128)(2,1)S(1)} all-gather(bf16[528,128]{1,0:T(8,128)(2,1)S(1)} %get-tuple-element.30), channel_id=2, replica_groups={{0,1},{2,3},{4,5},{6,7},{8,9},{10,11},{12,13},{14,15},{16,17},{18,19},{..., dimensions={0}, use_global_device_ids=true | all-gather | bytes 405504 | tf_op jit(solution)/shard_map/all_gather | solution.py:319
  21.3 0.0 collective-permute-done.halo_o
  21.3 1.2 %shard_map.65 = (f32[4,3,128,128]{3,2,1,0:T(8,128)S(1)}, f32[4,2,128,128]{3,2,1,0:T(8,128)S(1)}, bf16[2576,128]{1,0:T(8,128)(2,1)S(1)}) custom-call(bf16[2,4,128,128]{3,2,1,0:T(8,128)(2,1)S(1)} %get-tuple-element.27.own, bf16[2,4,5,128,128]{4,3,2,1,0:T(8,128)(2,1)S(1)} %get-tuple-element.28.a, bf16[2,2,128,128]{3,2,1,0:T(8,128)(2,1)S(1)} %get-tuple-element.29.sides, ...), custom_call_target="tpu_custom_call" | custom-call | tf_op jit(solution)/shard_map/pallas_call | solution.py:21
  22.6 0.0 collective-permute-done.1.from_west
  22.6 0.0 collective-permute-done.2.from_east
  22.6 5.3 %collective-permute-start.4 = (bf16[2576,128]{1,0:T(8,128)(2,1)S(1)}, bf16[2576,128]{1,0:T(8,128)(2,1)S(1)}, u32[]{:S(2)}, u32[]{:S(2)}) collective-permute-start(bf16[2576,128]{1,0:T(8,128)(2,1)S(1)} %get-tuple-element.44), channel_id=1, source_target_pairs={{0,1},{2,3},{4,5},{6,7},{8,9},{10,11},{12,13},{14,15},{16,17},{18,... | collective-permute-start | bytes 1978376 | tf_op jit(solution)/shard_map/ppermute | solution.py:324
  27.9 0.7 %shard_map.66 = (f32[2,3,128,128]{3,2,1,0:T(8,128)S(1)}, f32[2,2,128,128]{3,2,1,0:T(8,128)S(1)}, bf16[4,128,128]{2,1,0:T(8,128)(2,1)S(1)}) custom-call(bf16[2,4,128,128]{3,2,1,0:T(8,128)(2,1)S(1)} %get-tuple-element.27.own, bf16[2,4,5,128,128]{4,3,2,1,0:T(8,128)(2,1)S(1)} %get-tuple-element.28.a, bf16[2,2,128,128]{3,2,1,0:T(8,128)(2,1)S(1)} %get-tuple-element.29.sides, ...), custom_call_target="tpu_custom_call" | custom-call | tf_op jit(solution)/shard_map/pallas_call | solution.py:21
  28.6 1.9 %collective-permute-start.3 = (bf16[4,128,128]{2,1,0:T(8,128)(2,1)S(1)}, bf16[4,128,128]{2,1,0:T(8,128)(2,1)S(1)}, u32[]{:S(2)}, u32[]{:S(2)}) collective-permute-start(bf16[4,128,128]{2,1,0:T(8,128)(2,1)S(1)} %get-tuple-element.39), channel_id=1, source_target_pairs={{1,2},{3,4},{5,6},{7,8},{9,10},{11,12},{13,14},{15,16},{17,18},{19... | collective-permute-start | bytes 393224 | tf_op jit(solution)/shard_map/ppermute | solution.py:332
  30.5 0.0 collective-permute-done.4.message
  30.5 0.2 shard_map.68
  30.7 1.9 %collective-permute-start.6 = (bf16[12,128,128]{2,1,0:T(8,128)(2,1)S(1)}, bf16[12,128,128]{2,1,0:T(8,128)(2,1)S(1)}, u32[]{:S(2)}, u32[]{:S(2)}) collective-permute-start(bf16[12,128,128]{2,1,0:T(8,128)(2,1)S(1)} %get-tuple-element.46), channel_id=1, source_target_pairs={{0,2},{1,3},{2,0},{3,1},{4,6},{5,7},{6,4},{7,5},{8,10},{9,11},{10,... | collective-permute-start | bytes 1179656 | tf_op jit(solution)/shard_map/ppermute | solution.py:331
  32.7 2.2 %collective-permute-done.3.from_o = bf16[4,128,128]{2,1,0:T(8,128)(2,1)S(1)} collective-permute-done((bf16[4,128,128]{2,1,0:T(8,128)(2,1)S(1)}, bf16[4,128,128]{2,1,0:T(8,128)(2,1)S(1)}, u32[]{:S(2)}, u32[]{:S(2)}) %collective-permute-start.3) | collective-permute-done | bytes 131104 | tf_op jit(solution)/shard_map/ppermute | solution.py:332
  34.9 0.1 shard_map.67
  35.0 2.3 %all-gather.1 = bf16[2560,128]{1,0:T(8,128)(2,1)S(1)} all-gather(bf16[1280,128]{1,0:T(8,128)(2,1)S(1)} %get-tuple-element.41), channel_id=3, replica_groups={{0,1},{2,3},{4,5},{6,7},{8,9},{10,11},{12,13},{14,15},{16,17},{18,19},{..., dimensions={0}, use_global_device_ids=true | all-gather | bytes 983040 | tf_op jit(solution)/shard_map/all_gather | solution.py:335
  37.2 0.1 shard_map.69
  37.3 1.9 %collective-permute-start.5 = (bf16[6,128,128]{2,1,0:T(8,128)(2,1)S(1)}, bf16[6,128,128]{2,1,0:T(8,128)(2,1)S(1)}, u32[]{:S(2)}, u32[]{:S(2)}) collective-permute-start(bf16[6,128,128]{2,1,0:T(8,128)(2,1)S(1)} %shard_map.69), channel_id=1, source_target_pairs={{0,2},{1,3},{2,0},{3,1},{4,6},{5,7},{6,4},{7,5},{8,10},{9,11},{10,... | collective-permute-start | bytes 589832 | tf_op jit(solution)/shard_map/ppermute | solution.py:337
  39.3 4.0 %collective-permute-done.6.arrived = bf16[12,128,128]{2,1,0:T(8,128)(2,1)S(1)} collective-permute-done((bf16[12,128,128]{2,1,0:T(8,128)(2,1)S(1)}, bf16[12,128,128]{2,1,0:T(8,128)(2,1)S(1)}, u32[]{:S(2)}, u32[]{:S(2)}) %collective-permute-start.6) | collective-permute-done | bytes 393248 | tf_op jit(solution)/shard_map/ppermute | solution.py:331
  43.2 1.0 %shard_map.70.started = f32[2,1,3,3,128,128]{5,4,3,2,1,0:T(8,128)} custom-call(f32[16,128]{1,0:T(8,128)S(1)} %get-tuple-element.26.mine, f32[4,3,128,128]{3,2,1,0:T(8,128)S(1)} %get-tuple-element.42.row, f32[4,2,128,128]{3,2,1,0:T(8,128)S(1)} %get-tuple-element.43.for_e, bf16[2576,128]{1,0:T(8,128)(2,1)S(1)} %collective-permute-done.4.message, ...), custom_call_target="tpu_custom_call" | custom-call | tf_op jit(solution)/shard_map/pallas_call | solution.py:21
  44.2 3.2 %collective-permute-done.5.arrived = bf16[6,128,128]{2,1,0:T(8,128)(2,1)S(1)} collective-permute-done((bf16[6,128,128]{2,1,0:T(8,128)(2,1)S(1)}, bf16[6,128,128]{2,1,0:T(8,128)(2,1)S(1)}, u32[]{:S(2)}, u32[]{:S(2)}) %collective-permute-start.5) | collective-permute-done | bytes 196640 | tf_op jit(solution)/shard_map/ppermute | solution.py:337
  47.4 0.8 %shard_map.71 = f32[2,1,3,3,128,128]{5,4,3,2,1,0:T(8,128)} custom-call(f32[16,128]{1,0:T(8,128)S(1)} %get-tuple-element.26.mine, f32[2,3,128,128]{3,2,1,0:T(8,128)S(1)} %get-tuple-element.40.row, f32[2,2,128,128]{3,2,1,0:T(8,128)S(1)} %get-tuple-element.38.for_e, bf16[2,1280,128]{2,1,0:T(8,128)(2,1)S(1)} %bitcast.4, ...), custom_call_target="tpu_custom_call", output_to_operand_aliasing={{}: (5, {})} | custom-call | tf_op jit(solution)/shard_map/pallas_call | solution.py:21
Async XLA Ops:
  2.2 19.1 %collective-permute-start = (bf16[1808,128]{1,0:T(8,128)(2,1)S(1)}, bf16[1808,128]{1,0:T(8,128)(2,1)S(1)}, u32[]{:S(2)}, u32[]{:S(2)}) collective-permute-start(bf16[1808,128]{1,0:T(8,128)(2,1)S(1)} %get-tuple-element.31), channel_id=1, source_target_pairs={{1,2},{3,4},{5,6},{7,8},{9,10},{11,12},{13,14},{15,16},{17,18},{19... | collective-permute-start | bytes 1388552 | tf_op jit(solution)/shard_map/ppermute | solution.py:316
  7.2 15.4 %collective-permute-start.1 = (bf16[6,128,128]{2,1,0:T(8,128)(2,1)S(1)}, bf16[6,128,128]{2,1,0:T(8,128)(2,1)S(1)}, u32[]{:S(2)}, u32[]{:S(2)}) collective-permute-start(bf16[6,128,128]{2,1,0:T(8,128)(2,1)S(1)} %get-tuple-element.33), channel_id=1, source_target_pairs={{0,64},{64,128},{128,192},{192,256},{256,320},{320,384},{384,448},... | collective-permute-start | bytes 589832 | tf_op jit(solution)/shard_map/ppermute | solution.py:317
  10.4 12.2 %collective-permute-start.2 = (bf16[6,128,128]{2,1,0:T(8,128)(2,1)S(1)}, bf16[6,128,128]{2,1,0:T(8,128)(2,1)S(1)}, u32[]{:S(2)}, u32[]{:S(2)}) collective-permute-start(bf16[6,128,128]{2,1,0:T(8,128)(2,1)S(1)} %get-tuple-element.34), channel_id=1, source_target_pairs={{64,0},{128,64},{192,128},{256,192},{320,256},{384,320},{448,384},... | collective-permute-start | bytes 589832 | tf_op jit(solution)/shard_map/ppermute | solution.py:318
  22.6 7.9 %collective-permute-start.4 = (bf16[2576,128]{1,0:T(8,128)(2,1)S(1)}, bf16[2576,128]{1,0:T(8,128)(2,1)S(1)}, u32[]{:S(2)}, u32[]{:S(2)}) collective-permute-start(bf16[2576,128]{1,0:T(8,128)(2,1)S(1)} %get-tuple-element.44), channel_id=1, source_target_pairs={{0,1},{2,3},{4,5},{6,7},{8,9},{10,11},{12,13},{14,15},{16,17},{18,... | collective-permute-start | bytes 1978376 | tf_op jit(solution)/shard_map/ppermute | solution.py:324
  28.6 6.3 %collective-permute-start.3 = (bf16[4,128,128]{2,1,0:T(8,128)(2,1)S(1)}, bf16[4,128,128]{2,1,0:T(8,128)(2,1)S(1)}, u32[]{:S(2)}, u32[]{:S(2)}) collective-permute-start(bf16[4,128,128]{2,1,0:T(8,128)(2,1)S(1)} %get-tuple-element.39), channel_id=1, source_target_pairs={{1,2},{3,4},{5,6},{7,8},{9,10},{11,12},{13,14},{15,16},{17,18},{19... | collective-permute-start | bytes 393224 | tf_op jit(solution)/shard_map/ppermute | solution.py:332
  30.7 12.5 %collective-permute-start.6 = (bf16[12,128,128]{2,1,0:T(8,128)(2,1)S(1)}, bf16[12,128,128]{2,1,0:T(8,128)(2,1)S(1)}, u32[]{:S(2)}, u32[]{:S(2)}) collective-permute-start(bf16[12,128,128]{2,1,0:T(8,128)(2,1)S(1)} %get-tuple-element.46), channel_id=1, source_target_pairs={{0,2},{1,3},{2,0},{3,1},{4,6},{5,7},{6,4},{7,5},{8,10},{9,11},{10,... | collective-permute-start | bytes 1179656 | tf_op jit(solution)/shard_map/ppermute | solution.py:331
  37.3 10.1 %collective-permute-start.5 = (bf16[6,128,128]{2,1,0:T(8,128)(2,1)S(1)}, bf16[6,128,128]{2,1,0:T(8,128)(2,1)S(1)}, u32[]{:S(2)}, u32[]{:S(2)}) collective-permute-start(bf16[6,128,128]{2,1,0:T(8,128)(2,1)S(1)} %shard_map.69), channel_id=1, source_target_pairs={{0,2},{1,3},{2,0},{3,1},{4,6},{5,7},{6,4},{7,5},{8,10},{9,11},{10,... | collective-permute-start | bytes 589832 | tf_op jit(solution)/shard_map/ppermute | solution.py:337

commit v4 on v3

--- a/solution.py
+++ b/solution.py
@@ -83,10 +83,13 @@
             for k in range(4):
                 a[u, j, k + 1] = a[u, j, k + 1] * s_links[u, j, k].astype(F32).astype(BF16)
 
-    def fill(j_e, k_e, j_o, k_o):
+    def fill_e(j, k):
         for u in range(2):
-            msg_e[tile(2 * u)] = own[u, j_e]
-            msg_e[tile(2 * u + 1)] = sides[u, k_e]
+            msg_e[tile(2 * u)] = own[u, j]
+            msg_e[tile(2 * u + 1)] = sides[u, k]
+
+    def fill_o(j_o, k_o):
+        for u in range(2):
             side, block = sides[u, k_o], own[u, j_o]
             other_side, other_block = sides[1 - u, k_o], own[1 - u, j_o]
             zero = jnp.zeros((B, B), BF16)
@@ -109,13 +112,10 @@
             for i in range(5):
                 msg_o[tile(7 * u + 2 + i)] = result[:, i * B:(i + 1) * B]
 
-    @pl.when(core == 0)
-    def _():
-        fill(3, 1, 0, 0)
-
-    @pl.when(core == 1)
-    def _():
-        fill(0, 0, 3, 1)
+    pl.when(core == 0)(lambda: fill_e(3, 1))
+    pl.when(core == 1)(lambda: fill_e(0, 0))
+    pl.when(jnp.logical_and(core == 0, keep[0]))(lambda: fill_o(0, 0))
+    pl.when(jnp.logical_and(core == 1, keep[1]))(lambda: fill_o(3, 1))
 
 
 def reduce_units(own, u, products, count):
@@ -247,7 +247,8 @@
             out[3 * k + t] = jnp.where(use_mine, mine, jnp.where(use_theirs, theirs, 0.0)).astype(BF16)
 
 
-def choose_near_kernel(mine, row, for_e, message, halo_e, halo_o, out, wanted):
+def choose_near_kernel(mine, row, for_e, message, halo_e, halo_o, row_far, out, wanted):
+    del row_far
     c = lax.axis_index("gy")
     core, position = lax.rem(c, 2), lax.rem(c, 4)
     outer = jnp.logical_or(position == 0, position == 3)
@@ -320,13 +321,12 @@
     row_n, for_e_n, message_n = call(
         near_kernel, (own, a, sides, halo_e, halo_o),
         [((near, 3) + bb, F32), ((near, 2) + bb, F32), ((5 * near * B + PAD, B), BF16)])
-    message_n, from_west, from_east = lax.optimization_barrier((message_n, from_west, from_east))
     message_n = lax.ppermute(message_n, "gy", inside)
     row_f, for_e_f, for_o_f = call(
         far_kernel, (own, a, sides, from_west, from_east),
-        [((far, 3) + bb, F32), ((far, 2) + bb, F32), ((2 * far,) + bb, BF16)])
+        [((far, 3) + bb, F32), ((far, 2) + bb, F32), ((2 * far,) + bb, BF16)], cost=2 * 10**10)
     chosen_n, wanted = call(
-        choose_near_kernel, (mine, row_n, for_e_n, message_n, halo_e, halo_o),
+        choose_near_kernel, (mine, row_n, for_e_n, message_n, halo_e, halo_o, row_f),
         [((3 * near,) + bb, BF16), ((PAD, B), F32)])
     arrived_n = lax.ppermute(chosen_n, "gy", across)
     from_o_f = lax.ppermute(for_o_f, "gy", outside)
@@ -338,7 +338,7 @@
     shape = (2, 1, 3, 3) + bb
     (out,) = call(
         finish_near_kernel, (mine, row_n, for_e_n, message_n, arrived_n), [(shape, F32)], out_specs=[HBM],
-        scratch=[pltpu.VMEM((near, 3) + bb, F32), pltpu.SemaphoreType.DMA((near,))])
+        scratch=[pltpu.VMEM((near, 3) + bb, F32), pltpu.SemaphoreType.DMA((near,))], cost=2 * 10**10)
     (out,) = call(
         finish_far_kernel, (mine, row_f, for_e_f, message_f, arrived_f, out), [(shape, F32)],
         in_specs=[VMEM] * 5 + [HBM], out_specs=[HBM], aliases={5: 0},

time: 48.6 us -> 52.7 us (1.084)
  the two profiles are of different devices: /device:TPU:1 before, /device:TPU:8 now
where the time goes in v4:
time: 52.7 us; the launch traced here: 52.4 us
  starting transfers between devices  24.4 us (46%)
  blocking collectives  15.6 us (30%)
  waiting for transfers between devices  6.53 us (12%)
  Pallas kernels  5.81 us (11%)
    all_gather x1, blocking collectives, on_device(): message_f = lax.all_gather(message_f, 'gy', axis_index_groups=cores)  13.6 us
    ppermute x1, starting transfers between devices, on_device(): from_east = lax.ppermute(west, 'gx', westward)  12.8 us
    pallas_call x8, Pallas kernels, call(): pl.pallas_call(kernel, in_specs=in_specs or [VMEM] * len(args), out_specs...  5.81 us
    ppermute x1, waiting for transfers between devices, on_device(): arrived_f = lax.ppermute(chosen_f, 'gy', across)  5.32 us
    ppermute x1, starting transfers between devices, on_device(): from_west = lax.ppermute(east, 'gx', eastward)  3.48 us
    ppermute x1, starting transfers between devices, on_device(): arrived_f = lax.ppermute(chosen_f, 'gy', across)  2.75 us
    ppermute x1, starting transfers between devices, on_device(): message_n = lax.ppermute(message_n, 'gy', inside)  2.05 us
    all_gather x1, blocking collectives, on_device(): halo_e = lax.all_gather(msg_e, 'gy', axis_index_groups=cores)  2 us
  transfers between devices with their start and end apart: 7, of which 2 were waited for; matrix products, arithmetic and copies ran while one was open for 0% of the time, Pallas kernels for 6%

profile of v4, /device:TPU:8, one launch (start us, length us, event | category | flops | bytes accessed | tf_op | source)
XLA Modules:
  0.0 52.4 jit_solution(11054872510540498209)
XLA Ops:
  0.0 1.7 %shard_map.64 = (bf16[2,4,128,128]{3,2,1,0:T(8,128)(2,1)S(1)}, bf16[2,4,5,128,128]{4,3,2,1,0:T(8,128)(2,1)S(1)}, bf16[2,2,128,128]{3,2,1,0:T(8,128)(2,1)S(1)}, b...) custom-call(s32[2,4,4]{2,1,0:T(4,128)} %a_links.1, ...), custom_call_target="tpu_custom_call" | custom-call | tf_op jit(solution)/shard_map/pallas_call | solution.py:21
  1.7 0.7 %collective-permute-start.3 = (bf16[1808,128]{1,0:T(8,128)(2,1)S(1)}, bf16[1808,128]{1,0:T(8,128)(2,1)S(1)}, u32[]{:S(2)}, u32[]{:S(2)}) collective-permute-start(bf16[1808,128]{1,0:T(8,128)(2,1)S(1)} %get-tuple-element.35), channel_id=1, source_target_pairs={{1,2},{3,4},{5,6},{7,8},{9,10},{11,12},{13,14},{15,16},{17,18},{19... | collective-permute-start | bytes 1388552 | tf_op jit(solution)/shard_map/ppermute | solution.py:317
  2.4 3.5 %collective-permute-start = (bf16[6,128,128]{2,1,0:T(8,128)(2,1)S(1)}, bf16[6,128,128]{2,1,0:T(8,128)(2,1)S(1)}, u32[]{:S(2)}, u32[]{:S(2)}) collective-permute-start(bf16[6,128,128]{2,1,0:T(8,128)(2,1)S(1)} %get-tuple-element.27), channel_id=1, source_target_pairs={{0,64},{64,128},{128,192},{192,256},{256,320},{320,384},{384,448},... | collective-permute-start | bytes 589832 | tf_op jit(solution)/shard_map/ppermute | solution.py:318
  5.9 12.8 %collective-permute-start.1 = (bf16[6,128,128]{2,1,0:T(8,128)(2,1)S(1)}, bf16[6,128,128]{2,1,0:T(8,128)(2,1)S(1)}, u32[]{:S(2)}, u32[]{:S(2)}) collective-permute-start(bf16[6,128,128]{2,1,0:T(8,128)(2,1)S(1)} %get-tuple-element.28), channel_id=1, source_target_pairs={{64,0},{128,64},{192,128},{256,192},{320,256},{384,320},{448,384},... | collective-permute-start | bytes 589832 | tf_op jit(solution)/shard_map/ppermute | solution.py:319
  18.7 2.0 %all-gather.1 = bf16[1056,128]{1,0:T(8,128)(2,1)S(1)} all-gather(bf16[528,128]{1,0:T(8,128)(2,1)S(1)} %get-tuple-element.34), channel_id=3, replica_groups={{0,1},{2,3},{4,5},{6,7},{8,9},{10,11},{12,13},{14,15},{16,17},{18,19},{..., dimensions={0}, use_global_device_ids=true | all-gather | bytes 405504 | tf_op jit(solution)/shard_map/all_gather | solution.py:320
  20.7 0.0 collective-permute-done.3.halo_o
  20.7 1.2 %shard_map.67 = (f32[4,3,128,128]{3,2,1,0:T(8,128)S(1)}, f32[4,2,128,128]{3,2,1,0:T(8,128)S(1)}, bf16[2576,128]{1,0:T(8,128)(2,1)S(1)}) custom-call(bf16[2,4,128,128]{3,2,1,0:T(8,128)(2,1)S(1)} %get-tuple-element.24.own, bf16[2,4,5,128,128]{4,3,2,1,0:T(8,128)(2,1)S(1)} %get-tuple-element.25.a, bf16[2,2,128,128]{3,2,1,0:T(8,128)(2,1)S(1)} %get-tuple-element.26.sides, ...), custom_call_target="tpu_custom_call" | custom-call | tf_op jit(solution)/shard_map/pallas_call | solution.py:21
  22.0 2.1 %collective-permute-start.4 = (bf16[2576,128]{1,0:T(8,128)(2,1)S(1)}, bf16[2576,128]{1,0:T(8,128)(2,1)S(1)}, u32[]{:S(2)}, u32[]{:S(2)}) collective-permute-start(bf16[2576,128]{1,0:T(8,128)(2,1)S(1)} %get-tuple-element.38), channel_id=1, source_target_pairs={{0,1},{2,3},{4,5},{6,7},{8,9},{10,11},{12,13},{14,15},{16,17},{18,... | collective-permute-start | bytes 1978376 | tf_op jit(solution)/shard_map/ppermute | solution.py:324
  24.0 0.0 collective-permute-done.from_west
  24.0 0.0 collective-permute-done.1.from_east
  24.0 0.7 %shard_map.65 = (f32[2,3,128,128]{3,2,1,0:T(8,128)S(1)}, f32[2,2,128,128]{3,2,1,0:T(8,128)S(1)}, bf16[4,128,128]{2,1,0:T(8,128)(2,1)S(1)}) custom-call(bf16[2,4,128,128]{3,2,1,0:T(8,128)(2,1)S(1)} %get-tuple-element.24.own, bf16[2,4,5,128,128]{4,3,2,1,0:T(8,128)(2,1)S(1)} %get-tuple-element.25.a, bf16[2,2,128,128]{3,2,1,0:T(8,128)(2,1)S(1)} %get-tuple-element.26.sides, ...), custom_call_target="tpu_custom_call" | custom-call | flops 20000000000 | bytes 20000000000 | tf_op jit(solution)/shard_map/pallas_call | solution.py:21
  24.7 1.2 %collective-permute-done.4.message = bf16[2576,128]{1,0:T(8,128)(2,1)S(1)} collective-permute-done((bf16[2576,128]{1,0:T(8,128)(2,1)S(1)}, bf16[2576,128]{1,0:T(8,128)(2,1)S(1)}, u32[]{:S(2)}, u32[]{:S(2)}) %collective-permute-start.4) | collective-permute-done | bytes 659488 | tf_op jit(solution)/shard_map/ppermute | solution.py:324
  25.9 0.2 shard_map.68
  26.2 1.9 %collective-permute-start.6 = (bf16[12,128,128]{2,1,0:T(8,128)(2,1)S(1)}, bf16[12,128,128]{2,1,0:T(8,128)(2,1)S(1)}, u32[]{:S(2)}, u32[]{:S(2)}) collective-permute-start(bf16[12,128,128]{2,1,0:T(8,128)(2,1)S(1)} %get-tuple-element.40), channel_id=1, source_target_pairs={{0,2},{1,3},{2,0},{3,1},{4,6},{5,7},{6,4},{7,5},{8,10},{9,11},{10,... | collective-permute-start | bytes 1179656 | tf_op jit(solution)/shard_map/ppermute | solution.py:331
  28.1 0.7 %collective-permute-start.2 = (bf16[4,128,128]{2,1,0:T(8,128)(2,1)S(1)}, bf16[4,128,128]{2,1,0:T(8,128)(2,1)S(1)}, u32[]{:S(2)}, u32[]{:S(2)}) collective-permute-start(bf16[4,128,128]{2,1,0:T(8,128)(2,1)S(1)} %get-tuple-element.31), channel_id=1, source_target_pairs={{1,2},{3,4},{5,6},{7,8},{9,10},{11,12},{13,14},{15,16},{17,18},{19... | collective-permute-start | bytes 393224 | tf_op jit(solution)/shard_map/ppermute | solution.py:332
  28.8 0.0 collective-permute-done.2.from_o
  28.8 0.1 shard_map.66
  28.9 13.6 %all-gather = bf16[2560,128]{1,0:T(8,128)(2,1)S(1)} all-gather(bf16[1280,128]{1,0:T(8,128)(2,1)S(1)} %get-tuple-element.33), channel_id=2, replica_groups={{0,1},{2,3},{4,5},{6,7},{8,9},{10,11},{12,13},{14,15},{16,17},{18,19},{..., dimensions={0}, use_global_device_ids=true | all-gather | bytes 983040 | tf_op jit(solution)/shard_map/all_gather | solution.py:335
  42.4 0.1 shard_map.69
  42.5 2.8 %collective-permute-start.5 = (bf16[6,128,128]{2,1,0:T(8,128)(2,1)S(1)}, bf16[6,128,128]{2,1,0:T(8,128)(2,1)S(1)}, u32[]{:S(2)}, u32[]{:S(2)}) collective-permute-start(bf16[6,128,128]{2,1,0:T(8,128)(2,1)S(1)} %shard_map.69), channel_id=1, source_target_pairs={{0,2},{1,3},{2,0},{3,1},{4,6},{5,7},{6,4},{7,5},{8,10},{9,11},{10,... | collective-permute-start | bytes 589832 | tf_op jit(solution)/shard_map/ppermute | solution.py:337
  45.3 0.0 collective-permute-done.6.arrived
  45.3 1.0 %shard_map.70.started = f32[2,1,3,3,128,128]{5,4,3,2,1,0:T(8,128)} custom-call(f32[16,128]{1,0:T(8,128)S(1)} %get-tuple-element.23.mine, f32[4,3,128,128]{3,2,1,0:T(8,128)S(1)} %get-tuple-element.36.row, f32[4,2,128,128]{3,2,1,0:T(8,128)S(1)} %get-tuple-element.37.for_e, bf16[2576,128]{1,0:T(8,128)(2,1)S(1)} %collective-permute-done.4.message, ...), custom_call_target="tpu_custom_call" | custom-call | flops 20000000000 | bytes 20000000000 | tf_op jit(solution)/shard_map/pallas_call | solution.py:21
  46.3 5.3 %collective-permute-done.5.arrived = bf16[6,128,128]{2,1,0:T(8,128)(2,1)S(1)} collective-permute-done((bf16[6,128,128]{2,1,0:T(8,128)(2,1)S(1)}, bf16[6,128,128]{2,1,0:T(8,128)(2,1)S(1)}, u32[]{:S(2)}, u32[]{:S(2)}) %collective-permute-start.5) | collective-permute-done | bytes 196640 | tf_op jit(solution)/shard_map/ppermute | solution.py:337
  51.6 0.8 %shard_map.71 = f32[2,1,3,3,128,128]{5,4,3,2,1,0:T(8,128)} custom-call(f32[16,128]{1,0:T(8,128)S(1)} %get-tuple-element.23.mine, f32[2,3,128,128]{3,2,1,0:T(8,128)S(1)} %get-tuple-element.32.row, f32[2,2,128,128]{3,2,1,0:T(8,128)S(1)} %get-tuple-element.30.for_e, bf16[2,1280,128]{2,1,0:T(8,128)(2,1)S(1)} %bitcast.4, ...), custom_call_target="tpu_custom_call", output_to_operand_aliasing={{}: (5, {})} | custom-call | tf_op jit(solution)/shard_map/pallas_call | solution.py:21
Async XLA Ops:
  1.7 19.0 %collective-permute-start.3 = (bf16[1808,128]{1,0:T(8,128)(2,1)S(1)}, bf16[1808,128]{1,0:T(8,128)(2,1)S(1)}, u32[]{:S(2)}, u32[]{:S(2)}) collective-permute-start(bf16[1808,128]{1,0:T(8,128)(2,1)S(1)} %get-tuple-element.35), channel_id=1, source_target_pairs={{1,2},{3,4},{5,6},{7,8},{9,10},{11,12},{13,14},{15,16},{17,18},{19... | collective-permute-start | bytes 1388552 | tf_op jit(solution)/shard_map/ppermute | solution.py:317
  2.4 21.6 %collective-permute-start = (bf16[6,128,128]{2,1,0:T(8,128)(2,1)S(1)}, bf16[6,128,128]{2,1,0:T(8,128)(2,1)S(1)}, u32[]{:S(2)}, u32[]{:S(2)}) collective-permute-start(bf16[6,128,128]{2,1,0:T(8,128)(2,1)S(1)} %get-tuple-element.27), channel_id=1, source_target_pairs={{0,64},{64,128},{128,192},{192,256},{256,320},{320,384},{384,448},... | collective-permute-start | bytes 589832 | tf_op jit(solution)/shard_map/ppermute | solution.py:318
  5.9 18.1 %collective-permute-start.1 = (bf16[6,128,128]{2,1,0:T(8,128)(2,1)S(1)}, bf16[6,128,128]{2,1,0:T(8,128)(2,1)S(1)}, u32[]{:S(2)}, u32[]{:S(2)}) collective-permute-start(bf16[6,128,128]{2,1,0:T(8,128)(2,1)S(1)} %get-tuple-element.28), channel_id=1, source_target_pairs={{64,0},{128,64},{192,128},{256,192},{320,256},{384,320},{448,384},... | collective-permute-start | bytes 589832 | tf_op jit(solution)/shard_map/ppermute | solution.py:319
  22.0 4.0 %collective-permute-start.4 = (bf16[2576,128]{1,0:T(8,128)(2,1)S(1)}, bf16[2576,128]{1,0:T(8,128)(2,1)S(1)}, u32[]{:S(2)}, u32[]{:S(2)}) collective-permute-start(bf16[2576,128]{1,0:T(8,128)(2,1)S(1)} %get-tuple-element.38), channel_id=1, source_target_pairs={{0,1},{2,3},{4,5},{6,7},{8,9},{10,11},{12,13},{14,15},{16,17},{18,... | collective-permute-start | bytes 1978376 | tf_op jit(solution)/shard_map/ppermute | solution.py:324
  26.2 19.1 %collective-permute-start.6 = (bf16[12,128,128]{2,1,0:T(8,128)(2,1)S(1)}, bf16[12,128,128]{2,1,0:T(8,128)(2,1)S(1)}, u32[]{:S(2)}, u32[]{:S(2)}) collective-permute-start(bf16[12,128,128]{2,1,0:T(8,128)(2,1)S(1)} %get-tuple-element.40), channel_id=1, source_target_pairs={{0,2},{1,3},{2,0},{3,1},{4,6},{5,7},{6,4},{7,5},{8,10},{9,11},{10,... | collective-permute-start | bytes 1179656 | tf_op jit(solution)/shard_map/ppermute | solution.py:331
  28.1 0.7 %collective-permute-start.2 = (bf16[4,128,128]{2,1,0:T(8,128)(2,1)S(1)}, bf16[4,128,128]{2,1,0:T(8,128)(2,1)S(1)}, u32[]{:S(2)}, u32[]{:S(2)}) collective-permute-start(bf16[4,128,128]{2,1,0:T(8,128)(2,1)S(1)} %get-tuple-element.31), channel_id=1, source_target_pairs={{1,2},{3,4},{5,6},{7,8},{9,10},{11,12},{13,14},{15,16},{17,18},{19... | collective-permute-start | bytes 393224 | tf_op jit(solution)/shard_map/ppermute | solution.py:332
  42.5 9.1 %collective-permute-start.5 = (bf16[6,128,128]{2,1,0:T(8,128)(2,1)S(1)}, bf16[6,128,128]{2,1,0:T(8,128)(2,1)S(1)}, u32[]{:S(2)}, u32[]{:S(2)}) collective-permute-start(bf16[6,128,128]{2,1,0:T(8,128)(2,1)S(1)} %shard_map.69), channel_id=1, source_target_pairs={{0,2},{1,3},{2,0},{3,1},{4,6},{5,7},{6,4},{7,5},{8,10},{9,11},{10,... | collective-permute-start | bytes 589832 | tf_op jit(solution)/shard_map/ppermute | solution.py:337

commit v5 on v4

--- a/solution.py
+++ b/solution.py
@@ -190,44 +190,59 @@
                 message[tile(5 * k + t)] = row[k, t].astype(BF16)
 
 
-def far_kernel(own, a, sides, from_west, from_east, row, for_e, for_o):
+def far_kernel(own, a, sides, from_west, from_east, row, for_e, message):
     even = lax.rem(lax.axis_index("gy"), 2) == 0
     for k, (u, d) in enumerate(FAR):
         arrived = from_west if d == 0 else from_east
         first, middle, last = link_products(a, u, d, [arrived[j] for j in range(4)], [arrived[4], arrived[5]])
         slots = reduce_units(own, u, (first, middle, last), 1)
-        for t in range(3):
-            row[k, t] = slots[t][0]
         down = dot_t(sides[u, 0], cat([first, middle[0]], 1))
         up = dot_t(sides[u, 1], cat([middle[3], last], 1))
         to_e, to_o = jnp.where(even, up, down), jnp.where(even, down, up)
+        for t in range(3):
+            row[k, t] = slots[t][0]
+            message[tile(7 * k + t)] = slots[t][0].astype(BF16)
         for s in range(2):
-            for_e[k, s] = to_e[:, s * B:(s + 1) * B]
-            for_o[2 * k + s] = to_o[:, s * B:(s + 1) * B].astype(BF16)
-
-
-def merge_kernel(row, for_e, from_o, row_out, message):
-    core = lax.rem(lax.axis_index("gy"), 2)
+            at = slice(s * B, (s + 1) * B)
+            for_e[k, s] = to_e[:, at]
+            message[tile(7 * k + 3 + s)] = to_e[:, at].astype(BF16)
+            message[tile(7 * k + 5 + s)] = to_o[:, at].astype(BF16)
+
+
+def between_kernel(message, out):
+    half = lax.rem(lax.axis_index("gy"), 4) // 2
     for k in range(len(FAR)):
-        for t in range(3):
-            row_out[k, t] = row[k, t]
         for s in range(2):
-            row_out[k, core + s] += from_o[2 * k + s].astype(F32)
-            message[tile(5 * k + 3 + s)] = for_e[k, s].astype(BF16)
-        for t in range(3):
-            message[tile(5 * k + t)] = row_out[k, t].astype(BF16)
+            out[2 * k + s] = message[half, tile(7 * k + 5 + s)]
+
+
+def far_tiles(core, half, row, for_e, message, from_group, k, t):
+    def theirs_at(i):
+        return message[1 - core, tile(7 * k + i)].astype(F32)
+
+    def slot(get, shift):
+        if t == 1:
+            return get(1 - shift)
+        return jnp.where(shift == t // 2, get(t // 2), 0.0)
+
+    mine = row[k, t] + slot(lambda s: theirs_at(3 + s), 1 - core)
+    theirs = theirs_at(t) + slot(lambda s: for_e[k, s], core)
+    group = slot(lambda s: from_group[2 * k + s].astype(F32), half)
+    inner = slot(lambda s: message[1 - half, tile(7 * k + 5 + s)].astype(F32), half)
+    border = core == half
+    return mine + jnp.where(border, group, 0.0), theirs + jnp.where(border, 0.0, group), inner
 
 
 def complete(core, row, for_e, message, k, t):
     mine = row[k, t]
-    theirs = message(5 * k + t).astype(F32)
+    theirs = message[tile(5 * k + t)].astype(F32)
     if t == 1:
-        mine = mine + message(5 * k + 3 + core).astype(F32)
+        mine = mine + message[tile(5 * k + 3 + core)].astype(F32)
         theirs = theirs + for_e[k, 1 - core]
     else:
         gets = (core == 0) == (t == 2)
         s = 1 if t == 2 else 0
-        mine = mine + jnp.where(gets, message(5 * k + 3 + s).astype(F32), 0.0)
+        mine = mine + jnp.where(gets, message[tile(5 * k + 3 + s)].astype(F32), 0.0)
         theirs = theirs + jnp.where(gets, 0.0, for_e[k, s])
     return mine, theirs
 
@@ -237,14 +252,6 @@
     other = position + 1 - 2 * core
     return (jnp.broadcast_to(code == position.astype(F32), (B, B)),
             jnp.broadcast_to(code == other.astype(F32), (B, B)))
-
-
-def choose(units, core, position, codes, row, for_e, message, out):
-    for k, (u, _) in enumerate(units):
-        use_mine, use_theirs = masks(codes, u, position, core)
-        for t in range(3):
-            mine, theirs = complete(core, row, for_e, message, k, t)
-            out[3 * k + t] = jnp.where(use_mine, mine, jnp.where(use_theirs, theirs, 0.0)).astype(BF16)
 
 
 def choose_near_kernel(mine, row, for_e, message, halo_e, halo_o, row_far, out, wanted):
@@ -256,40 +263,60 @@
     inferred = inferred - halo_o[pl.ds(14 * B, PAD)].astype(F32)
     codes = jnp.where(outer, message[pl.ds(20 * B, PAD)].astype(F32), inferred)
     wanted[...] = codes
-    choose(NEAR, core, position, codes, row, for_e, lambda i: message[tile(i)], out)
-
-
-def choose_far_kernel(wanted, row, for_e, message, out):
+    for k, (u, _) in enumerate(NEAR):
+        use_mine, use_theirs = masks(codes, u, position, core)
+        for t in range(3):
+            own_row, other_row = complete(core, row, for_e, message, k, t)
+            out[3 * k + t] = jnp.where(use_mine, own_row, jnp.where(use_theirs, other_row, 0.0)).astype(BF16)
+
+
+def choose_far_kernel(wanted, row, for_e, message, from_group, out):
     c = lax.axis_index("gy")
     core, position = lax.rem(c, 2), lax.rem(c, 4)
-    choose(FAR, core, position, wanted[...], row, for_e, lambda i: message[1 - core, tile(i)], out)
-
-
-def finish(units, core, position, codes, row, for_e, message, arrived, out, buffer, sems):
+    for k, (u, _) in enumerate(FAR):
+        use_mine, use_theirs = masks(wanted[...], u, position, core)
+        for t in range(3):
+            mine, theirs, inner = far_tiles(core, position // 2, row, for_e, message, from_group, k, t)
+            out[3 * k + t] = jnp.where(use_mine, mine, jnp.where(use_theirs, theirs, inner)).astype(BF16)
+
+
+def finish_near_kernel(mine, row, for_e, message, arrived, out, buffer, sems):
+    c = lax.axis_index("gy")
+    core, position = lax.rem(c, 2), lax.rem(c, 4)
     copies = []
-    for k, (u, d) in enumerate(units):
-        use_mine, use_theirs = masks(codes, u, position, core)
-        for t in range(3):
-            mine, theirs = complete(core, row, for_e, message, k, t)
-            far = arrived[3 * k + t].astype(F32)
-            buffer[k, t] = jnp.where(use_mine, mine, jnp.where(use_theirs, theirs, far))
+    for k, (u, d) in enumerate(NEAR):
+        use_mine, use_theirs = masks(mine[...], u, position, core)
+        for t in range(3):
+            own_row, other_row = complete(core, row, for_e, message, k, t)
+            got = arrived[3 * k + t].astype(F32)
+            buffer[k, t] = jnp.where(use_mine, own_row, jnp.where(use_theirs, other_row, got))
         copies.append(pltpu.make_async_copy(buffer.at[k], out.at[u, 0, d], sems.at[k]))
         copies[-1].start()
     for copy in copies:
         copy.wait()
 
 
-def finish_near_kernel(mine, row, for_e, message, arrived, out, buffer, sems):
+def finish_far_kernel(mine, row, for_e, message, from_group, arrived, started, out, buffer, sems):
+    del started
     c = lax.axis_index("gy")
     core, position = lax.rem(c, 2), lax.rem(c, 4)
-    finish(NEAR, core, position, mine[...], row, for_e, lambda i: message[tile(i)], arrived, out, buffer, sems)
-
-
-def finish_far_kernel(mine, row, for_e, message, arrived, started, out, buffer, sems):
-    del started
-    c = lax.axis_index("gy")
-    core, position = lax.rem(c, 2), lax.rem(c, 4)
-    finish(FAR, core, position, mine[...], row, for_e, lambda i: message[1 - core, tile(i)], arrived, out, buffer, sems)
+    half = position // 2
+    copies = []
+    for k, (u, d) in enumerate(FAR):
+        use_mine, use_theirs = masks(mine[...], u, position, core)
+        code = mine[u * PAD // 2:u * PAD // 2 + 1]
+        add_arrived = jnp.broadcast_to(code == (1 + half).astype(F32), (B, B))
+        add_inner = jnp.broadcast_to(code == (2 - half).astype(F32), (B, B))
+        for t in range(3):
+            own_row, other_row, inner = far_tiles(core, half, row, for_e, message, from_group, k, t)
+            got = arrived[3 * k + t].astype(F32)
+            here = jnp.where(use_mine, own_row, other_row) + jnp.where(add_arrived, got, 0.0)
+            there = got + jnp.where(add_inner, inner, 0.0)
+            buffer[k, t] = jnp.where(jnp.logical_or(use_mine, use_theirs), here, there)
+        copies.append(pltpu.make_async_copy(buffer.at[k], out.at[u, 0, d], sems.at[k]))
+        copies[-1].start()
+    for copy in copies:
+        copy.wait()
 
 
 def on_device(a_tiles, a_links, p_own, p_side, p_links, coarse_pick):
@@ -299,6 +326,8 @@
     inside = pairs + [(b, a) for a, b in pairs]
     outside = [(i + 1, i + 2) for i in range(0, count - 2, 2)]
     outside = outside + [(b, a) for a, b in outside]
+    between = [(i, i + 2) for i in range(count - 2) if i % 4 > 1]
+    between = between + [(b, a) for a, b in between]
     across = [(i, i ^ 2) for i in range(count)]
     eastward = [(i, i + 1) for i in range(columns - 1)]
     westward = [(b, a) for a, b in eastward]
@@ -322,26 +351,26 @@
         near_kernel, (own, a, sides, halo_e, halo_o),
         [((near, 3) + bb, F32), ((near, 2) + bb, F32), ((5 * near * B + PAD, B), BF16)])
     message_n = lax.ppermute(message_n, "gy", inside)
-    row_f, for_e_f, for_o_f = call(
+    row_f, for_e_f, message_f = call(
         far_kernel, (own, a, sides, from_west, from_east),
-        [((far, 3) + bb, F32), ((far, 2) + bb, F32), ((2 * far,) + bb, BF16)], cost=2 * 10**10)
+        [((far, 3) + bb, F32), ((far, 2) + bb, F32), ((7 * far * B, B), BF16)], cost=2 * 10**10)
     chosen_n, wanted = call(
         choose_near_kernel, (mine, row_n, for_e_n, message_n, halo_e, halo_o, row_f),
         [((3 * near,) + bb, BF16), ((PAD, B), F32)])
     arrived_n = lax.ppermute(chosen_n, "gy", across)
-    from_o_f = lax.ppermute(for_o_f, "gy", outside)
-    row_f, message_f = call(
-        merge_kernel, (row_f, for_e_f, from_o_f), [((far, 3) + bb, F32), ((5 * far * B, B), BF16)])
     message_f = lax.all_gather(message_f, "gy", axis_index_groups=cores)
-    (chosen_f,) = call(choose_far_kernel, (wanted, row_f, for_e_f, message_f), [((3 * far,) + bb, BF16)])
+    (for_group,) = call(between_kernel, (message_f,), [((2 * far,) + bb, BF16)])
+    from_group = lax.ppermute(for_group, "gy", between)
+    (chosen_f,) = call(
+        choose_far_kernel, (wanted, row_f, for_e_f, message_f, from_group), [((3 * far,) + bb, BF16)])
     arrived_f = lax.ppermute(chosen_f, "gy", across)
     shape = (2, 1, 3, 3) + bb
     (out,) = call(
         finish_near_kernel, (mine, row_n, for_e_n, message_n, arrived_n), [(shape, F32)], out_specs=[HBM],
         scratch=[pltpu.VMEM((near, 3) + bb, F32), pltpu.SemaphoreType.DMA((near,))], cost=2 * 10**10)
     (out,) = call(
-        finish_far_kernel, (mine, row_f, for_e_f, message_f, arrived_f, out), [(shape, F32)],
-        in_specs=[VMEM] * 5 + [HBM], out_specs=[HBM], aliases={5: 0},
+        finish_far_kernel, (mine, row_f, for_e_f, message_f, from_group, arrived_f, out), [(shape, F32)],
+        in_specs=[VMEM] * 6 + [HBM], out_specs=[HBM], aliases={6: 0},
         scratch=[pltpu.VMEM((far, 3) + bb, F32), pltpu.SemaphoreType.DMA((far,))])
     return out
 

time: 52.7 us -> 47.8 us (0.907)
  blocking collectives: 15.6 us -> 4.46 us
  starting transfers between devices: 24.4 us -> 32.3 us
  waiting for transfers between devices: 6.53 us -> 4.58 us
    all_gather x1, blocking collectives: 13.6 us -> 2.46 us  [on_device(): message_f = lax.all_gather(message_f, 'gy', axis_index_groups=cores)]
    ppermute x1, starting transfers between devices: 2.75 us -> 10.7 us  [on_device(): arrived_f = lax.ppermute(chosen_f, 'gy', across)]
    ppermute x1, waiting for transfers between devices: 5.32 us -> 3.37 us  [on_device(): arrived_f = lax.ppermute(chosen_f, 'gy', across)]
  transfers between devices with their start and end apart: 7 -> 7, of which waited for: 2 -> 2; matrix products, arithmetic and copies ran while one was open for 0% -> 0% of each run, Pallas kernels for 6% -> 7%
where the time goes in v5:
time: 47.8 us; the launch traced here: 47.5 us
  starting transfers between devices  32.3 us (68%)
  Pallas kernels  5.99 us (13%)
  waiting for transfers between devices  4.58 us (10%)
  blocking collectives  4.46 us (9%)
    ppermute x1, starting transfers between devices, on_device(): from_east = lax.ppermute(west, 'gx', westward)  12.8 us
    ppermute x1, starting transfers between devices, on_device(): arrived_f = lax.ppermute(chosen_f, 'gy', across)  10.7 us
    pallas_call x8, Pallas kernels, call(): pl.pallas_call(kernel, in_specs=in_specs or [VMEM] * len(args), out_specs...  5.99 us
    ppermute x1, starting transfers between devices, on_device(): from_west = lax.ppermute(east, 'gx', eastward)  3.48 us
    ppermute x1, waiting for transfers between devices, on_device(): arrived_f = lax.ppermute(chosen_f, 'gy', across)  3.37 us
    all_gather x1, blocking collectives, on_device(): message_f = lax.all_gather(message_f, 'gy', axis_index_groups=cores)  2.46 us
    ppermute x1, starting transfers between devices, on_device(): message_n = lax.ppermute(message_n, 'gy', inside)  2.05 us
    all_gather x1, blocking collectives, on_device(): halo_e = lax.all_gather(msg_e, 'gy', axis_index_groups=cores)  2 us
  transfers between devices with their start and end apart: 7, of which 2 were waited for; matrix products, arithmetic and copies ran while one was open for 0% of the time, Pallas kernels for 7%

profile of v5, /device:TPU:8, one launch (start us, length us, event | category | flops | bytes accessed | tf_op | source)
XLA Modules:
  0.0 47.5 jit_solution(13315382415258541002)
XLA Ops:
  0.0 1.7 %shard_map.64 = (bf16[2,4,128,128]{3,2,1,0:T(8,128)(2,1)S(1)}, bf16[2,4,5,128,128]{4,3,2,1,0:T(8,128)(2,1)S(1)}, bf16[2,2,128,128]{3,2,1,0:T(8,128)(2,1)S(1)}, b...) custom-call(s32[2,4,4]{2,1,0:T(4,128)} %a_links.1, ...), custom_call_target="tpu_custom_call" | custom-call | tf_op jit(solution)/shard_map/pallas_call | solution.py:21
  1.7 0.7 %collective-permute-start.3 = (bf16[1808,128]{1,0:T(8,128)(2,1)S(1)}, bf16[1808,128]{1,0:T(8,128)(2,1)S(1)}, u32[]{:S(2)}, u32[]{:S(2)}) collective-permute-start(bf16[1808,128]{1,0:T(8,128)(2,1)S(1)} %get-tuple-element.31), channel_id=1, source_target_pairs={{1,2},{3,4},{5,6},{7,8},{9,10},{11,12},{13,14},{15,16},{17,18},{19... | collective-permute-start | bytes 1388552 | tf_op jit(solution)/shard_map/ppermute | solution.py:346
  2.4 3.5 %collective-permute-start = (bf16[6,128,128]{2,1,0:T(8,128)(2,1)S(1)}, bf16[6,128,128]{2,1,0:T(8,128)(2,1)S(1)}, u32[]{:S(2)}, u32[]{:S(2)}) collective-permute-start(bf16[6,128,128]{2,1,0:T(8,128)(2,1)S(1)} %get-tuple-element.25), channel_id=1, source_target_pairs={{0,64},{64,128},{128,192},{192,256},{256,320},{320,384},{384,448},... | collective-permute-start | bytes 589832 | tf_op jit(solution)/shard_map/ppermute | solution.py:347
  5.9 12.8 %collective-permute-start.1 = (bf16[6,128,128]{2,1,0:T(8,128)(2,1)S(1)}, bf16[6,128,128]{2,1,0:T(8,128)(2,1)S(1)}, u32[]{:S(2)}, u32[]{:S(2)}) collective-permute-start(bf16[6,128,128]{2,1,0:T(8,128)(2,1)S(1)} %get-tuple-element.26), channel_id=1, source_target_pairs={{64,0},{128,64},{192,128},{256,192},{320,256},{384,320},{448,384},... | collective-permute-start | bytes 589832 | tf_op jit(solution)/shard_map/ppermute | solution.py:348
  18.7 2.0 %all-gather.1 = bf16[1056,128]{1,0:T(8,128)(2,1)S(1)} all-gather(bf16[528,128]{1,0:T(8,128)(2,1)S(1)} %get-tuple-element.30), channel_id=3, replica_groups={{0,1},{2,3},{4,5},{6,7},{8,9},{10,11},{12,13},{14,15},{16,17},{18,19},{..., dimensions={0}, use_global_device_ids=true | all-gather | bytes 405504 | tf_op jit(solution)/shard_map/all_gather | solution.py:349
  20.7 0.0 collective-permute-done.3.halo_o
  20.7 1.2 %shard_map.67 = (f32[4,3,128,128]{3,2,1,0:T(8,128)S(1)}, f32[4,2,128,128]{3,2,1,0:T(8,128)S(1)}, bf16[2576,128]{1,0:T(8,128)(2,1)S(1)}) custom-call(bf16[2,4,128,128]{3,2,1,0:T(8,128)(2,1)S(1)} %get-tuple-element.22.own, bf16[2,4,5,128,128]{4,3,2,1,0:T(8,128)(2,1)S(1)} %get-tuple-element.23.a, bf16[2,2,128,128]{3,2,1,0:T(8,128)(2,1)S(1)} %get-tuple-element.24.sides, ...), custom_call_target="tpu_custom_call" | custom-call | tf_op jit(solution)/shard_map/pallas_call | solution.py:21
  22.0 2.1 %collective-permute-start.4 = (bf16[2576,128]{1,0:T(8,128)(2,1)S(1)}, bf16[2576,128]{1,0:T(8,128)(2,1)S(1)}, u32[]{:S(2)}, u32[]{:S(2)}) collective-permute-start(bf16[2576,128]{1,0:T(8,128)(2,1)S(1)} %get-tuple-element.34), channel_id=1, source_target_pairs={{0,1},{2,3},{4,5},{6,7},{8,9},{10,11},{12,13},{14,15},{16,17},{18,... | collective-permute-start | bytes 1978376 | tf_op jit(solution)/shard_map/ppermute | solution.py:353
  24.0 0.0 collective-permute-done.from_west
  24.0 0.0 collective-permute-done.1.from_east
  24.0 0.7 %shard_map.65 = (f32[2,3,128,128]{3,2,1,0:T(8,128)S(1)}, f32[2,2,128,128]{3,2,1,0:T(8,128)S(1)}, bf16[1792,128]{1,0:T(8,128)(2,1)S(1)}) custom-call(bf16[2,4,128,128]{3,2,1,0:T(8,128)(2,1)S(1)} %get-tuple-element.22.own, bf16[2,4,5,128,128]{4,3,2,1,0:T(8,128)(2,1)S(1)} %get-tuple-element.23.a, bf16[2,2,128,128]{3,2,1,0:T(8,128)(2,1)S(1)} %get-tuple-element.24.sides, ...), custom_call_target="tpu_custom_call" | custom-call | flops 20000000000 | bytes 20000000000 | tf_op jit(solution)/shard_map/pallas_call | solution.py:21
  24.8 1.2 %collective-permute-done.4.message = bf16[2576,128]{1,0:T(8,128)(2,1)S(1)} collective-permute-done((bf16[2576,128]{1,0:T(8,128)(2,1)S(1)}, bf16[2576,128]{1,0:T(8,128)(2,1)S(1)}, u32[]{:S(2)}, u32[]{:S(2)}) %collective-permute-start.4) | collective-permute-done | bytes 659488 | tf_op jit(solution)/shard_map/ppermute | solution.py:353
  25.9 0.2 shard_map.68
  26.2 1.9 %collective-permute-start.6 = (bf16[12,128,128]{2,1,0:T(8,128)(2,1)S(1)}, bf16[12,128,128]{2,1,0:T(8,128)(2,1)S(1)}, u32[]{:S(2)}, u32[]{:S(2)}) collective-permute-start(bf16[12,128,128]{2,1,0:T(8,128)(2,1)S(1)} %get-tuple-element.36), channel_id=1, source_target_pairs={{0,2},{1,3},{2,0},{3,1},{4,6},{5,7},{6,4},{7,5},{8,10},{9,11},{10,... | collective-permute-start | bytes 1179656 | tf_op jit(solution)/shard_map/ppermute | solution.py:360
  28.1 2.5 %all-gather = bf16[3584,128]{1,0:T(8,128)(2,1)S(1)} all-gather(bf16[1792,128]{1,0:T(8,128)(2,1)S(1)} %get-tuple-element.29), channel_id=2, replica_groups={{0,1},{2,3},{4,5},{6,7},{8,9},{10,11},{12,13},{14,15},{16,17},{18,19},{..., dimensions={0}, use_global_device_ids=true | all-gather | bytes 1376256 | tf_op jit(solution)/shard_map/all_gather | solution.py:361
  30.6 0.7 %collective-permute-start.2 = (bf16[4,128,128]{2,1,0:T(8,128)(2,1)S(1)}, bf16[4,128,128]{2,1,0:T(8,128)(2,1)S(1)}, u32[]{:S(2)}, u32[]{:S(2)}) collective-permute-start(bf16[4,128,128]{2,1,0:T(8,128)(2,1)S(1)} %shard_map.66), channel_id=1, source_target_pairs={{2,4},{3,5},{6,8},{7,9},{10,12},{11,13},{14,16},{15,17},{18,20},{1... | collective-permute-start | bytes 393224 | tf_op jit(solution)/shard_map/ppermute | solution.py:363
  31.2 0.0 collective-permute-done.2.from_group
  31.3 0.2 shard_map.69
  31.5 10.7 %collective-permute-start.5 = (bf16[6,128,128]{2,1,0:T(8,128)(2,1)S(1)}, bf16[6,128,128]{2,1,0:T(8,128)(2,1)S(1)}, u32[]{:S(2)}, u32[]{:S(2)}) collective-permute-start(bf16[6,128,128]{2,1,0:T(8,128)(2,1)S(1)} %shard_map.69), channel_id=1, source_target_pairs={{0,2},{1,3},{2,0},{3,1},{4,6},{5,7},{6,4},{7,5},{8,10},{9,11},{10,... | collective-permute-start | bytes 589832 | tf_op jit(solution)/shard_map/ppermute | solution.py:366
  42.1 0.0 collective-permute-done.6.arrived
  42.1 1.0 %shard_map.70.started = f32[2,1,3,3,128,128]{5,4,3,2,1,0:T(8,128)} custom-call(f32[16,128]{1,0:T(8,128)S(1)} %get-tuple-element.21.mine, f32[4,3,128,128]{3,2,1,0:T(8,128)S(1)} %get-tuple-element.32.row, f32[4,2,128,128]{3,2,1,0:T(8,128)S(1)} %get-tuple-element.33.for_e, bf16[2576,128]{1,0:T(8,128)(2,1)S(1)} %collective-permute-done.4.message, ...), custom_call_target="tpu_custom_call" | custom-call | flops 20000000000 | bytes 20000000000 | tf_op jit(solution)/shard_map/pallas_call | solution.py:21
  43.1 3.4 %collective-permute-done.5.arrived = bf16[6,128,128]{2,1,0:T(8,128)(2,1)S(1)} collective-permute-done((bf16[6,128,128]{2,1,0:T(8,128)(2,1)S(1)}, bf16[6,128,128]{2,1,0:T(8,128)(2,1)S(1)}, u32[]{:S(2)}, u32[]{:S(2)}) %collective-permute-start.5) | collective-permute-done | bytes 196640 | tf_op jit(solution)/shard_map/ppermute | solution.py:366
  46.5 1.0 %shard_map.71 = f32[2,1,3,3,128,128]{5,4,3,2,1,0:T(8,128)} custom-call(f32[16,128]{1,0:T(8,128)S(1)} %get-tuple-element.21.mine, f32[2,3,128,128]{3,2,1,0:T(8,128)S(1)} %get-tuple-element.27.row_far.row, f32[2,2,128,128]{3,2,1,0:T(8,128)S(1)} %get-tuple-element.28.for_e, bf16[2,1792,128]{2,1,0:T(8,128)(2,1)S(1)} %bitcast.5, ...), custom_call_target="tpu_custom_call", output_to_operand_aliasing={{}: (6, {})} | custom-call | tf_op jit(solution)/shard_map/pallas_call | solution.py:21
  (1 shorter events, 0.0 us)
Async XLA Ops:
  1.7 19.0 %collective-permute-start.3 = (bf16[1808,128]{1,0:T(8,128)(2,1)S(1)}, bf16[1808,128]{1,0:T(8,128)(2,1)S(1)}, u32[]{:S(2)}, u32[]{:S(2)}) collective-permute-start(bf16[1808,128]{1,0:T(8,128)(2,1)S(1)} %get-tuple-element.31), channel_id=1, source_target_pairs={{1,2},{3,4},{5,6},{7,8},{9,10},{11,12},{13,14},{15,16},{17,18},{19... | collective-permute-start | bytes 1388552 | tf_op jit(solution)/shard_map/ppermute | solution.py:346
  2.4 21.6 %collective-permute-start = (bf16[6,128,128]{2,1,0:T(8,128)(2,1)S(1)}, bf16[6,128,128]{2,1,0:T(8,128)(2,1)S(1)}, u32[]{:S(2)}, u32[]{:S(2)}) collective-permute-start(bf16[6,128,128]{2,1,0:T(8,128)(2,1)S(1)} %get-tuple-element.25), channel_id=1, source_target_pairs={{0,64},{64,128},{128,192},{192,256},{256,320},{320,384},{384,448},... | collective-permute-start | bytes 589832 | tf_op jit(solution)/shard_map/ppermute | solution.py:347
  5.9 18.1 %collective-permute-start.1 = (bf16[6,128,128]{2,1,0:T(8,128)(2,1)S(1)}, bf16[6,128,128]{2,1,0:T(8,128)(2,1)S(1)}, u32[]{:S(2)}, u32[]{:S(2)}) collective-permute-start(bf16[6,128,128]{2,1,0:T(8,128)(2,1)S(1)} %get-tuple-element.26), channel_id=1, source_target_pairs={{64,0},{128,64},{192,128},{256,192},{320,256},{384,320},{448,384},... | collective-permute-start | bytes 589832 | tf_op jit(solution)/shard_map/ppermute | solution.py:348
  22.0 4.0 %collective-permute-start.4 = (bf16[2576,128]{1,0:T(8,128)(2,1)S(1)}, bf16[2576,128]{1,0:T(8,128)(2,1)S(1)}, u32[]{:S(2)}, u32[]{:S(2)}) collective-permute-start(bf16[2576,128]{1,0:T(8,128)(2,1)S(1)} %get-tuple-element.34), channel_id=1, source_target_pairs={{0,1},{2,3},{4,5},{6,7},{8,9},{10,11},{12,13},{14,15},{16,17},{18,... | collective-permute-start | bytes 1978376 | tf_op jit(solution)/shard_map/ppermute | solution.py:353
  26.2 16.0 %collective-permute-start.6 = (bf16[12,128,128]{2,1,0:T(8,128)(2,1)S(1)}, bf16[12,128,128]{2,1,0:T(8,128)(2,1)S(1)}, u32[]{:S(2)}, u32[]{:S(2)}) collective-permute-start(bf16[12,128,128]{2,1,0:T(8,128)(2,1)S(1)} %get-tuple-element.36), channel_id=1, source_target_pairs={{0,2},{1,3},{2,0},{3,1},{4,6},{5,7},{6,4},{7,5},{8,10},{9,11},{10,... | collective-permute-start | bytes 1179656 | tf_op jit(solution)/shard_map/ppermute | solution.py:360
  30.6 0.7 %collective-permute-start.2 = (bf16[4,128,128]{2,1,0:T(8,128)(2,1)S(1)}, bf16[4,128,128]{2,1,0:T(8,128)(2,1)S(1)}, u32[]{:S(2)}, u32[]{:S(2)}) collective-permute-start(bf16[4,128,128]{2,1,0:T(8,128)(2,1)S(1)} %shard_map.66), channel_id=1, source_target_pairs={{2,4},{3,5},{6,8},{7,9},{10,12},{11,13},{14,16},{15,17},{18,20},{1... | collective-permute-start | bytes 393224 | tf_op jit(solution)/shard_map/ppermute | solution.py:363
  31.5 15.0 %collective-permute-start.5 = (bf16[6,128,128]{2,1,0:T(8,128)(2,1)S(1)}, bf16[6,128,128]{2,1,0:T(8,128)(2,1)S(1)}, u32[]{:S(2)}, u32[]{:S(2)}) collective-permute-start(bf16[6,128,128]{2,1,0:T(8,128)(2,1)S(1)} %shard_map.69), channel_id=1, source_target_pairs={{0,2},{1,3},{2,0},{3,1},{4,6},{5,7},{6,4},{7,5},{8,10},{9,11},{10,... | collective-permute-start | bytes 589832 | tf_op jit(solution)/shard_map/ppermute | solution.py:366

commit v6 on v5

--- a/solution.py
+++ b/solution.py
@@ -190,7 +190,7 @@
                 message[tile(5 * k + t)] = row[k, t].astype(BF16)
 
 
-def far_kernel(own, a, sides, from_west, from_east, row, for_e, message):
+def far_kernel(own, a, sides, from_west, from_east, row, for_e, for_o):
     even = lax.rem(lax.axis_index("gy"), 2) == 0
     for k, (u, d) in enumerate(FAR):
         arrived = from_west if d == 0 else from_east
@@ -201,22 +201,26 @@
         to_e, to_o = jnp.where(even, up, down), jnp.where(even, down, up)
         for t in range(3):
             row[k, t] = slots[t][0]
-            message[tile(7 * k + t)] = slots[t][0].astype(BF16)
         for s in range(2):
             at = slice(s * B, (s + 1) * B)
             for_e[k, s] = to_e[:, at]
-            message[tile(7 * k + 3 + s)] = to_e[:, at].astype(BF16)
-            message[tile(7 * k + 5 + s)] = to_o[:, at].astype(BF16)
-
-
-def between_kernel(message, out):
-    half = lax.rem(lax.axis_index("gy"), 4) // 2
+            for_o[2 * k + s] = to_o[:, at].astype(BF16)
+
+
+def merge_kernel(row, for_e, for_o, from_group, row_out, message):
+    core = lax.rem(lax.axis_index("gy"), 2)
     for k in range(len(FAR)):
+        for t in range(3):
+            row_out[k, t] = row[k, t]
         for s in range(2):
-            out[2 * k + s] = message[half, tile(7 * k + 5 + s)]
-
-
-def far_tiles(core, half, row, for_e, message, from_group, k, t):
+            row_out[k, core + s] += from_group[2 * k + s].astype(F32)
+            message[tile(7 * k + 3 + s)] = for_e[k, s].astype(BF16)
+            message[tile(7 * k + 5 + s)] = for_o[2 * k + s]
+        for t in range(3):
+            message[tile(7 * k + t)] = row_out[k, t].astype(BF16)
+
+
+def far_tiles(core, half, row, for_e, message, k, t):
     def theirs_at(i):
         return message[1 - core, tile(7 * k + i)].astype(F32)
 
@@ -227,10 +231,8 @@
 
     mine = row[k, t] + slot(lambda s: theirs_at(3 + s), 1 - core)
     theirs = theirs_at(t) + slot(lambda s: for_e[k, s], core)
-    group = slot(lambda s: from_group[2 * k + s].astype(F32), half)
     inner = slot(lambda s: message[1 - half, tile(7 * k + 5 + s)].astype(F32), half)
-    border = core == half
-    return mine + jnp.where(border, group, 0.0), theirs + jnp.where(border, 0.0, group), inner
+    return mine, theirs, inner
 
 
 def complete(core, row, for_e, message, k, t):
@@ -270,13 +272,13 @@
             out[3 * k + t] = jnp.where(use_mine, own_row, jnp.where(use_theirs, other_row, 0.0)).astype(BF16)
 
 
-def choose_far_kernel(wanted, row, for_e, message, from_group, out):
+def choose_far_kernel(wanted, row, for_e, message, out):
     c = lax.axis_index("gy")
     core, position = lax.rem(c, 2), lax.rem(c, 4)
     for k, (u, _) in enumerate(FAR):
         use_mine, use_theirs = masks(wanted[...], u, position, core)
         for t in range(3):
-            mine, theirs, inner = far_tiles(core, position // 2, row, for_e, message, from_group, k, t)
+            mine, theirs, inner = far_tiles(core, position // 2, row, for_e, message, k, t)
             out[3 * k + t] = jnp.where(use_mine, mine, jnp.where(use_theirs, theirs, inner)).astype(BF16)
 
 
@@ -296,7 +298,7 @@
         copy.wait()
 
 
-def finish_far_kernel(mine, row, for_e, message, from_group, arrived, started, out, buffer, sems):
+def finish_far_kernel(mine, row, for_e, message, arrived, started, out, buffer, sems):
     del started
     c = lax.axis_index("gy")
     core, position = lax.rem(c, 2), lax.rem(c, 4)
@@ -308,7 +310,7 @@
         add_arrived = jnp.broadcast_to(code == (1 + half).astype(F32), (B, B))
         add_inner = jnp.broadcast_to(code == (2 - half).astype(F32), (B, B))
         for t in range(3):
-            own_row, other_row, inner = far_tiles(core, half, row, for_e, message, from_group, k, t)
+            own_row, other_row, inner = far_tiles(core, half, row, for_e, message, k, t)
             got = arrived[3 * k + t].astype(F32)
             here = jnp.where(use_mine, own_row, other_row) + jnp.where(add_arrived, got, 0.0)
             there = got + jnp.where(add_inner, inner, 0.0)
@@ -326,7 +328,7 @@
     inside = pairs + [(b, a) for a, b in pairs]
     outside = [(i + 1, i + 2) for i in range(0, count - 2, 2)]
     outside = outside + [(b, a) for a, b in outside]
-    between = [(i, i + 2) for i in range(count - 2) if i % 4 > 1]
+    between = [(i, i + 1) for i in range(3, count - 1, 4)]
     between = between + [(b, a) for a, b in between]
     across = [(i, i ^ 2) for i in range(count)]
     eastward = [(i, i + 1) for i in range(columns - 1)]
@@ -351,26 +353,26 @@
         near_kernel, (own, a, sides, halo_e, halo_o),
         [((near, 3) + bb, F32), ((near, 2) + bb, F32), ((5 * near * B + PAD, B), BF16)])
     message_n = lax.ppermute(message_n, "gy", inside)
-    row_f, for_e_f, message_f = call(
+    row_f, for_e_f, for_o_f = call(
         far_kernel, (own, a, sides, from_west, from_east),
-        [((far, 3) + bb, F32), ((far, 2) + bb, F32), ((7 * far * B, B), BF16)], cost=2 * 10**10)
+        [((far, 3) + bb, F32), ((far, 2) + bb, F32), ((2 * far,) + bb, BF16)], cost=2 * 10**10)
     chosen_n, wanted = call(
         choose_near_kernel, (mine, row_n, for_e_n, message_n, halo_e, halo_o, row_f),
         [((3 * near,) + bb, BF16), ((PAD, B), F32)])
     arrived_n = lax.ppermute(chosen_n, "gy", across)
+    from_group = lax.ppermute(for_o_f, "gy", between)
+    row_f, message_f = call(
+        merge_kernel, (row_f, for_e_f, for_o_f, from_group), [((far, 3) + bb, F32), ((7 * far * B, B), BF16)])
     message_f = lax.all_gather(message_f, "gy", axis_index_groups=cores)
-    (for_group,) = call(between_kernel, (message_f,), [((2 * far,) + bb, BF16)])
-    from_group = lax.ppermute(for_group, "gy", between)
-    (chosen_f,) = call(
-        choose_far_kernel, (wanted, row_f, for_e_f, message_f, from_group), [((3 * far,) + bb, BF16)])
+    (chosen_f,) = call(choose_far_kernel, (wanted, row_f, for_e_f, message_f), [((3 * far,) + bb, BF16)])
     arrived_f = lax.ppermute(chosen_f, "gy", across)
     shape = (2, 1, 3, 3) + bb
     (out,) = call(
         finish_near_kernel, (mine, row_n, for_e_n, message_n, arrived_n), [(shape, F32)], out_specs=[HBM],
         scratch=[pltpu.VMEM((near, 3) + bb, F32), pltpu.SemaphoreType.DMA((near,))], cost=2 * 10**10)
     (out,) = call(
-        finish_far_kernel, (mine, row_f, for_e_f, message_f, from_group, arrived_f, out), [(shape, F32)],
-        in_specs=[VMEM] * 6 + [HBM], out_specs=[HBM], aliases={6: 0},
+        finish_far_kernel, (mine, row_f, for_e_f, message_f, arrived_f, out), [(shape, F32)],
+        in_specs=[VMEM] * 5 + [HBM], out_specs=[HBM], aliases={5: 0},
         scratch=[pltpu.VMEM((far, 3) + bb, F32), pltpu.SemaphoreType.DMA((far,))])
     return out
 

time: 47.8 us -> 47.4 us (level)
  starting transfers between devices: 32.3 us -> 31 us
  waiting for transfers between devices: 4.58 us -> 5.63 us
    ppermute x1, starting transfers between devices: 10.7 us -> 9.31 us  [on_device(): arrived_f = lax.ppermute(chosen_f, 'gy', across)]
    ppermute x1, waiting for transfers between devices: 3.37 us -> 4.42 us  [on_device(): arrived_f = lax.ppermute(chosen_f, 'gy', across)]
where the time goes in v6:
time: 47.4 us; the launch traced here: 47.1 us
  starting transfers between devices  31 us (65%)
  Pallas kernels  5.93 us (13%)
  waiting for transfers between devices  5.63 us (12%)
  blocking collectives  4.46 us (9%)
    ppermute x1, starting transfers between devices, on_device(): from_east = lax.ppermute(west, 'gx', westward)  12.8 us
    ppermute x1, starting transfers between devices, on_device(): arrived_f = lax.ppermute(chosen_f, 'gy', across)  9.31 us
    pallas_call x8, Pallas kernels, call(): pl.pallas_call(kernel, in_specs=in_specs or [VMEM] * len(args), out_specs...  5.93 us
    ppermute x1, waiting for transfers between devices, on_device(): arrived_f = lax.ppermute(chosen_f, 'gy', across)  4.42 us
    ppermute x1, starting transfers between devices, on_device(): from_west = lax.ppermute(east, 'gx', eastward)  3.48 us
    all_gather x1, blocking collectives, on_device(): message_f = lax.all_gather(message_f, 'gy', axis_index_groups=cores)  2.46 us
    ppermute x1, starting transfers between devices, on_device(): message_n = lax.ppermute(message_n, 'gy', inside)  2.05 us
    all_gather x1, blocking collectives, on_device(): halo_e = lax.all_gather(msg_e, 'gy', axis_index_groups=cores)  2 us
  transfers between devices with their start and end apart: 7, of which 2 were waited for; matrix products, arithmetic and copies ran while one was open for 0% of the time, Pallas kernels for 7%

profile of v6, /device:TPU:8, one launch (start us, length us, event | category | flops | bytes accessed | tf_op | source)
XLA Modules:
  0.0 47.1 jit_solution(16004926178540688995)
XLA Ops:
  0.0 1.7 %shard_map.64 = (bf16[2,4,128,128]{3,2,1,0:T(8,128)(2,1)S(1)}, bf16[2,4,5,128,128]{4,3,2,1,0:T(8,128)(2,1)S(1)}, bf16[2,2,128,128]{3,2,1,0:T(8,128)(2,1)S(1)}, b...) custom-call(s32[2,4,4]{2,1,0:T(4,128)} %a_links.1, ...), custom_call_target="tpu_custom_call" | custom-call | tf_op jit(solution)/shard_map/pallas_call | solution.py:21
  1.7 0.7 %collective-permute-start.3 = (bf16[1808,128]{1,0:T(8,128)(2,1)S(1)}, bf16[1808,128]{1,0:T(8,128)(2,1)S(1)}, u32[]{:S(2)}, u32[]{:S(2)}) collective-permute-start(bf16[1808,128]{1,0:T(8,128)(2,1)S(1)} %get-tuple-element.35), channel_id=1, source_target_pairs={{1,2},{3,4},{5,6},{7,8},{9,10},{11,12},{13,14},{15,16},{17,18},{19... | collective-permute-start | bytes 1388552 | tf_op jit(solution)/shard_map/ppermute | solution.py:348
  2.4 3.5 %collective-permute-start = (bf16[6,128,128]{2,1,0:T(8,128)(2,1)S(1)}, bf16[6,128,128]{2,1,0:T(8,128)(2,1)S(1)}, u32[]{:S(2)}, u32[]{:S(2)}) collective-permute-start(bf16[6,128,128]{2,1,0:T(8,128)(2,1)S(1)} %get-tuple-element.27), channel_id=1, source_target_pairs={{0,64},{64,128},{128,192},{192,256},{256,320},{320,384},{384,448},... | collective-permute-start | bytes 589832 | tf_op jit(solution)/shard_map/ppermute | solution.py:349
  5.9 12.8 %collective-permute-start.1 = (bf16[6,128,128]{2,1,0:T(8,128)(2,1)S(1)}, bf16[6,128,128]{2,1,0:T(8,128)(2,1)S(1)}, u32[]{:S(2)}, u32[]{:S(2)}) collective-permute-start(bf16[6,128,128]{2,1,0:T(8,128)(2,1)S(1)} %get-tuple-element.28), channel_id=1, source_target_pairs={{64,0},{128,64},{192,128},{256,192},{320,256},{384,320},{448,384},... | collective-permute-start | bytes 589832 | tf_op jit(solution)/shard_map/ppermute | solution.py:350
  18.7 2.0 %all-gather.1 = bf16[1056,128]{1,0:T(8,128)(2,1)S(1)} all-gather(bf16[528,128]{1,0:T(8,128)(2,1)S(1)} %get-tuple-element.34), channel_id=3, replica_groups={{0,1},{2,3},{4,5},{6,7},{8,9},{10,11},{12,13},{14,15},{16,17},{18,19},{..., dimensions={0}, use_global_device_ids=true | all-gather | bytes 405504 | tf_op jit(solution)/shard_map/all_gather | solution.py:351
  20.7 0.0 collective-permute-done.3.halo_o
  20.7 1.2 %shard_map.67 = (f32[4,3,128,128]{3,2,1,0:T(8,128)S(1)}, f32[4,2,128,128]{3,2,1,0:T(8,128)S(1)}, bf16[2576,128]{1,0:T(8,128)(2,1)S(1)}) custom-call(bf16[2,4,128,128]{3,2,1,0:T(8,128)(2,1)S(1)} %get-tuple-element.24.own, bf16[2,4,5,128,128]{4,3,2,1,0:T(8,128)(2,1)S(1)} %get-tuple-element.25.a, bf16[2,2,128,128]{3,2,1,0:T(8,128)(2,1)S(1)} %get-tuple-element.26.sides, ...), custom_call_target="tpu_custom_call" | custom-call | tf_op jit(solution)/shard_map/pallas_call | solution.py:21
  22.0 2.1 %collective-permute-start.4 = (bf16[2576,128]{1,0:T(8,128)(2,1)S(1)}, bf16[2576,128]{1,0:T(8,128)(2,1)S(1)}, u32[]{:S(2)}, u32[]{:S(2)}) collective-permute-start(bf16[2576,128]{1,0:T(8,128)(2,1)S(1)} %get-tuple-element.38), channel_id=1, source_target_pairs={{0,1},{2,3},{4,5},{6,7},{8,9},{10,11},{12,13},{14,15},{16,17},{18,... | collective-permute-start | bytes 1978376 | tf_op jit(solution)/shard_map/ppermute | solution.py:355
  24.0 0.0 collective-permute-done.from_west
  24.0 0.0 collective-permute-done.1.from_east
  24.0 0.7 %shard_map.65 = (f32[2,3,128,128]{3,2,1,0:T(8,128)S(1)}, f32[2,2,128,128]{3,2,1,0:T(8,128)S(1)}, bf16[4,128,128]{2,1,0:T(8,128)(2,1)S(1)}) custom-call(bf16[2,4,128,128]{3,2,1,0:T(8,128)(2,1)S(1)} %get-tuple-element.24.own, bf16[2,4,5,128,128]{4,3,2,1,0:T(8,128)(2,1)S(1)} %get-tuple-element.25.a, bf16[2,2,128,128]{3,2,1,0:T(8,128)(2,1)S(1)} %get-tuple-element.26.sides, ...), custom_call_target="tpu_custom_call" | custom-call | flops 20000000000 | bytes 20000000000 | tf_op jit(solution)/shard_map/pallas_call | solution.py:21
  24.8 1.2 %collective-permute-done.4.message = bf16[2576,128]{1,0:T(8,128)(2,1)S(1)} collective-permute-done((bf16[2576,128]{1,0:T(8,128)(2,1)S(1)}, bf16[2576,128]{1,0:T(8,128)(2,1)S(1)}, u32[]{:S(2)}, u32[]{:S(2)}) %collective-permute-start.4) | collective-permute-done | bytes 659488 | tf_op jit(solution)/shard_map/ppermute | solution.py:355
  25.9 0.2 shard_map.68
  26.2 1.9 %collective-permute-start.6 = (bf16[12,128,128]{2,1,0:T(8,128)(2,1)S(1)}, bf16[12,128,128]{2,1,0:T(8,128)(2,1)S(1)}, u32[]{:S(2)}, u32[]{:S(2)}) collective-permute-start(bf16[12,128,128]{2,1,0:T(8,128)(2,1)S(1)} %get-tuple-element.40), channel_id=1, source_target_pairs={{0,2},{1,3},{2,0},{3,1},{4,6},{5,7},{6,4},{7,5},{8,10},{9,11},{10,... | collective-permute-start | bytes 1179656 | tf_op jit(solution)/shard_map/ppermute | solution.py:362
  28.1 0.7 %collective-permute-start.2 = (bf16[4,128,128]{2,1,0:T(8,128)(2,1)S(1)}, bf16[4,128,128]{2,1,0:T(8,128)(2,1)S(1)}, u32[]{:S(2)}, u32[]{:S(2)}) collective-permute-start(bf16[4,128,128]{2,1,0:T(8,128)(2,1)S(1)} %get-tuple-element.31.for_o), channel_id=1, source_target_pairs={{3,4},{7,8},{11,12},{15,16},{19,20},{23,24},{27,28},{31,32},{35,36... | collective-permute-start | bytes 393224 | tf_op jit(solution)/shard_map/ppermute | solution.py:363
  28.8 0.0 collective-permute-done.2.from_group
  28.8 0.1 shard_map.66
  28.9 2.5 %all-gather = bf16[3584,128]{1,0:T(8,128)(2,1)S(1)} all-gather(bf16[1792,128]{1,0:T(8,128)(2,1)S(1)} %get-tuple-element.33), channel_id=2, replica_groups={{0,1},{2,3},{4,5},{6,7},{8,9},{10,11},{12,13},{14,15},{16,17},{18,19},{..., dimensions={0}, use_global_device_ids=true | all-gather | bytes 1376256 | tf_op jit(solution)/shard_map/all_gather | solution.py:366
  31.3 0.1 shard_map.69
  31.5 9.3 %collective-permute-start.5 = (bf16[6,128,128]{2,1,0:T(8,128)(2,1)S(1)}, bf16[6,128,128]{2,1,0:T(8,128)(2,1)S(1)}, u32[]{:S(2)}, u32[]{:S(2)}) collective-permute-start(bf16[6,128,128]{2,1,0:T(8,128)(2,1)S(1)} %shard_map.69), channel_id=1, source_target_pairs={{0,2},{1,3},{2,0},{3,1},{4,6},{5,7},{6,4},{7,5},{8,10},{9,11},{10,... | collective-permute-start | bytes 589832 | tf_op jit(solution)/shard_map/ppermute | solution.py:368
  40.8 0.0 collective-permute-done.6.arrived
  40.8 1.0 %shard_map.70.started = f32[2,1,3,3,128,128]{5,4,3,2,1,0:T(8,128)} custom-call(f32[16,128]{1,0:T(8,128)S(1)} %get-tuple-element.23.mine, f32[4,3,128,128]{3,2,1,0:T(8,128)S(1)} %get-tuple-element.36.row, f32[4,2,128,128]{3,2,1,0:T(8,128)S(1)} %get-tuple-element.37.for_e, bf16[2576,128]{1,0:T(8,128)(2,1)S(1)} %collective-permute-done.4.message, ...), custom_call_target="tpu_custom_call" | custom-call | flops 20000000000 | bytes 20000000000 | tf_op jit(solution)/shard_map/pallas_call | solution.py:21
  41.8 4.4 %collective-permute-done.5.arrived = bf16[6,128,128]{2,1,0:T(8,128)(2,1)S(1)} collective-permute-done((bf16[6,128,128]{2,1,0:T(8,128)(2,1)S(1)}, bf16[6,128,128]{2,1,0:T(8,128)(2,1)S(1)}, u32[]{:S(2)}, u32[]{:S(2)}) %collective-permute-start.5) | collective-permute-done | bytes 196640 | tf_op jit(solution)/shard_map/ppermute | solution.py:368
  46.2 0.9 %shard_map.71 = f32[2,1,3,3,128,128]{5,4,3,2,1,0:T(8,128)} custom-call(f32[16,128]{1,0:T(8,128)S(1)} %get-tuple-element.23.mine, f32[2,3,128,128]{3,2,1,0:T(8,128)S(1)} %get-tuple-element.32.row, f32[2,2,128,128]{3,2,1,0:T(8,128)S(1)} %get-tuple-element.30.for_e, bf16[2,1792,128]{2,1,0:T(8,128)(2,1)S(1)} %bitcast.4, ...), custom_call_target="tpu_custom_call", output_to_operand_aliasing={{}: (5, {})} | custom-call | tf_op jit(solution)/shard_map/pallas_call | solution.py:21
Async XLA Ops:
  1.7 19.0 %collective-permute-start.3 = (bf16[1808,128]{1,0:T(8,128)(2,1)S(1)}, bf16[1808,128]{1,0:T(8,128)(2,1)S(1)}, u32[]{:S(2)}, u32[]{:S(2)}) collective-permute-start(bf16[1808,128]{1,0:T(8,128)(2,1)S(1)} %get-tuple-element.35), channel_id=1, source_target_pairs={{1,2},{3,4},{5,6},{7,8},{9,10},{11,12},{13,14},{15,16},{17,18},{19... | collective-permute-start | bytes 1388552 | tf_op jit(solution)/shard_map/ppermute | solution.py:348
  2.4 21.6 %collective-permute-start = (bf16[6,128,128]{2,1,0:T(8,128)(2,1)S(1)}, bf16[6,128,128]{2,1,0:T(8,128)(2,1)S(1)}, u32[]{:S(2)}, u32[]{:S(2)}) collective-permute-start(bf16[6,128,128]{2,1,0:T(8,128)(2,1)S(1)} %get-tuple-element.27), channel_id=1, source_target_pairs={{0,64},{64,128},{128,192},{192,256},{256,320},{320,384},{384,448},... | collective-permute-start | bytes 589832 | tf_op jit(solution)/shard_map/ppermute | solution.py:349
  5.9 18.1 %collective-permute-start.1 = (bf16[6,128,128]{2,1,0:T(8,128)(2,1)S(1)}, bf16[6,128,128]{2,1,0:T(8,128)(2,1)S(1)}, u32[]{:S(2)}, u32[]{:S(2)}) collective-permute-start(bf16[6,128,128]{2,1,0:T(8,128)(2,1)S(1)} %get-tuple-element.28), channel_id=1, source_target_pairs={{64,0},{128,64},{192,128},{256,192},{320,256},{384,320},{448,384},... | collective-permute-start | bytes 589832 | tf_op jit(solution)/shard_map/ppermute | solution.py:350
  22.0 4.0 %collective-permute-start.4 = (bf16[2576,128]{1,0:T(8,128)(2,1)S(1)}, bf16[2576,128]{1,0:T(8,128)(2,1)S(1)}, u32[]{:S(2)}, u32[]{:S(2)}) collective-permute-start(bf16[2576,128]{1,0:T(8,128)(2,1)S(1)} %get-tuple-element.38), channel_id=1, source_target_pairs={{0,1},{2,3},{4,5},{6,7},{8,9},{10,11},{12,13},{14,15},{16,17},{18,... | collective-permute-start | bytes 1978376 | tf_op jit(solution)/shard_map/ppermute | solution.py:355
  26.2 14.6 %collective-permute-start.6 = (bf16[12,128,128]{2,1,0:T(8,128)(2,1)S(1)}, bf16[12,128,128]{2,1,0:T(8,128)(2,1)S(1)}, u32[]{:S(2)}, u32[]{:S(2)}) collective-permute-start(bf16[12,128,128]{2,1,0:T(8,128)(2,1)S(1)} %get-tuple-element.40), channel_id=1, source_target_pairs={{0,2},{1,3},{2,0},{3,1},{4,6},{5,7},{6,4},{7,5},{8,10},{9,11},{10,... | collective-permute-start | bytes 1179656 | tf_op jit(solution)/shard_map/ppermute | solution.py:362
  28.1 0.7 %collective-permute-start.2 = (bf16[4,128,128]{2,1,0:T(8,128)(2,1)S(1)}, bf16[4,128,128]{2,1,0:T(8,128)(2,1)S(1)}, u32[]{:S(2)}, u32[]{:S(2)}) collective-permute-start(bf16[4,128,128]{2,1,0:T(8,128)(2,1)S(1)} %get-tuple-element.31.for_o), channel_id=1, source_target_pairs={{3,4},{7,8},{11,12},{15,16},{19,20},{23,24},{27,28},{31,32},{35,36... | collective-permute-start | bytes 393224 | tf_op jit(solution)/shard_map/ppermute | solution.py:363
  31.5 14.7 %collective-permute-start.5 = (bf16[6,128,128]{2,1,0:T(8,128)(2,1)S(1)}, bf16[6,128,128]{2,1,0:T(8,128)(2,1)S(1)}, u32[]{:S(2)}, u32[]{:S(2)}) collective-permute-start(bf16[6,128,128]{2,1,0:T(8,128)(2,1)S(1)} %shard_map.69), channel_id=1, source_target_pairs={{0,2},{1,3},{2,0},{3,1},{4,6},{5,7},{6,4},{7,5},{8,10},{9,11},{10,... | collective-permute-start | bytes 589832 | tf_op jit(solution)/shard_map/ppermute | solution.py:368

commit v7 on v6

--- a/solution.py
+++ b/solution.py
@@ -207,7 +207,7 @@
             for_o[2 * k + s] = to_o[:, at].astype(BF16)
 
 
-def merge_kernel(row, for_e, for_o, from_group, row_out, message):
+def merge_kernel(row, for_e, for_o, from_group, chosen, row_out, message):
     core = lax.rem(lax.axis_index("gy"), 2)
     for k in range(len(FAR)):
         for t in range(3):
@@ -355,21 +355,21 @@
     message_n = lax.ppermute(message_n, "gy", inside)
     row_f, for_e_f, for_o_f = call(
         far_kernel, (own, a, sides, from_west, from_east),
-        [((far, 3) + bb, F32), ((far, 2) + bb, F32), ((2 * far,) + bb, BF16)], cost=2 * 10**10)
+        [((far, 3) + bb, F32), ((far, 2) + bb, F32), ((2 * far,) + bb, BF16)], cost=20000000000)
     chosen_n, wanted = call(
         choose_near_kernel, (mine, row_n, for_e_n, message_n, halo_e, halo_o, row_f),
         [((3 * near,) + bb, BF16), ((PAD, B), F32)])
     arrived_n = lax.ppermute(chosen_n, "gy", across)
     from_group = lax.ppermute(for_o_f, "gy", between)
     row_f, message_f = call(
-        merge_kernel, (row_f, for_e_f, for_o_f, from_group), [((far, 3) + bb, F32), ((7 * far * B, B), BF16)])
+        merge_kernel, (row_f, for_e_f, for_o_f, from_group, chosen_n), [((far, 3) + bb, F32), ((7 * far * B, B), BF16)])
     message_f = lax.all_gather(message_f, "gy", axis_index_groups=cores)
     (chosen_f,) = call(choose_far_kernel, (wanted, row_f, for_e_f, message_f), [((3 * far,) + bb, BF16)])
     arrived_f = lax.ppermute(chosen_f, "gy", across)
     shape = (2, 1, 3, 3) + bb
     (out,) = call(
         finish_near_kernel, (mine, row_n, for_e_n, message_n, arrived_n), [(shape, F32)], out_specs=[HBM],
-        scratch=[pltpu.VMEM((near, 3) + bb, F32), pltpu.SemaphoreType.DMA((near,))], cost=2 * 10**10)
+        scratch=[pltpu.VMEM((near, 3) + bb, F32), pltpu.SemaphoreType.DMA((near,))], cost=0)
     (out,) = call(
         finish_far_kernel, (mine, row_f, for_e_f, message_f, arrived_f, out), [(shape, F32)],
         in_specs=[VMEM] * 5 + [HBM], out_specs=[HBM], aliases={5: 0},

time: 47.4 us -> 44.6 us (0.941)
  starting transfers between devices: 31 us -> 25.6 us
  waiting for transfers between devices: 5.63 us -> 8.26 us
    ppermute x1, starting transfers between devices: 9.31 us -> 3.92 us  [on_device(): arrived_f = lax.ppermute(chosen_f, 'gy', across)]
    ppermute x1, waiting for transfers between devices: 0.01 us -> 5.28 us  [on_device(): arrived_n = lax.ppermute(chosen_n, 'gy', across)]
    ppermute x1, waiting for transfers between devices: 4.42 us -> 2.44 us  [on_device(): arrived_f = lax.ppermute(chosen_f, 'gy', across)]
    ppermute x1, waiting for transfers between devices: 1.2 us -> 0.52 us  [on_device(): message_n = lax.ppermute(message_n, 'gy', inside)]
  transfers between devices with their start and end apart: 7 -> 7, of which waited for: 2 -> 3; matrix products, arithmetic and copies ran while one was open for 0% -> 0% of each run, Pallas kernels for 7% -> 8%
where the time goes in v7:
time: 44.6 us; the launch traced here: 44.3 us
  starting transfers between devices  25.6 us (57%)
  waiting for transfers between devices  8.26 us (19%)
  Pallas kernels  5.92 us (13%)
  blocking collectives  4.46 us (10%)
    ppermute x1, starting transfers between devices, on_device(): from_east = lax.ppermute(west, 'gx', westward)  12.8 us
    pallas_call x8, Pallas kernels, call(): pl.pallas_call(kernel, in_specs=in_specs or [VMEM] * len(args), out_specs...  5.92 us
    ppermute x1, waiting for transfers between devices, on_device(): arrived_n = lax.ppermute(chosen_n, 'gy', across)  5.28 us
    ppermute x1, starting transfers between devices, on_device(): arrived_f = lax.ppermute(chosen_f, 'gy', across)  3.92 us
    ppermute x1, starting transfers between devices, on_device(): from_west = lax.ppermute(east, 'gx', eastward)  3.48 us
    all_gather x1, blocking collectives, on_device(): message_f = lax.all_gather(message_f, 'gy', axis_index_groups=cores)  2.46 us
    ppermute x1, waiting for transfers between devices, on_device(): arrived_f = lax.ppermute(chosen_f, 'gy', across)  2.44 us
    ppermute x1, starting transfers between devices, on_device(): message_n = lax.ppermute(message_n, 'gy', inside)  2.06 us
  transfers between devices with their start and end apart: 7, of which 3 were waited for; matrix products, arithmetic and copies ran while one was open for 0% of the time, Pallas kernels for 8%

profile of v7, /device:TPU:8, one launch (start us, length us, event | category | flops | bytes accessed | tf_op | source)
XLA Modules:
  0.0 44.3 jit_solution(14898534395009359197)
XLA Ops:
  0.0 1.7 %shard_map.64 = (bf16[2,4,128,128]{3,2,1,0:T(8,128)(2,1)S(1)}, bf16[2,4,5,128,128]{4,3,2,1,0:T(8,128)(2,1)S(1)}, bf16[2,2,128,128]{3,2,1,0:T(8,128)(2,1)S(1)}, b...) custom-call(s32[2,4,4]{2,1,0:T(4,128)} %a_links.1, ...), custom_call_target="tpu_custom_call" | custom-call | tf_op jit(solution)/shard_map/pallas_call | solution.py:21
  1.7 0.7 %collective-permute-start.3 = (bf16[1808,128]{1,0:T(8,128)(2,1)S(1)}, bf16[1808,128]{1,0:T(8,128)(2,1)S(1)}, u32[]{:S(2)}, u32[]{:S(2)}) collective-permute-start(bf16[1808,128]{1,0:T(8,128)(2,1)S(1)} %get-tuple-element.33), channel_id=1, source_target_pairs={{1,2},{3,4},{5,6},{7,8},{9,10},{11,12},{13,14},{15,16},{17,18},{19... | collective-permute-start | bytes 1388552 | tf_op jit(solution)/shard_map/ppermute | solution.py:348
  2.4 3.5 %collective-permute-start = (bf16[6,128,128]{2,1,0:T(8,128)(2,1)S(1)}, bf16[6,128,128]{2,1,0:T(8,128)(2,1)S(1)}, u32[]{:S(2)}, u32[]{:S(2)}) collective-permute-start(bf16[6,128,128]{2,1,0:T(8,128)(2,1)S(1)} %get-tuple-element.27), channel_id=1, source_target_pairs={{0,64},{64,128},{128,192},{192,256},{256,320},{320,384},{384,448},... | collective-permute-start | bytes 589832 | tf_op jit(solution)/shard_map/ppermute | solution.py:349
  5.9 12.8 %collective-permute-start.1 = (bf16[6,128,128]{2,1,0:T(8,128)(2,1)S(1)}, bf16[6,128,128]{2,1,0:T(8,128)(2,1)S(1)}, u32[]{:S(2)}, u32[]{:S(2)}) collective-permute-start(bf16[6,128,128]{2,1,0:T(8,128)(2,1)S(1)} %get-tuple-element.28), channel_id=1, source_target_pairs={{64,0},{128,64},{192,128},{256,192},{320,256},{384,320},{448,384},... | collective-permute-start | bytes 589832 | tf_op jit(solution)/shard_map/ppermute | solution.py:350
  18.7 2.0 %all-gather = bf16[1056,128]{1,0:T(8,128)(2,1)S(1)} all-gather(bf16[528,128]{1,0:T(8,128)(2,1)S(1)} %get-tuple-element.32), channel_id=2, replica_groups={{0,1},{2,3},{4,5},{6,7},{8,9},{10,11},{12,13},{14,15},{16,17},{18,19},{..., dimensions={0}, use_global_device_ids=true | all-gather | bytes 405504 | tf_op jit(solution)/shard_map/all_gather | solution.py:351
  20.7 0.0 collective-permute-done.3.halo_o
  20.7 1.2 %shard_map.66 = (f32[4,3,128,128]{3,2,1,0:T(8,128)S(1)}, f32[4,2,128,128]{3,2,1,0:T(8,128)S(1)}, bf16[2576,128]{1,0:T(8,128)(2,1)S(1)}) custom-call(bf16[2,4,128,128]{3,2,1,0:T(8,128)(2,1)S(1)} %get-tuple-element.24.own, bf16[2,4,5,128,128]{4,3,2,1,0:T(8,128)(2,1)S(1)} %get-tuple-element.25.a, bf16[2,2,128,128]{3,2,1,0:T(8,128)(2,1)S(1)} %get-tuple-element.26.sides, ...), custom_call_target="tpu_custom_call" | custom-call | tf_op jit(solution)/shard_map/pallas_call | solution.py:21
  21.9 2.1 %collective-permute-start.4 = (bf16[2576,128]{1,0:T(8,128)(2,1)S(1)}, bf16[2576,128]{1,0:T(8,128)(2,1)S(1)}, u32[]{:S(2)}, u32[]{:S(2)}) collective-permute-start(bf16[2576,128]{1,0:T(8,128)(2,1)S(1)} %get-tuple-element.36), channel_id=1, source_target_pairs={{0,1},{2,3},{4,5},{6,7},{8,9},{10,11},{12,13},{14,15},{16,17},{18,... | collective-permute-start | bytes 1978376 | tf_op jit(solution)/shard_map/ppermute | solution.py:355
  24.0 0.0 collective-permute-done.from_west
  24.0 0.0 collective-permute-done.1.from_east
  24.0 0.7 %shard_map.65 = (f32[2,3,128,128]{3,2,1,0:T(8,128)S(1)}, f32[2,2,128,128]{3,2,1,0:T(8,128)S(1)}, bf16[4,128,128]{2,1,0:T(8,128)(2,1)S(1)}) custom-call(bf16[2,4,128,128]{3,2,1,0:T(8,128)(2,1)S(1)} %get-tuple-element.24.own, bf16[2,4,5,128,128]{4,3,2,1,0:T(8,128)(2,1)S(1)} %get-tuple-element.25.a, bf16[2,2,128,128]{3,2,1,0:T(8,128)(2,1)S(1)} %get-tuple-element.26.sides, ...), custom_call_target="tpu_custom_call" | custom-call | flops 20000000000 | bytes 20000000000 | tf_op jit(solution)/shard_map/pallas_call | solution.py:21
  24.7 0.7 %collective-permute-start.2 = (bf16[4,128,128]{2,1,0:T(8,128)(2,1)S(1)}, bf16[4,128,128]{2,1,0:T(8,128)(2,1)S(1)}, u32[]{:S(2)}, u32[]{:S(2)}) collective-permute-start(bf16[4,128,128]{2,1,0:T(8,128)(2,1)S(1)} %get-tuple-element.31.for_o), channel_id=1, source_target_pairs={{3,4},{7,8},{11,12},{15,16},{19,20},{23,24},{27,28},{31,32},{35,36... | collective-permute-start | bytes 393224 | tf_op jit(solution)/shard_map/ppermute | solution.py:363
  25.4 0.5 %collective-permute-done.4.message = bf16[2576,128]{1,0:T(8,128)(2,1)S(1)} collective-permute-done((bf16[2576,128]{1,0:T(8,128)(2,1)S(1)}, bf16[2576,128]{1,0:T(8,128)(2,1)S(1)}, u32[]{:S(2)}, u32[]{:S(2)}) %collective-permute-start.4) | collective-permute-done | bytes 659488 | tf_op jit(solution)/shard_map/ppermute | solution.py:355
  25.9 0.2 shard_map.67
  26.2 1.9 %collective-permute-start.6 = (bf16[12,128,128]{2,1,0:T(8,128)(2,1)S(1)}, bf16[12,128,128]{2,1,0:T(8,128)(2,1)S(1)}, u32[]{:S(2)}, u32[]{:S(2)}) collective-permute-start(bf16[12,128,128]{2,1,0:T(8,128)(2,1)S(1)} %get-tuple-element.37.chosen), channel_id=1, source_target_pairs={{0,2},{1,3},{2,0},{3,1},{4,6},{5,7},{6,4},{7,5},{8,10},{9,11},{10,... | collective-permute-start | bytes 1179656 | tf_op jit(solution)/shard_map/ppermute | solution.py:362
  28.1 0.0 collective-permute-done.2.from_group
  28.1 0.1 shard_map.68
  28.2 2.5 %all-gather.1 = bf16[3584,128]{1,0:T(8,128)(2,1)S(1)} all-gather(bf16[1792,128]{1,0:T(8,128)(2,1)S(1)} %get-tuple-element.39), channel_id=3, replica_groups={{0,1},{2,3},{4,5},{6,7},{8,9},{10,11},{12,13},{14,15},{16,17},{18,19},{..., dimensions={0}, use_global_device_ids=true | all-gather | bytes 1376256 | tf_op jit(solution)/shard_map/all_gather | solution.py:366
  30.7 0.1 shard_map.69
  30.8 3.9 %collective-permute-start.5 = (bf16[6,128,128]{2,1,0:T(8,128)(2,1)S(1)}, bf16[6,128,128]{2,1,0:T(8,128)(2,1)S(1)}, u32[]{:S(2)}, u32[]{:S(2)}) collective-permute-start(bf16[6,128,128]{2,1,0:T(8,128)(2,1)S(1)} %shard_map.69), channel_id=1, source_target_pairs={{0,2},{1,3},{2,0},{3,1},{4,6},{5,7},{6,4},{7,5},{8,10},{9,11},{10,... | collective-permute-start | bytes 589832 | tf_op jit(solution)/shard_map/ppermute | solution.py:368
  34.7 5.3 %collective-permute-done.6.arrived = bf16[12,128,128]{2,1,0:T(8,128)(2,1)S(1)} collective-permute-done((bf16[12,128,128]{2,1,0:T(8,128)(2,1)S(1)}, bf16[12,128,128]{2,1,0:T(8,128)(2,1)S(1)}, u32[]{:S(2)}, u32[]{:S(2)}) %collective-permute-start.6) | collective-permute-done | bytes 393248 | tf_op jit(solution)/shard_map/ppermute | solution.py:362
  40.0 1.0 %shard_map.70.started = f32[2,1,3,3,128,128]{5,4,3,2,1,0:T(8,128)} custom-call(f32[16,128]{1,0:T(8,128)S(1)} %get-tuple-element.23.mine, f32[4,3,128,128]{3,2,1,0:T(8,128)S(1)} %get-tuple-element.34.row, f32[4,2,128,128]{3,2,1,0:T(8,128)S(1)} %get-tuple-element.35.for_e, bf16[2576,128]{1,0:T(8,128)(2,1)S(1)} %collective-permute-done.4.message, ...), custom_call_target="tpu_custom_call" | custom-call | tf_op jit(solution)/shard_map/pallas_call | solution.py:21
  41.0 2.4 %collective-permute-done.5.arrived = bf16[6,128,128]{2,1,0:T(8,128)(2,1)S(1)} collective-permute-done((bf16[6,128,128]{2,1,0:T(8,128)(2,1)S(1)}, bf16[6,128,128]{2,1,0:T(8,128)(2,1)S(1)}, u32[]{:S(2)}, u32[]{:S(2)}) %collective-permute-start.5) | collective-permute-done | bytes 196640 | tf_op jit(solution)/shard_map/ppermute | solution.py:368
  43.4 0.9 %shard_map.71 = f32[2,1,3,3,128,128]{5,4,3,2,1,0:T(8,128)} custom-call(f32[16,128]{1,0:T(8,128)S(1)} %get-tuple-element.23.mine, f32[2,3,128,128]{3,2,1,0:T(8,128)S(1)} %get-tuple-element.38.row, f32[2,2,128,128]{3,2,1,0:T(8,128)S(1)} %get-tuple-element.30.for_e, bf16[2,1792,128]{2,1,0:T(8,128)(2,1)S(1)} %bitcast.4, ...), custom_call_target="tpu_custom_call", output_to_operand_aliasing={{}: (5, {})} | custom-call | tf_op jit(solution)/shard_map/pallas_call | solution.py:21
Async XLA Ops:
  1.7 19.0 %collective-permute-start.3 = (bf16[1808,128]{1,0:T(8,128)(2,1)S(1)}, bf16[1808,128]{1,0:T(8,128)(2,1)S(1)}, u32[]{:S(2)}, u32[]{:S(2)}) collective-permute-start(bf16[1808,128]{1,0:T(8,128)(2,1)S(1)} %get-tuple-element.33), channel_id=1, source_target_pairs={{1,2},{3,4},{5,6},{7,8},{9,10},{11,12},{13,14},{15,16},{17,18},{19... | collective-permute-start | bytes 1388552 | tf_op jit(solution)/shard_map/ppermute | solution.py:348
  2.4 21.6 %collective-permute-start = (bf16[6,128,128]{2,1,0:T(8,128)(2,1)S(1)}, bf16[6,128,128]{2,1,0:T(8,128)(2,1)S(1)}, u32[]{:S(2)}, u32[]{:S(2)}) collective-permute-start(bf16[6,128,128]{2,1,0:T(8,128)(2,1)S(1)} %get-tuple-element.27), channel_id=1, source_target_pairs={{0,64},{64,128},{128,192},{192,256},{256,320},{320,384},{384,448},... | collective-permute-start | bytes 589832 | tf_op jit(solution)/shard_map/ppermute | solution.py:349
  5.9 18.1 %collective-permute-start.1 = (bf16[6,128,128]{2,1,0:T(8,128)(2,1)S(1)}, bf16[6,128,128]{2,1,0:T(8,128)(2,1)S(1)}, u32[]{:S(2)}, u32[]{:S(2)}) collective-permute-start(bf16[6,128,128]{2,1,0:T(8,128)(2,1)S(1)} %get-tuple-element.28), channel_id=1, source_target_pairs={{64,0},{128,64},{192,128},{256,192},{320,256},{384,320},{448,384},... | collective-permute-start | bytes 589832 | tf_op jit(solution)/shard_map/ppermute | solution.py:350
  21.9 4.0 %collective-permute-start.4 = (bf16[2576,128]{1,0:T(8,128)(2,1)S(1)}, bf16[2576,128]{1,0:T(8,128)(2,1)S(1)}, u32[]{:S(2)}, u32[]{:S(2)}) collective-permute-start(bf16[2576,128]{1,0:T(8,128)(2,1)S(1)} %get-tuple-element.36), channel_id=1, source_target_pairs={{0,1},{2,3},{4,5},{6,7},{8,9},{10,11},{12,13},{14,15},{16,17},{18,... | collective-permute-start | bytes 1978376 | tf_op jit(solution)/shard_map/ppermute | solution.py:355
  24.7 3.3 %collective-permute-start.2 = (bf16[4,128,128]{2,1,0:T(8,128)(2,1)S(1)}, bf16[4,128,128]{2,1,0:T(8,128)(2,1)S(1)}, u32[]{:S(2)}, u32[]{:S(2)}) collective-permute-start(bf16[4,128,128]{2,1,0:T(8,128)(2,1)S(1)} %get-tuple-element.31.for_o), channel_id=1, source_target_pairs={{3,4},{7,8},{11,12},{15,16},{19,20},{23,24},{27,28},{31,32},{35,36... | collective-permute-start | bytes 393224 | tf_op jit(solution)/shard_map/ppermute | solution.py:363
  26.2 13.9 %collective-permute-start.6 = (bf16[12,128,128]{2,1,0:T(8,128)(2,1)S(1)}, bf16[12,128,128]{2,1,0:T(8,128)(2,1)S(1)}, u32[]{:S(2)}, u32[]{:S(2)}) collective-permute-start(bf16[12,128,128]{2,1,0:T(8,128)(2,1)S(1)} %get-tuple-element.37.chosen), channel_id=1, source_target_pairs={{0,2},{1,3},{2,0},{3,1},{4,6},{5,7},{6,4},{7,5},{8,10},{9,11},{10,... | collective-permute-start | bytes 1179656 | tf_op jit(solution)/shard_map/ppermute | solution.py:362
  30.8 12.6 %collective-permute-start.5 = (bf16[6,128,128]{2,1,0:T(8,128)(2,1)S(1)}, bf16[6,128,128]{2,1,0:T(8,128)(2,1)S(1)}, u32[]{:S(2)}, u32[]{:S(2)}) collective-permute-start(bf16[6,128,128]{2,1,0:T(8,128)(2,1)S(1)} %shard_map.69), channel_id=1, source_target_pairs={{0,2},{1,3},{2,0},{3,1},{4,6},{5,7},{6,4},{7,5},{8,10},{9,11},{10,... | collective-permute-start | bytes 589832 | tf_op jit(solution)/shard_map/ppermute | solution.py:368

commit v8 on v7

--- a/solution.py
+++ b/solution.py
@@ -12,7 +12,8 @@
 VMEM = pl.BlockSpec(memory_space=pltpu.VMEM)
 HBM = pl.BlockSpec(memory_space=pltpu.HBM)
 
-NEAR = ((0, 2), (0, 1), (1, 0), (1, 1))
+A = ((0, 2), (1, 0))
+M = ((0, 1), (1, 1))
 FAR = ((0, 0), (1, 2))
 LINK_TILE = {0: 1, 2: 2}
 
@@ -47,7 +48,7 @@
 
 
 def begin_kernel(a_links, p_links, picks, own_in, side_in, a_in,
-                 own, a, sides, east, west, msg_o, msg_e, mine,
+                 own, a, sides, east, west, msg_o, mine,
                  s_links, s_side, s_picks, raw, sems):
     copies = [
         pltpu.make_async_copy(src, dst, sems.at[i])
@@ -76,17 +77,11 @@
     codes = jnp.where(rows < PAD // 2, s_picks[0, 0], s_picks[0, 1]).astype(F32)
     mine[...] = codes
     msg_o[pl.ds(14 * B, PAD)] = codes.astype(BF16)
-    msg_e[pl.ds(4 * B, PAD)] = codes.astype(BF16)
     copies[5].wait()
     for u in range(2):
         for j in range(4):
             for k in range(4):
                 a[u, j, k + 1] = a[u, j, k + 1] * s_links[u, j, k].astype(F32).astype(BF16)
-
-    def fill_e(j, k):
-        for u in range(2):
-            msg_e[tile(2 * u)] = own[u, j]
-            msg_e[tile(2 * u + 1)] = sides[u, k]
 
     def fill_o(j_o, k_o):
         for u in range(2):
@@ -105,15 +100,13 @@
                 beyond = a[u, j_o, 4]
                 panel = cat([other_block, other_side], 1)
             centre = dot(left, right).astype(BF16)
-            beside = dot(a[u, j_o, LINK_TILE[NEAR[2 * u][1]]], panel).astype(BF16)
+            beside = dot(a[u, j_o, LINK_TILE[A[u][1]]], panel).astype(BF16)
             result = dot_t(side, cat([centre, beyond, beside], 1)).astype(BF16)
             msg_o[tile(7 * u)] = block
             msg_o[tile(7 * u + 1)] = side
             for i in range(5):
                 msg_o[tile(7 * u + 2 + i)] = result[:, i * B:(i + 1) * B]
 
-    pl.when(core == 0)(lambda: fill_e(3, 1))
-    pl.when(core == 1)(lambda: fill_e(0, 0))
     pl.when(jnp.logical_and(core == 0, keep[0]))(lambda: fill_o(0, 0))
     pl.when(jnp.logical_and(core == 1, keep[1]))(lambda: fill_o(3, 1))
 
@@ -135,14 +128,43 @@
     return first[:, :B], [first[:, B:], inner[0], inner[1], last[:, :B]], last[:, B:]
 
 
-def near_kernel(own, a, sides, halo_e, halo_o, row, for_e, message):
+def first_kernel(own, a, sides, halo_o, mine, row, for_e, message):
+    core = lax.rem(lax.axis_index("gy"), 2)
+    even = core == 0
+    message[pl.ds(14 * B, PAD)] = mine[...].astype(BF16)
+    message[pl.ds(14 * B + PAD, PAD)] = halo_o[pl.ds(14 * B, PAD)]
+    for u, d in A:
+        message[tile(10 + 2 * u)] = jnp.where(even, own[u, 3], own[u, 0])
+        message[tile(10 + 2 * u + 1)] = jnp.where(even, sides[u, 1], sides[u, 0])
+        first, middle, last = link_products(a, u, d, [own[1 - u, j] for j in range(4)],
+                                            [sides[1 - u, k] for k in range(2)])
+        slots = reduce_units(own, u, (first, middle, last), 1)
+        given = dot_t(jnp.where(even, sides[u, 1], sides[u, 0]),
+                      cat([jnp.where(even, middle[3], first), jnp.where(even, last, middle[0])], 1))
+        emit(core, row, for_e, message, u, [value[0] for value in slots],
+             [halo_o[tile(7 * u + 5 + s)].astype(F32) for s in range(2)],
+             [given[:, s * B:(s + 1) * B] for s in range(2)])
+
+
+def emit(core, row, for_e, message, k, slots, extras, given):
+    for t in range(3):
+        row[k, t] = slots[t]
+    for s in range(2):
+        row[k, core + s] += extras[s]
+        for_e[k, s] = given[s]
+        message[tile(5 * k + 3 + s)] = given[s].astype(BF16)
+    for t in range(3):
+        message[tile(5 * k + t)] = row[k, t].astype(BF16)
+
+
+def second_kernel(own, a, sides, halo_e, halo_o, started, row, for_e, message):
+    del started
     core = lax.rem(lax.axis_index("gy"), 2)
     even = core == 0
     zero = jnp.zeros((B, B), BF16)
-    message[pl.ds(20 * B, PAD)] = halo_o[pl.ds(14 * B, PAD)]
     for u in range(2):
         def edge(k):
-            from_e, from_o = halo_e[1 - core, tile(2 * u + k)], halo_o[tile(7 * u + k)]
+            from_e, from_o = halo_e[1 - core, tile(10 + 2 * u + k)], halo_o[tile(7 * u + k)]
             return jnp.where(even, from_o, from_e), jnp.where(even, from_e, from_o)
 
         own_down, own_up = edge(0)
@@ -161,36 +183,21 @@
             centre.append(dot(left, cat([cat(r, 1) for r in right[j]], 0)).astype(BF16))
         left_part = [value[:, :B] for value in centre]
         right_part = [value[:, B:] for value in centre]
-        beside = link_products(a, u, NEAR[2 * u][1], [own[1 - u, j] for j in range(4)],
-                               [sides[1 - u, k] for k in range(2)])
-        first = cat([beside[0], left_part[0]], 1)
-        middle = [cat([beside[1][0], right_part[0]], 1), cat([beside[1][1], right_part[1]], 1),
-                  cat([beside[1][2], left_part[2]], 1), cat([beside[1][3], left_part[3]], 1)]
-        last = cat([beside[2], right_part[3]], 1)
-        slots = reduce_units(own, u, (first, middle, last), 2)
-        slots[0][1] = slots[0][1] + dot_t(o[1], left_part[1])
-        slots[2][1] = slots[2][1] + dot_t(o[2], right_part[2])
+        first, last = left_part[0], right_part[3]
+        middle = [right_part[0], right_part[1], left_part[2], left_part[3]]
+        slots = [value[0] for value in reduce_units(own, u, (first, middle, last), 1)]
+        slots[0] = slots[0] + dot_t(o[1], left_part[1])
+        slots[2] = slots[2] + dot_t(o[2], right_part[2])
         beyond = dot(halo_o[tile(7 * u + 4)], cat([jnp.where(even, low, o[3]), jnp.where(even, o[0], high)], 1))
         given = dot_t(jnp.where(even, high, low),
                       cat([jnp.where(even, middle[3], first), jnp.where(even, last, middle[0])], 1))
-        for i in range(2):
-            k = 2 * u + i
-            for t in range(3):
-                row[k, t] = slots[t][i]
-            for s in range(2):
-                if i == 0:
-                    extra = halo_o[tile(7 * u + 5 + s)].astype(F32)
-                else:
-                    extra = halo_o[tile(7 * u + 2 + s)].astype(F32) + beyond[:, s * B:(s + 1) * B]
-                row[k, core + s] += extra
-                part = given[:, (2 * s + i) * B:(2 * s + i + 1) * B]
-                for_e[k, s] = part
-                message[tile(5 * k + 3 + s)] = part.astype(BF16)
-            for t in range(3):
-                message[tile(5 * k + t)] = row[k, t].astype(BF16)
-
-
-def far_kernel(own, a, sides, from_west, from_east, row, for_e, for_o):
+        emit(core, row, for_e, message, u, slots,
+             [halo_o[tile(7 * u + 2 + s)].astype(F32) + beyond[:, s * B:(s + 1) * B] for s in range(2)],
+             [given[:, s * B:(s + 1) * B] for s in range(2)])
+
+
+def far_kernel(own, a, sides, from_east, from_west, started, row, for_e, for_o):
+    del started
     even = lax.rem(lax.axis_index("gy"), 2) == 0
     for k, (u, d) in enumerate(FAR):
         arrived = from_west if d == 0 else from_east
@@ -207,7 +214,8 @@
             for_o[2 * k + s] = to_o[:, at].astype(BF16)
 
 
-def merge_kernel(row, for_e, for_o, from_group, chosen, row_out, message):
+def merge_kernel(row, for_e, for_o, from_group, started, row_out, message):
+    del started
     core = lax.rem(lax.axis_index("gy"), 2)
     for k in range(len(FAR)):
         for t in range(3):
@@ -236,15 +244,18 @@
 
 
 def complete(core, row, for_e, message, k, t):
+    def theirs_at(i):
+        return message[1 - core, tile(5 * k + i)].astype(F32)
+
     mine = row[k, t]
-    theirs = message[tile(5 * k + t)].astype(F32)
+    theirs = theirs_at(t)
     if t == 1:
-        mine = mine + message[tile(5 * k + 3 + core)].astype(F32)
+        mine = mine + theirs_at(3 + core)
         theirs = theirs + for_e[k, 1 - core]
     else:
         gets = (core == 0) == (t == 2)
         s = 1 if t == 2 else 0
-        mine = mine + jnp.where(gets, message[tile(5 * k + 3 + s)].astype(F32), 0.0)
+        mine = mine + jnp.where(gets, theirs_at(3 + s), 0.0)
         theirs = theirs + jnp.where(gets, 0.0, for_e[k, s])
     return mine, theirs
 
@@ -256,20 +267,28 @@
             jnp.broadcast_to(code == other.astype(F32), (B, B)))
 
 
-def choose_near_kernel(mine, row, for_e, message, halo_e, halo_o, row_far, out, wanted):
-    del row_far
+def choose(units, core, position, codes, row, for_e, message, out):
+    for k, (u, _) in enumerate(units):
+        use_mine, use_theirs = masks(codes, u, position, core)
+        for t in range(3):
+            own_row, other_row = complete(core, row, for_e, message, k, t)
+            out[3 * k + t] = jnp.where(use_mine, own_row, jnp.where(use_theirs, other_row, 0.0)).astype(BF16)
+
+
+def choose_first_kernel(mine, row, for_e, message, halo_o, out, wanted):
     c = lax.axis_index("gy")
     core, position = lax.rem(c, 2), lax.rem(c, 4)
     outer = jnp.logical_or(position == 0, position == 3)
-    inferred = 6.0 - mine[...] - halo_e[1 - core, pl.ds(4 * B, PAD)].astype(F32)
+    inferred = 6.0 - mine[...] - message[1 - core, pl.ds(14 * B, PAD)].astype(F32)
     inferred = inferred - halo_o[pl.ds(14 * B, PAD)].astype(F32)
-    codes = jnp.where(outer, message[pl.ds(20 * B, PAD)].astype(F32), inferred)
+    codes = jnp.where(outer, message[1 - core, pl.ds(14 * B + PAD, PAD)].astype(F32), inferred)
     wanted[...] = codes
-    for k, (u, _) in enumerate(NEAR):
-        use_mine, use_theirs = masks(codes, u, position, core)
-        for t in range(3):
-            own_row, other_row = complete(core, row, for_e, message, k, t)
-            out[3 * k + t] = jnp.where(use_mine, own_row, jnp.where(use_theirs, other_row, 0.0)).astype(BF16)
+    choose(A, core, position, codes, row, for_e, message, out)
+
+
+def choose_second_kernel(wanted, row, for_e, message, out):
+    c = lax.axis_index("gy")
+    choose(M, lax.rem(c, 2), lax.rem(c, 4), wanted[...], row, for_e, message, out)
 
 
 def choose_far_kernel(wanted, row, for_e, message, out):
@@ -282,18 +301,22 @@
             out[3 * k + t] = jnp.where(use_mine, mine, jnp.where(use_theirs, theirs, inner)).astype(BF16)
 
 
-def finish_near_kernel(mine, row, for_e, message, arrived, out, buffer, sems):
+def finish_near_kernel(mine, row_a, for_e_a, message_a, arrived_a, row_m, for_e_m, message_m, arrived_m,
+                       out, buffer, sems):
     c = lax.axis_index("gy")
     core, position = lax.rem(c, 2), lax.rem(c, 4)
     copies = []
-    for k, (u, d) in enumerate(NEAR):
-        use_mine, use_theirs = masks(mine[...], u, position, core)
-        for t in range(3):
-            own_row, other_row = complete(core, row, for_e, message, k, t)
-            got = arrived[3 * k + t].astype(F32)
-            buffer[k, t] = jnp.where(use_mine, own_row, jnp.where(use_theirs, other_row, got))
-        copies.append(pltpu.make_async_copy(buffer.at[k], out.at[u, 0, d], sems.at[k]))
-        copies[-1].start()
+    for units, row, for_e, message, arrived in ((A, row_a, for_e_a, message_a, arrived_a),
+                                                (M, row_m, for_e_m, message_m, arrived_m)):
+        for k, (u, d) in enumerate(units):
+            use_mine, use_theirs = masks(mine[...], u, position, core)
+            at = len(copies)
+            for t in range(3):
+                own_row, other_row = complete(core, row, for_e, message, k, t)
+                got = arrived[3 * k + t].astype(F32)
+                buffer[at, t] = jnp.where(use_mine, own_row, jnp.where(use_theirs, other_row, got))
+            copies.append(pltpu.make_async_copy(buffer.at[at], out.at[u, 0, d], sems.at[at]))
+            copies[-1].start()
     for copy in copies:
         copy.wait()
 
@@ -334,46 +357,55 @@
     eastward = [(i, i + 1) for i in range(columns - 1)]
     westward = [(b, a) for a, b in eastward]
     bb = (B, B)
-    near, far = len(NEAR), len(FAR)
-
-    own, a, sides, east, west, msg_o, msg_e, mine = call(
+    pair, six = ((2, 3) + bb, F32), ((6,) + bb, BF16)
+    give = ((2, 2) + bb, F32)
+    four = ((4,) + bb, BF16)
+
+    own, a, sides, east, west, msg_o, mine = call(
         begin_kernel,
         [pltpu.with_memory_space_constraint(x, pltpu.HBM)
          for x in (a_links, p_links, coarse_pick.T, p_own, p_side, a_tiles)],
-        [(p_own.shape, BF16), (a_tiles.shape, BF16), ((2, 2) + bb, BF16), ((6,) + bb, BF16), ((6,) + bb, BF16),
-         ((14 * B + PAD, B), BF16), ((4 * B + PAD, B), BF16), ((PAD, B), F32)],
+        [(p_own.shape, BF16), (a_tiles.shape, BF16), ((2, 2) + bb, BF16), six, six,
+         ((14 * B + PAD, B), BF16), ((PAD, B), F32)],
         in_specs=[HBM] * 6,
         scratch=[pltpu.SMEM(a_links.shape, jnp.int32), pltpu.SMEM(p_links.shape, jnp.int32),
                  pltpu.SMEM((1, 2), jnp.int32), pltpu.VMEM(p_side.shape, BF16), pltpu.SemaphoreType.DMA((6,))])
+    from_east = lax.ppermute(west, "gx", westward)
+    from_west = lax.ppermute(east, "gx", eastward)
     halo_o = lax.ppermute(msg_o, "gy", outside)
-    from_west = lax.ppermute(east, "gx", eastward)
-    from_east = lax.ppermute(west, "gx", westward)
-    halo_e = lax.all_gather(msg_e, "gy", axis_index_groups=cores)
-    row_n, for_e_n, message_n = call(
-        near_kernel, (own, a, sides, halo_e, halo_o),
-        [((near, 3) + bb, F32), ((near, 2) + bb, F32), ((5 * near * B + PAD, B), BF16)])
-    message_n = lax.ppermute(message_n, "gy", inside)
+
+    row_a, for_e_a, message_a = call(
+        first_kernel, (own, a, sides, halo_o, mine), [pair, give, ((14 * B + 2 * PAD, B), BF16)])
+    message_a = lax.all_gather(message_a, "gy", axis_index_groups=cores)
+    chosen_a, wanted = call(
+        choose_first_kernel, (mine, row_a, for_e_a, message_a, halo_o), [six, ((PAD, B), F32)])
+    arrived_a = lax.ppermute(chosen_a, "gy", across)
+
     row_f, for_e_f, for_o_f = call(
-        far_kernel, (own, a, sides, from_west, from_east),
-        [((far, 3) + bb, F32), ((far, 2) + bb, F32), ((2 * far,) + bb, BF16)], cost=20000000000)
-    chosen_n, wanted = call(
-        choose_near_kernel, (mine, row_n, for_e_n, message_n, halo_e, halo_o, row_f),
-        [((3 * near,) + bb, BF16), ((PAD, B), F32)])
-    arrived_n = lax.ppermute(chosen_n, "gy", across)
+        far_kernel, (own, a, sides, from_east, from_west, chosen_a), [pair, give, four], cost=0)
     from_group = lax.ppermute(for_o_f, "gy", between)
+
+    row_m, for_e_m, message_m = call(
+        second_kernel, (own, a, sides, message_a, halo_o, row_f), [pair, give, ((10 * B, B), BF16)], cost=0)
+    message_m = lax.all_gather(message_m, "gy", axis_index_groups=cores)
+    (chosen_m,) = call(choose_second_kernel, (wanted, row_m, for_e_m, message_m), [six])
+    arrived_m = lax.ppermute(chosen_m, "gy", across)
+
     row_f, message_f = call(
-        merge_kernel, (row_f, for_e_f, for_o_f, from_group, chosen_n), [((far, 3) + bb, F32), ((7 * far * B, B), BF16)])
+        merge_kernel, (row_f, for_e_f, for_o_f, from_group, arrived_a), [pair, ((14 * B, B), BF16)])
     message_f = lax.all_gather(message_f, "gy", axis_index_groups=cores)
-    (chosen_f,) = call(choose_far_kernel, (wanted, row_f, for_e_f, message_f), [((3 * far,) + bb, BF16)])
+    (chosen_f,) = call(choose_far_kernel, (wanted, row_f, for_e_f, message_f), [six])
     arrived_f = lax.ppermute(chosen_f, "gy", across)
+
     shape = (2, 1, 3, 3) + bb
     (out,) = call(
-        finish_near_kernel, (mine, row_n, for_e_n, message_n, arrived_n), [(shape, F32)], out_specs=[HBM],
-        scratch=[pltpu.VMEM((near, 3) + bb, F32), pltpu.SemaphoreType.DMA((near,))], cost=0)
+        finish_near_kernel, (mine, row_a, for_e_a, message_a, arrived_a, row_m, for_e_m, message_m, arrived_m),
+        [(shape, F32)], out_specs=[HBM], cost=0,
+        scratch=[pltpu.VMEM((4, 3) + bb, F32), pltpu.SemaphoreType.DMA((4,))])
     (out,) = call(
         finish_far_kernel, (mine, row_f, for_e_f, message_f, arrived_f, out), [(shape, F32)],
         in_specs=[VMEM] * 5 + [HBM], out_specs=[HBM], aliases={5: 0},
-        scratch=[pltpu.VMEM((far, 3) + bb, F32), pltpu.SemaphoreType.DMA((far,))])
+        scratch=[pltpu.VMEM((2, 3) + bb, F32), pltpu.SemaphoreType.DMA((2,))])
     return out
 
 

time: 44.6 us -> 48.7 us (1.092)
  the two profiles are of different devices: /device:TPU:8 before, /device:TPU:1 now
where the time goes in v8:
time: 48.7 us; the launch traced here: 48.4 us
  starting transfers between devices  19.3 us (40%)
  blocking collectives  15.9 us (33%)
  Pallas kernels  7 us (14%)
  waiting for transfers between devices  6 us (12%)
    all_gather x1, blocking collectives, on_device(): message_a = lax.all_gather(message_a, 'gy', axis_index_groups=cores)  11.1 us
    pallas_call x10, Pallas kernels, call(): pl.pallas_call(kernel, in_specs=in_specs or [VMEM] * len(args), out_specs...  7 us
    ppermute x1, starting transfers between devices, on_device(): halo_o = lax.ppermute(msg_o, 'gy', outside)  4.93 us
    ppermute x1, waiting for transfers between devices, on_device(): arrived_f = lax.ppermute(chosen_f, 'gy', across)  4.69 us
    ppermute x1, starting transfers between devices, on_device(): arrived_m = lax.ppermute(chosen_m, 'gy', across)  4.61 us
    ppermute x1, starting transfers between devices, on_device(): from_west = lax.ppermute(east, 'gx', eastward)  4 us
    all_gather x1, blocking collectives, on_device(): message_f = lax.all_gather(message_f, 'gy', axis_index_groups=cores)  2.52 us
    all_gather x1, blocking collectives, on_device(): message_m = lax.all_gather(message_m, 'gy', axis_index_groups=cores)  2.28 us
  transfers between devices with their start and end apart: 7, of which 3 were waited for; matrix products, arithmetic and copies ran while one was open for 0% of the time, Pallas kernels for 8%

profile of v8, /device:TPU:1, one launch (start us, length us, event | category | flops | bytes accessed | tf_op | source)
XLA Modules:
  0.0 48.4 jit_solution(1213665975992510407)
XLA Ops:
  0.0 2.2 %shard_map.64 = (bf16[2,4,128,128]{3,2,1,0:T(8,128)(2,1)S(1)}, bf16[2,4,5,128,128]{4,3,2,1,0:T(8,128)(2,1)S(1)}, bf16[2,2,128,128]{3,2,1,0:T(8,128)(2,1)S(1)}, b...) custom-call(s32[2,4,4]{2,1,0:T(4,128)} %a_links.1, ...), custom_call_target="tpu_custom_call" | custom-call | tf_op jit(solution)/shard_map/pallas_call | solution.py:22
  2.2 4.9 %collective-permute-start.2 = (bf16[1808,128]{1,0:T(8,128)(2,1)S(1)}, bf16[1808,128]{1,0:T(8,128)(2,1)S(1)}, u32[]{:S(2)}, u32[]{:S(2)}) collective-permute-start(bf16[1808,128]{1,0:T(8,128)(2,1)S(1)} %get-tuple-element.31), channel_id=1, source_target_pairs={{1,2},{3,4},{5,6},{7,8},{9,10},{11,12},{13,14},{15,16},{17,18},{19... | collective-permute-start | bytes 1388552 | tf_op jit(solution)/shard_map/ppermute | solution.py:375
  7.2 1.3 %collective-permute-start = (bf16[6,128,128]{2,1,0:T(8,128)(2,1)S(1)}, bf16[6,128,128]{2,1,0:T(8,128)(2,1)S(1)}, u32[]{:S(2)}, u32[]{:S(2)}) collective-permute-start(bf16[6,128,128]{2,1,0:T(8,128)(2,1)S(1)} %get-tuple-element.29), channel_id=1, source_target_pairs={{64,0},{128,64},{192,128},{256,192},{320,256},{384,320},{448,384},... | collective-permute-start | bytes 589832 | tf_op jit(solution)/shard_map/ppermute | solution.py:373
  8.5 4.0 %collective-permute-start.1 = (bf16[6,128,128]{2,1,0:T(8,128)(2,1)S(1)}, bf16[6,128,128]{2,1,0:T(8,128)(2,1)S(1)}, u32[]{:S(2)}, u32[]{:S(2)}) collective-permute-start(bf16[6,128,128]{2,1,0:T(8,128)(2,1)S(1)} %get-tuple-element.30), channel_id=1, source_target_pairs={{0,64},{64,128},{128,192},{192,256},{256,320},{320,384},{384,448},... | collective-permute-start | bytes 589832 | tf_op jit(solution)/shard_map/ppermute | solution.py:374
  12.5 0.9 %collective-permute-done.2.halo_o = bf16[1808,128]{1,0:T(8,128)(2,1)S(1)} collective-permute-done((bf16[1808,128]{1,0:T(8,128)(2,1)S(1)}, bf16[1808,128]{1,0:T(8,128)(2,1)S(1)}, u32[]{:S(2)}, u32[]{:S(2)}) %collective-permute-start.2) | collective-permute-done | bytes 462880 | tf_op jit(solution)/shard_map/ppermute | solution.py:375
  13.4 0.7 %shard_map.65 = (f32[2,3,128,128]{3,2,1,0:T(8,128)S(1)}, f32[2,2,128,128]{3,2,1,0:T(8,128)S(1)}, bf16[1824,128]{1,0:T(8,128)(2,1)S(1)}) custom-call(bf16[2,4,128,128]{3,2,1,0:T(8,128)(2,1)S(1)} %get-tuple-element.26.own, bf16[2,4,5,128,128]{4,3,2,1,0:T(8,128)(2,1)S(1)} %get-tuple-element.27.a, bf16[2,2,128,128]{3,2,1,0:T(8,128)(2,1)S(1)} %get-tuple-element.28.sides, ...), custom_call_target="tpu_custom_call" | custom-call | tf_op jit(solution)/shard_map/pallas_call | solution.py:22
  14.1 11.1 %all-gather = bf16[3648,128]{1,0:T(8,128)(2,1)S(1)} all-gather(bf16[1824,128]{1,0:T(8,128)(2,1)S(1)} %get-tuple-element.34), channel_id=2, replica_groups={{0,1},{2,3},{4,5},{6,7},{8,9},{10,11},{12,13},{14,15},{16,17},{18,19},{..., dimensions={0}, use_global_device_ids=true | all-gather | bytes 1400832 | tf_op jit(solution)/shard_map/all_gather | solution.py:379
  25.3 0.1 shard_map.66
  25.4 1.9 %collective-permute-start.4 = (bf16[6,128,128]{2,1,0:T(8,128)(2,1)S(1)}, bf16[6,128,128]{2,1,0:T(8,128)(2,1)S(1)}, u32[]{:S(2)}, u32[]{:S(2)}) collective-permute-start(bf16[6,128,128]{2,1,0:T(8,128)(2,1)S(1)} %get-tuple-element.35.started), channel_id=1, source_target_pairs={{0,2},{1,3},{2,0},{3,1},{4,6},{5,7},{6,4},{7,5},{8,10},{9,11},{10,... | collective-permute-start | bytes 589832 | tf_op jit(solution)/shard_map/ppermute | solution.py:382
  27.3 0.0 collective-permute-done.from_east
  27.3 0.7 %shard_map.67 = (f32[2,3,128,128]{3,2,1,0:T(8,128)S(1)}, f32[2,2,128,128]{3,2,1,0:T(8,128)S(1)}, bf16[4,128,128]{2,1,0:T(8,128)(2,1)S(1)}) custom-call(bf16[2,4,128,128]{3,2,1,0:T(8,128)(2,1)S(1)} %get-tuple-element.26.own, bf16[2,4,5,128,128]{4,3,2,1,0:T(8,128)(2,1)S(1)} %get-tuple-element.27.a, bf16[2,2,128,128]{3,2,1,0:T(8,128)(2,1)S(1)} %get-tuple-element.28.sides, ...), custom_call_target="tpu_custom_call" | custom-call | tf_op jit(solution)/shard_map/pallas_call | solution.py:22
  28.0 0.7 %collective-permute-start.3 = (bf16[4,128,128]{2,1,0:T(8,128)(2,1)S(1)}, bf16[4,128,128]{2,1,0:T(8,128)(2,1)S(1)}, u32[]{:S(2)}, u32[]{:S(2)}) collective-permute-start(bf16[4,128,128]{2,1,0:T(8,128)(2,1)S(1)} %get-tuple-element.38.for_o), channel_id=1, source_target_pairs={{3,4},{7,8},{11,12},{15,16},{19,20},{23,24},{27,28},{31,32},{35,36... | collective-permute-start | bytes 393224 | tf_op jit(solution)/shard_map/ppermute | solution.py:386
  28.7 1.0 %shard_map.70 = (f32[2,3,128,128]{3,2,1,0:T(8,128)S(1)}, f32[2,2,128,128]{3,2,1,0:T(8,128)S(1)}, bf16[1280,128]{1,0:T(8,128)(2,1)S(1)}) custom-call(bf16[2,4,128,128]{3,2,1,0:T(8,128)(2,1)S(1)} %get-tuple-element.26.own, bf16[2,4,5,128,128]{4,3,2,1,0:T(8,128)(2,1)S(1)} %get-tuple-element.27.a, bf16[2,2,128,128]{3,2,1,0:T(8,128)(2,1)S(1)} %get-tuple-element.28.sides, ...), custom_call_target="tpu_custom_call" | custom-call | tf_op jit(solution)/shard_map/pallas_call | solution.py:22
  29.7 2.3 %all-gather.2 = bf16[2560,128]{1,0:T(8,128)(2,1)S(1)} all-gather(bf16[1280,128]{1,0:T(8,128)(2,1)S(1)} %get-tuple-element.44), channel_id=4, replica_groups={{0,1},{2,3},{4,5},{6,7},{8,9},{10,11},{12,13},{14,15},{16,17},{18,19},{..., dimensions={0}, use_global_device_ids=true | all-gather | bytes 983040 | tf_op jit(solution)/shard_map/all_gather | solution.py:390
  32.0 0.1 shard_map.71
  32.1 4.6 %collective-permute-start.6 = (bf16[6,128,128]{2,1,0:T(8,128)(2,1)S(1)}, bf16[6,128,128]{2,1,0:T(8,128)(2,1)S(1)}, u32[]{:S(2)}, u32[]{:S(2)}) collective-permute-start(bf16[6,128,128]{2,1,0:T(8,128)(2,1)S(1)} %shard_map.71), channel_id=1, source_target_pairs={{0,2},{1,3},{2,0},{3,1},{4,6},{5,7},{6,4},{7,5},{8,10},{9,11},{10,... | collective-permute-start | bytes 589832 | tf_op jit(solution)/shard_map/ppermute | solution.py:392
  36.7 0.1 shard_map.68
  36.9 2.5 %all-gather.1 = bf16[3584,128]{1,0:T(8,128)(2,1)S(1)} all-gather(bf16[1792,128]{1,0:T(8,128)(2,1)S(1)} %get-tuple-element.40), channel_id=3, replica_groups={{0,1},{2,3},{4,5},{6,7},{8,9},{10,11},{12,13},{14,15},{16,17},{18,19},{..., dimensions={0}, use_global_device_ids=true | all-gather | bytes 1376256 | tf_op jit(solution)/shard_map/all_gather | solution.py:396
  39.4 0.1 shard_map.69
  39.5 1.9 %collective-permute-start.5 = (bf16[6,128,128]{2,1,0:T(8,128)(2,1)S(1)}, bf16[6,128,128]{2,1,0:T(8,128)(2,1)S(1)}, u32[]{:S(2)}, u32[]{:S(2)}) collective-permute-start(bf16[6,128,128]{2,1,0:T(8,128)(2,1)S(1)} %shard_map.69), channel_id=1, source_target_pairs={{0,2},{1,3},{2,0},{3,1},{4,6},{5,7},{6,4},{7,5},{8,10},{9,11},{10,... | collective-permute-start | bytes 589832 | tf_op jit(solution)/shard_map/ppermute | solution.py:398
  41.4 0.4 collective-permute-done.6.arrived_m
  41.9 1.0 %shard_map.72.started = f32[2,1,3,3,128,128]{5,4,3,2,1,0:T(8,128)} custom-call(f32[16,128]{1,0:T(8,128)S(1)} %get-tuple-element.25.mine, f32[2,3,128,128]{3,2,1,0:T(8,128)S(1)} %get-tuple-element.32.row.row_a, f32[2,2,128,128]{3,2,1,0:T(8,128)S(1)} %get-tuple-element.33.for_e.for_e_a, bf16[2,1824,128]{2,1,0:T(8,128)(2,1)S(1)} %bitcast.6, ...), custom_call_target="tpu_custom_call" | custom-call | tf_op jit(solution)/shard_map/pallas_call | solution.py:22
  42.8 4.7 %collective-permute-done.5.arrived = bf16[6,128,128]{2,1,0:T(8,128)(2,1)S(1)} collective-permute-done((bf16[6,128,128]{2,1,0:T(8,128)(2,1)S(1)}, bf16[6,128,128]{2,1,0:T(8,128)(2,1)S(1)}, u32[]{:S(2)}, u32[]{:S(2)}) %collective-permute-start.5) | collective-permute-done | bytes 196640 | tf_op jit(solution)/shard_map/ppermute | solution.py:398
  47.5 0.9 %shard_map.73 = f32[2,1,3,3,128,128]{5,4,3,2,1,0:T(8,128)} custom-call(f32[16,128]{1,0:T(8,128)S(1)} %get-tuple-element.25.mine, f32[2,3,128,128]{3,2,1,0:T(8,128)S(1)} %get-tuple-element.39.row, f32[2,2,128,128]{3,2,1,0:T(8,128)S(1)} %get-tuple-element.37.for_e, bf16[2,1792,128]{2,1,0:T(8,128)(2,1)S(1)} %bitcast.8, ...), custom_call_target="tpu_custom_call", output_to_operand_aliasing={{}: (5, {})} | custom-call | tf_op jit(solution)/shard_map/pallas_call | solution.py:22
  (3 shorter events, 0.0 us)
Async XLA Ops:
  2.2 11.1 %collective-permute-start.2 = (bf16[1808,128]{1,0:T(8,128)(2,1)S(1)}, bf16[1808,128]{1,0:T(8,128)(2,1)S(1)}, u32[]{:S(2)}, u32[]{:S(2)}) collective-permute-start(bf16[1808,128]{1,0:T(8,128)(2,1)S(1)} %get-tuple-element.31), channel_id=1, source_target_pairs={{1,2},{3,4},{5,6},{7,8},{9,10},{11,12},{13,14},{15,16},{17,18},{19... | collective-permute-start | bytes 1388552 | tf_op jit(solution)/shard_map/ppermute | solution.py:375
  7.2 20.1 %collective-permute-start = (bf16[6,128,128]{2,1,0:T(8,128)(2,1)S(1)}, bf16[6,128,128]{2,1,0:T(8,128)(2,1)S(1)}, u32[]{:S(2)}, u32[]{:S(2)}) collective-permute-start(bf16[6,128,128]{2,1,0:T(8,128)(2,1)S(1)} %get-tuple-element.29), channel_id=1, source_target_pairs={{64,0},{128,64},{192,128},{256,192},{320,256},{384,320},{448,384},... | collective-permute-start | bytes 589832 | tf_op jit(solution)/shard_map/ppermute | solution.py:373
  8.5 18.8 %collective-permute-start.1 = (bf16[6,128,128]{2,1,0:T(8,128)(2,1)S(1)}, bf16[6,128,128]{2,1,0:T(8,128)(2,1)S(1)}, u32[]{:S(2)}, u32[]{:S(2)}) collective-permute-start(bf16[6,128,128]{2,1,0:T(8,128)(2,1)S(1)} %get-tuple-element.30), channel_id=1, source_target_pairs={{0,64},{64,128},{128,192},{192,256},{256,320},{320,384},{384,448},... | collective-permute-start | bytes 589832 | tf_op jit(solution)/shard_map/ppermute | solution.py:374
  25.4 11.4 %collective-permute-start.4 = (bf16[6,128,128]{2,1,0:T(8,128)(2,1)S(1)}, bf16[6,128,128]{2,1,0:T(8,128)(2,1)S(1)}, u32[]{:S(2)}, u32[]{:S(2)}) collective-permute-start(bf16[6,128,128]{2,1,0:T(8,128)(2,1)S(1)} %get-tuple-element.35.started), channel_id=1, source_target_pairs={{0,2},{1,3},{2,0},{3,1},{4,6},{5,7},{6,4},{7,5},{8,10},{9,11},{10,... | collective-permute-start | bytes 589832 | tf_op jit(solution)/shard_map/ppermute | solution.py:382
  28.0 8.7 %collective-permute-start.3 = (bf16[4,128,128]{2,1,0:T(8,128)(2,1)S(1)}, bf16[4,128,128]{2,1,0:T(8,128)(2,1)S(1)}, u32[]{:S(2)}, u32[]{:S(2)}) collective-permute-start(bf16[4,128,128]{2,1,0:T(8,128)(2,1)S(1)} %get-tuple-element.38.for_o), channel_id=1, source_target_pairs={{3,4},{7,8},{11,12},{15,16},{19,20},{23,24},{27,28},{31,32},{35,36... | collective-permute-start | bytes 393224 | tf_op jit(solution)/shard_map/ppermute | solution.py:386
  32.1 9.7 %collective-permute-start.6 = (bf16[6,128,128]{2,1,0:T(8,128)(2,1)S(1)}, bf16[6,128,128]{2,1,0:T(8,128)(2,1)S(1)}, u32[]{:S(2)}, u32[]{:S(2)}) collective-permute-start(bf16[6,128,128]{2,1,0:T(8,128)(2,1)S(1)} %shard_map.71), channel_id=1, source_target_pairs={{0,2},{1,3},{2,0},{3,1},{4,6},{5,7},{6,4},{7,5},{8,10},{9,11},{10,... | collective-permute-start | bytes 589832 | tf_op jit(solution)/shard_map/ppermute | solution.py:392
  39.5 8.0 %collective-permute-start.5 = (bf16[6,128,128]{2,1,0:T(8,128)(2,1)S(1)}, bf16[6,128,128]{2,1,0:T(8,128)(2,1)S(1)}, u32[]{:S(2)}, u32[]{:S(2)}) collective-permute-start(bf16[6,128,128]{2,1,0:T(8,128)(2,1)S(1)} %shard_map.69), channel_id=1, source_target_pairs={{0,2},{1,3},{2,0},{3,1},{4,6},{5,7},{6,4},{7,5},{8,10},{9,11},{10,... | collective-permute-start | bytes 589832 | tf_op jit(solution)/shard_map/ppermute | solution.py:398

commit v9 on v8

--- a/solution.py
+++ b/solution.py
@@ -196,7 +196,7 @@
              [given[:, s * B:(s + 1) * B] for s in range(2)])
 
 
-def far_kernel(own, a, sides, from_east, from_west, started, row, for_e, for_o):
+def far_kernel(own, a, sides, from_west, from_east, started, row, for_e, for_o):
     del started
     even = lax.rem(lax.axis_index("gy"), 2) == 0
     for k, (u, d) in enumerate(FAR):
@@ -214,8 +214,8 @@
             for_o[2 * k + s] = to_o[:, at].astype(BF16)
 
 
-def merge_kernel(row, for_e, for_o, from_group, started, row_out, message):
-    del started
+def merge_kernel(row, for_e, for_o, from_group, started, chosen, row_out, message):
+    del started, chosen
     core = lax.rem(lax.axis_index("gy"), 2)
     for k in range(len(FAR)):
         for t in range(3):
@@ -245,7 +245,8 @@
 
 def complete(core, row, for_e, message, k, t):
     def theirs_at(i):
-        return message[1 - core, tile(5 * k + i)].astype(F32)
+        value = message[1 - core, tile(5 * k + i)] if len(message.shape) == 3 else message[tile(5 * k + i)]
+        return value.astype(F32)
 
     mine = row[k, t]
     theirs = theirs_at(t)
@@ -286,7 +287,8 @@
     choose(A, core, position, codes, row, for_e, message, out)
 
 
-def choose_second_kernel(wanted, row, for_e, message, out):
+def choose_second_kernel(wanted, row, for_e, message, started, out):
+    del started
     c = lax.axis_index("gy")
     choose(M, lax.rem(c, 2), lax.rem(c, 4), wanted[...], row, for_e, message, out)
 
@@ -381,18 +383,18 @@
         choose_first_kernel, (mine, row_a, for_e_a, message_a, halo_o), [six, ((PAD, B), F32)])
     arrived_a = lax.ppermute(chosen_a, "gy", across)
 
+    row_m, for_e_m, message_m = call(
+        second_kernel, (own, a, sides, message_a, halo_o, chosen_a), [pair, give, ((10 * B, B), BF16)], cost=0)
+    message_m = lax.ppermute(message_m, "gy", inside)
     row_f, for_e_f, for_o_f = call(
-        far_kernel, (own, a, sides, from_east, from_west, chosen_a), [pair, give, four], cost=0)
+        far_kernel, (own, a, sides, from_west, from_east, row_m), [pair, give, four], cost=20000000000)
     from_group = lax.ppermute(for_o_f, "gy", between)
 
-    row_m, for_e_m, message_m = call(
-        second_kernel, (own, a, sides, message_a, halo_o, row_f), [pair, give, ((10 * B, B), BF16)], cost=0)
-    message_m = lax.all_gather(message_m, "gy", axis_index_groups=cores)
-    (chosen_m,) = call(choose_second_kernel, (wanted, row_m, for_e_m, message_m), [six])
+    (chosen_m,) = call(choose_second_kernel, (wanted, row_m, for_e_m, message_m, row_f), [six])
     arrived_m = lax.ppermute(chosen_m, "gy", across)
 
     row_f, message_f = call(
-        merge_kernel, (row_f, for_e_f, for_o_f, from_group, arrived_a), [pair, ((14 * B, B), BF16)])
+        merge_kernel, (row_f, for_e_f, for_o_f, from_group, arrived_a, chosen_m), [pair, ((14 * B, B), BF16)])
     message_f = lax.all_gather(message_f, "gy", axis_index_groups=cores)
     (chosen_f,) = call(choose_far_kernel, (wanted, row_f, for_e_f, message_f), [six])
     arrived_f = lax.ppermute(chosen_f, "gy", across)

time: 48.7 us -> 47.6 us (0.977)
  the two profiles are of different devices: /device:TPU:1 before, /device:TPU:8 now
where the time goes in v9:
time: 47.6 us; the launch traced here: 47.3 us
  starting transfers between devices  30.4 us (64%)
  Pallas kernels  6.42 us (13%)
  blocking collectives  5.87 us (12%)
  waiting for transfers between devices  4.48 us (9%)
    ppermute x1, starting transfers between devices, on_device(): from_east = lax.ppermute(west, 'gx', westward)  12.8 us
    pallas_call x10, Pallas kernels, call(): pl.pallas_call(kernel, in_specs=in_specs or [VMEM] * len(args), out_specs...  6.42 us
    ppermute x1, starting transfers between devices, on_device(): arrived_f = lax.ppermute(chosen_f, 'gy', across)  4.79 us
    ppermute x1, waiting for transfers between devices, on_device(): arrived_f = lax.ppermute(chosen_f, 'gy', across)  4.42 us
    ppermute x1, starting transfers between devices, on_device(): arrived_m = lax.ppermute(chosen_m, 'gy', across)  3.92 us
    ppermute x1, starting transfers between devices, on_device(): from_west = lax.ppermute(east, 'gx', eastward)  3.48 us
    all_gather x1, blocking collectives, on_device(): message_f = lax.all_gather(message_f, 'gy', axis_index_groups=cores)  3.39 us
    all_gather x1, blocking collectives, on_device(): message_a = lax.all_gather(message_a, 'gy', axis_index_groups=cores)  2.47 us
  transfers between devices with their start and end apart: 8, of which 2 were waited for; matrix products, arithmetic and copies ran while one was open for 0% of the time, Pallas kernels for 8%

profile of v9, /device:TPU:8, one launch (start us, length us, event | category | flops | bytes accessed | tf_op | source)
XLA Modules:
  0.0 47.3 jit_solution(7254726903461495543)
XLA Ops:
  0.0 1.7 %shard_map.64 = (bf16[2,4,128,128]{3,2,1,0:T(8,128)(2,1)S(1)}, bf16[2,4,5,128,128]{4,3,2,1,0:T(8,128)(2,1)S(1)}, bf16[2,2,128,128]{3,2,1,0:T(8,128)(2,1)S(1)}, b...) custom-call(s32[2,4,4]{2,1,0:T(4,128)} %a_links.1, ...), custom_call_target="tpu_custom_call" | custom-call | tf_op jit(solution)/shard_map/pallas_call | solution.py:22
  1.7 0.7 %collective-permute-start.2 = (bf16[1808,128]{1,0:T(8,128)(2,1)S(1)}, bf16[1808,128]{1,0:T(8,128)(2,1)S(1)}, u32[]{:S(2)}, u32[]{:S(2)}) collective-permute-start(bf16[1808,128]{1,0:T(8,128)(2,1)S(1)} %get-tuple-element.31), channel_id=1, source_target_pairs={{1,2},{3,4},{5,6},{7,8},{9,10},{11,12},{13,14},{15,16},{17,18},{19... | collective-permute-start | bytes 1388552 | tf_op jit(solution)/shard_map/ppermute | solution.py:377
  2.4 3.5 %collective-permute-start = (bf16[6,128,128]{2,1,0:T(8,128)(2,1)S(1)}, bf16[6,128,128]{2,1,0:T(8,128)(2,1)S(1)}, u32[]{:S(2)}, u32[]{:S(2)}) collective-permute-start(bf16[6,128,128]{2,1,0:T(8,128)(2,1)S(1)} %get-tuple-element.29), channel_id=1, source_target_pairs={{0,64},{64,128},{128,192},{192,256},{256,320},{320,384},{384,448},... | collective-permute-start | bytes 589832 | tf_op jit(solution)/shard_map/ppermute | solution.py:376
  5.9 12.8 %collective-permute-start.1 = (bf16[6,128,128]{2,1,0:T(8,128)(2,1)S(1)}, bf16[6,128,128]{2,1,0:T(8,128)(2,1)S(1)}, u32[]{:S(2)}, u32[]{:S(2)}) collective-permute-start(bf16[6,128,128]{2,1,0:T(8,128)(2,1)S(1)} %get-tuple-element.30), channel_id=1, source_target_pairs={{64,0},{128,64},{192,128},{256,192},{320,256},{384,320},{448,384},... | collective-permute-start | bytes 589832 | tf_op jit(solution)/shard_map/ppermute | solution.py:375
  18.7 0.0 collective-permute-done.2.halo_o
  18.7 0.7 %shard_map.65 = (f32[2,3,128,128]{3,2,1,0:T(8,128)S(1)}, f32[2,2,128,128]{3,2,1,0:T(8,128)S(1)}, bf16[1824,128]{1,0:T(8,128)(2,1)S(1)}) custom-call(bf16[2,4,128,128]{3,2,1,0:T(8,128)(2,1)S(1)} %get-tuple-element.26.own, bf16[2,4,5,128,128]{4,3,2,1,0:T(8,128)(2,1)S(1)} %get-tuple-element.27.a, bf16[2,2,128,128]{3,2,1,0:T(8,128)(2,1)S(1)} %get-tuple-element.28.sides, ...), custom_call_target="tpu_custom_call" | custom-call | tf_op jit(solution)/shard_map/pallas_call | solution.py:22
  19.5 2.5 %all-gather = bf16[3648,128]{1,0:T(8,128)(2,1)S(1)} all-gather(bf16[1824,128]{1,0:T(8,128)(2,1)S(1)} %get-tuple-element.32), channel_id=2, replica_groups={{0,1},{2,3},{4,5},{6,7},{8,9},{10,11},{12,13},{14,15},{16,17},{18,19},{..., dimensions={0}, use_global_device_ids=true | all-gather | bytes 1400832 | tf_op jit(solution)/shard_map/all_gather | solution.py:381
  21.9 0.1 shard_map.66
  22.1 1.9 %collective-permute-start.4 = (bf16[6,128,128]{2,1,0:T(8,128)(2,1)S(1)}, bf16[6,128,128]{2,1,0:T(8,128)(2,1)S(1)}, u32[]{:S(2)}, u32[]{:S(2)}) collective-permute-start(bf16[6,128,128]{2,1,0:T(8,128)(2,1)S(1)} %get-tuple-element.35.started), channel_id=1, source_target_pairs={{0,2},{1,3},{2,0},{3,1},{4,6},{5,7},{6,4},{7,5},{8,10},{9,11},{10,... | collective-permute-start | bytes 589832 | tf_op jit(solution)/shard_map/ppermute | solution.py:384
  24.0 1.0 %shard_map.67 = (f32[2,3,128,128]{3,2,1,0:T(8,128)S(1)}, f32[2,2,128,128]{3,2,1,0:T(8,128)S(1)}, bf16[1280,128]{1,0:T(8,128)(2,1)S(1)}) custom-call(bf16[2,4,128,128]{3,2,1,0:T(8,128)(2,1)S(1)} %get-tuple-element.26.own, bf16[2,4,5,128,128]{4,3,2,1,0:T(8,128)(2,1)S(1)} %get-tuple-element.27.a, bf16[2,2,128,128]{3,2,1,0:T(8,128)(2,1)S(1)} %get-tuple-element.28.sides, ...), custom_call_target="tpu_custom_call" | custom-call | tf_op jit(solution)/shard_map/pallas_call | solution.py:22
  25.0 2.1 %collective-permute-start.5 = (bf16[1280,128]{1,0:T(8,128)(2,1)S(1)}, bf16[1280,128]{1,0:T(8,128)(2,1)S(1)}, u32[]{:S(2)}, u32[]{:S(2)}) collective-permute-start(bf16[1280,128]{1,0:T(8,128)(2,1)S(1)} %get-tuple-element.42), channel_id=1, source_target_pairs={{0,1},{2,3},{4,5},{6,7},{8,9},{10,11},{12,13},{14,15},{16,17},{18,... | collective-permute-start | bytes 983048 | tf_op jit(solution)/shard_map/ppermute | solution.py:388
  27.1 0.0 collective-permute-done.1.from_east
  27.1 0.7 %shard_map.68 = (f32[2,3,128,128]{3,2,1,0:T(8,128)S(1)}, f32[2,2,128,128]{3,2,1,0:T(8,128)S(1)}, bf16[4,128,128]{2,1,0:T(8,128)(2,1)S(1)}) custom-call(bf16[2,4,128,128]{3,2,1,0:T(8,128)(2,1)S(1)} %get-tuple-element.26.own, bf16[2,4,5,128,128]{4,3,2,1,0:T(8,128)(2,1)S(1)} %get-tuple-element.27.a, bf16[2,2,128,128]{3,2,1,0:T(8,128)(2,1)S(1)} %get-tuple-element.28.sides, ...), custom_call_target="tpu_custom_call" | custom-call | flops 20000000000 | bytes 20000000000 | tf_op jit(solution)/shard_map/pallas_call | solution.py:22
  27.8 0.7 %collective-permute-start.3 = (bf16[4,128,128]{2,1,0:T(8,128)(2,1)S(1)}, bf16[4,128,128]{2,1,0:T(8,128)(2,1)S(1)}, u32[]{:S(2)}, u32[]{:S(2)}) collective-permute-start(bf16[4,128,128]{2,1,0:T(8,128)(2,1)S(1)} %get-tuple-element.39.for_o), channel_id=1, source_target_pairs={{3,4},{7,8},{11,12},{15,16},{19,20},{23,24},{27,28},{31,32},{35,36... | collective-permute-start | bytes 393224 | tf_op jit(solution)/shard_map/ppermute | solution.py:391
  28.4 0.1 collective-permute-done.5.message.message_m
  28.5 0.1 shard_map.69.chosen
  28.6 3.9 %collective-permute-start.7 = (bf16[6,128,128]{2,1,0:T(8,128)(2,1)S(1)}, bf16[6,128,128]{2,1,0:T(8,128)(2,1)S(1)}, u32[]{:S(2)}, u32[]{:S(2)}) collective-permute-start(bf16[6,128,128]{2,1,0:T(8,128)(2,1)S(1)} %shard_map.69.chosen), channel_id=1, source_target_pairs={{0,2},{1,3},{2,0},{3,1},{4,6},{5,7},{6,4},{7,5},{8,10},{9,11},{10,... | collective-permute-start | bytes 589832 | tf_op jit(solution)/shard_map/ppermute | solution.py:394
  32.6 0.1 shard_map.70
  32.7 3.4 %all-gather.1 = bf16[3584,128]{1,0:T(8,128)(2,1)S(1)} all-gather(bf16[1792,128]{1,0:T(8,128)(2,1)S(1)} %get-tuple-element.44), channel_id=3, replica_groups={{0,1},{2,3},{4,5},{6,7},{8,9},{10,11},{12,13},{14,15},{16,17},{18,19},{..., dimensions={0}, use_global_device_ids=true | all-gather | bytes 1376256 | tf_op jit(solution)/shard_map/all_gather | solution.py:398
  36.1 0.1 shard_map.71
  36.2 4.8 %collective-permute-start.6 = (bf16[6,128,128]{2,1,0:T(8,128)(2,1)S(1)}, bf16[6,128,128]{2,1,0:T(8,128)(2,1)S(1)}, u32[]{:S(2)}, u32[]{:S(2)}) collective-permute-start(bf16[6,128,128]{2,1,0:T(8,128)(2,1)S(1)} %shard_map.71), channel_id=1, source_target_pairs={{0,2},{1,3},{2,0},{3,1},{4,6},{5,7},{6,4},{7,5},{8,10},{9,11},{10,... | collective-permute-start | bytes 589832 | tf_op jit(solution)/shard_map/ppermute | solution.py:400
  41.0 1.0 %shard_map.72.started = f32[2,1,3,3,128,128]{5,4,3,2,1,0:T(8,128)} custom-call(f32[16,128]{1,0:T(8,128)S(1)} %get-tuple-element.25.mine, f32[2,3,128,128]{3,2,1,0:T(8,128)S(1)} %get-tuple-element.33.row.row_a, f32[2,2,128,128]{3,2,1,0:T(8,128)S(1)} %get-tuple-element.34.for_e.for_e_a, bf16[2,1824,128]{2,1,0:T(8,128)(2,1)S(1)} %bitcast.5, ...), custom_call_target="tpu_custom_call" | custom-call | tf_op jit(solution)/shard_map/pallas_call | solution.py:22
  42.0 4.4 %collective-permute-done.6.arrived = bf16[6,128,128]{2,1,0:T(8,128)(2,1)S(1)} collective-permute-done((bf16[6,128,128]{2,1,0:T(8,128)(2,1)S(1)}, bf16[6,128,128]{2,1,0:T(8,128)(2,1)S(1)}, u32[]{:S(2)}, u32[]{:S(2)}) %collective-permute-start.6) | collective-permute-done | bytes 196640 | tf_op jit(solution)/shard_map/ppermute | solution.py:400
  46.4 0.9 %shard_map.73 = f32[2,1,3,3,128,128]{5,4,3,2,1,0:T(8,128)} custom-call(f32[16,128]{1,0:T(8,128)S(1)} %get-tuple-element.25.mine, f32[2,3,128,128]{3,2,1,0:T(8,128)S(1)} %get-tuple-element.43.row, f32[2,2,128,128]{3,2,1,0:T(8,128)S(1)} %get-tuple-element.38.for_e, bf16[2,1792,128]{2,1,0:T(8,128)(2,1)S(1)} %bitcast.7, ...), custom_call_target="tpu_custom_call", output_to_operand_aliasing={{}: (5, {})} | custom-call | tf_op jit(solution)/shard_map/pallas_call | solution.py:22
  (4 shorter events, 0.0 us)
Async XLA Ops:
  1.7 17.0 %collective-permute-start.2 = (bf16[1808,128]{1,0:T(8,128)(2,1)S(1)}, bf16[1808,128]{1,0:T(8,128)(2,1)S(1)}, u32[]{:S(2)}, u32[]{:S(2)}) collective-permute-start(bf16[1808,128]{1,0:T(8,128)(2,1)S(1)} %get-tuple-element.31), channel_id=1, source_target_pairs={{1,2},{3,4},{5,6},{7,8},{9,10},{11,12},{13,14},{15,16},{17,18},{19... | collective-permute-start | bytes 1388552 | tf_op jit(solution)/shard_map/ppermute | solution.py:377
  2.4 24.7 %collective-permute-start = (bf16[6,128,128]{2,1,0:T(8,128)(2,1)S(1)}, bf16[6,128,128]{2,1,0:T(8,128)(2,1)S(1)}, u32[]{:S(2)}, u32[]{:S(2)}) collective-permute-start(bf16[6,128,128]{2,1,0:T(8,128)(2,1)S(1)} %get-tuple-element.29), channel_id=1, source_target_pairs={{0,64},{64,128},{128,192},{192,256},{256,320},{320,384},{384,448},... | collective-permute-start | bytes 589832 | tf_op jit(solution)/shard_map/ppermute | solution.py:376
  5.9 21.2 %collective-permute-start.1 = (bf16[6,128,128]{2,1,0:T(8,128)(2,1)S(1)}, bf16[6,128,128]{2,1,0:T(8,128)(2,1)S(1)}, u32[]{:S(2)}, u32[]{:S(2)}) collective-permute-start(bf16[6,128,128]{2,1,0:T(8,128)(2,1)S(1)} %get-tuple-element.30), channel_id=1, source_target_pairs={{64,0},{128,64},{192,128},{256,192},{320,256},{384,320},{448,384},... | collective-permute-start | bytes 589832 | tf_op jit(solution)/shard_map/ppermute | solution.py:375
  22.1 10.5 %collective-permute-start.4 = (bf16[6,128,128]{2,1,0:T(8,128)(2,1)S(1)}, bf16[6,128,128]{2,1,0:T(8,128)(2,1)S(1)}, u32[]{:S(2)}, u32[]{:S(2)}) collective-permute-start(bf16[6,128,128]{2,1,0:T(8,128)(2,1)S(1)} %get-tuple-element.35.started), channel_id=1, source_target_pairs={{0,2},{1,3},{2,0},{3,1},{4,6},{5,7},{6,4},{7,5},{8,10},{9,11},{10,... | collective-permute-start | bytes 589832 | tf_op jit(solution)/shard_map/ppermute | solution.py:384
  25.0 3.5 %collective-permute-start.5 = (bf16[1280,128]{1,0:T(8,128)(2,1)S(1)}, bf16[1280,128]{1,0:T(8,128)(2,1)S(1)}, u32[]{:S(2)}, u32[]{:S(2)}) collective-permute-start(bf16[1280,128]{1,0:T(8,128)(2,1)S(1)} %get-tuple-element.42), channel_id=1, source_target_pairs={{0,1},{2,3},{4,5},{6,7},{8,9},{10,11},{12,13},{14,15},{16,17},{18,... | collective-permute-start | bytes 983048 | tf_op jit(solution)/shard_map/ppermute | solution.py:388
  27.8 4.8 %collective-permute-start.3 = (bf16[4,128,128]{2,1,0:T(8,128)(2,1)S(1)}, bf16[4,128,128]{2,1,0:T(8,128)(2,1)S(1)}, u32[]{:S(2)}, u32[]{:S(2)}) collective-permute-start(bf16[4,128,128]{2,1,0:T(8,128)(2,1)S(1)} %get-tuple-element.39.for_o), channel_id=1, source_target_pairs={{3,4},{7,8},{11,12},{15,16},{19,20},{23,24},{27,28},{31,32},{35,36... | collective-permute-start | bytes 393224 | tf_op jit(solution)/shard_map/ppermute | solution.py:391
  28.6 12.4 %collective-permute-start.7 = (bf16[6,128,128]{2,1,0:T(8,128)(2,1)S(1)}, bf16[6,128,128]{2,1,0:T(8,128)(2,1)S(1)}, u32[]{:S(2)}, u32[]{:S(2)}) collective-permute-start(bf16[6,128,128]{2,1,0:T(8,128)(2,1)S(1)} %shard_map.69.chosen), channel_id=1, source_target_pairs={{0,2},{1,3},{2,0},{3,1},{4,6},{5,7},{6,4},{7,5},{8,10},{9,11},{10,... | collective-permute-start | bytes 589832 | tf_op jit(solution)/shard_map/ppermute | solution.py:394
  36.2 10.2 %collective-permute-start.6 = (bf16[6,128,128]{2,1,0:T(8,128)(2,1)S(1)}, bf16[6,128,128]{2,1,0:T(8,128)(2,1)S(1)}, u32[]{:S(2)}, u32[]{:S(2)}) collective-permute-start(bf16[6,128,128]{2,1,0:T(8,128)(2,1)S(1)} %shard_map.71), channel_id=1, source_target_pairs={{0,2},{1,3},{2,0},{3,1},{4,6},{5,7},{6,4},{7,5},{8,10},{9,11},{10,... | collective-permute-start | bytes 589832 | tf_op jit(solution)/shard_map/ppermute | solution.py:400

commit v10 on v7

--- a/solution.py
+++ b/solution.py
@@ -190,7 +190,25 @@
                 message[tile(5 * k + t)] = row[k, t].astype(BF16)
 
 
-def far_kernel(own, a, sides, from_west, from_east, row, for_e, for_o):
+def border_kernel(a, sides, from_west, from_east, out):
+    c = lax.axis_index("gy")
+    position = lax.rem(c, 4)
+
+    def fill(j, side):
+        for k, (u, d) in enumerate(FAR):
+            arrived = from_west if d == 0 else from_east
+            tiles = [arrived[4], arrived[0]] if j == 0 else [arrived[3], arrived[5]]
+            product = dot(a[u, j, LINK_TILE[d]], cat(tiles, 1)).astype(BF16)
+            result = dot_t(sides[u, side], product).astype(BF16)
+            for s in range(2):
+                out[2 * k + s] = result[:, s * B:(s + 1) * B]
+
+    pl.when(jnp.logical_and(position == 0, c > 0))(lambda: fill(0, 0))
+    pl.when(jnp.logical_and(position == 3, c < lax.axis_size("gy") - 1))(lambda: fill(3, 1))
+
+
+def far_kernel(own, a, sides, from_west, from_east, chosen, row, for_e, for_o):
+    del chosen
     even = lax.rem(lax.axis_index("gy"), 2) == 0
     for k, (u, d) in enumerate(FAR):
         arrived = from_west if d == 0 else from_east
@@ -256,8 +274,8 @@
             jnp.broadcast_to(code == other.astype(F32), (B, B)))
 
 
-def choose_near_kernel(mine, row, for_e, message, halo_e, halo_o, row_far, out, wanted):
-    del row_far
+def choose_near_kernel(mine, row, for_e, message, halo_e, halo_o, border, out, wanted):
+    del border
     c = lax.axis_index("gy")
     core, position = lax.rem(c, 2), lax.rem(c, 4)
     outer = jnp.logical_or(position == 0, position == 3)
@@ -353,14 +371,16 @@
         near_kernel, (own, a, sides, halo_e, halo_o),
         [((near, 3) + bb, F32), ((near, 2) + bb, F32), ((5 * near * B + PAD, B), BF16)])
     message_n = lax.ppermute(message_n, "gy", inside)
-    row_f, for_e_f, for_o_f = call(
-        far_kernel, (own, a, sides, from_west, from_east),
-        [((far, 3) + bb, F32), ((far, 2) + bb, F32), ((2 * far,) + bb, BF16)], cost=20000000000)
+    (for_group,) = call(
+        border_kernel, (a, sides, from_west, from_east), [((2 * far,) + bb, BF16)], cost=20000000000)
+    from_group = lax.ppermute(for_group, "gy", between)
     chosen_n, wanted = call(
-        choose_near_kernel, (mine, row_n, for_e_n, message_n, halo_e, halo_o, row_f),
+        choose_near_kernel, (mine, row_n, for_e_n, message_n, halo_e, halo_o, for_group),
         [((3 * near,) + bb, BF16), ((PAD, B), F32)])
     arrived_n = lax.ppermute(chosen_n, "gy", across)
-    from_group = lax.ppermute(for_o_f, "gy", between)
+    row_f, for_e_f, for_o_f = call(
+        far_kernel, (own, a, sides, from_west, from_east, chosen_n),
+        [((far, 3) + bb, F32), ((far, 2) + bb, F32), ((2 * far,) + bb, BF16)], cost=0)
     row_f, message_f = call(
         merge_kernel, (row_f, for_e_f, for_o_f, from_group, chosen_n), [((far, 3) + bb, F32), ((7 * far * B, B), BF16)])
     message_f = lax.all_gather(message_f, "gy", axis_index_groups=cores)

time: 44.6 us -> 44.6 us (level)
    ppermute x1, waiting for transfers between devices: 5.28 us -> 4.56 us  [on_device(): arrived_n = lax.ppermute(chosen_n, 'gy', across)]
    ppermute x1, waiting for transfers between devices: 0.52 us -> 1.19 us  [on_device(): message_n = lax.ppermute(message_n, 'gy', inside)]
    pallas_call x8 -> x9, Pallas kernels: 5.92 us -> 5.92 us  [call(): pl.pallas_call(kernel, in_specs=in_specs or [VMEM] * len(args), out_specs...]
where the time goes in v10:
time: 44.6 us; the launch traced here: 44.3 us
  starting transfers between devices  25.6 us (57%)
  waiting for transfers between devices  8.23 us (18%)
  Pallas kernels  5.92 us (13%)
  blocking collectives  4.46 us (10%)
    ppermute x1, starting transfers between devices, on_device(): from_east = lax.ppermute(west, 'gx', westward)  12.8 us
    pallas_call x9, Pallas kernels, call(): pl.pallas_call(kernel, in_specs=in_specs or [VMEM] * len(args), out_specs...  5.92 us
    ppermute x1, waiting for transfers between devices, on_device(): arrived_n = lax.ppermute(chosen_n, 'gy', across)  4.56 us
    ppermute x1, starting transfers between devices, on_device(): arrived_f = lax.ppermute(chosen_f, 'gy', across)  3.92 us
    ppermute x1, starting transfers between devices, on_device(): from_west = lax.ppermute(east, 'gx', eastward)  3.48 us
    all_gather x1, blocking collectives, on_device(): message_f = lax.all_gather(message_f, 'gy', axis_index_groups=cores)  2.46 us
    ppermute x1, waiting for transfers between devices, on_device(): arrived_f = lax.ppermute(chosen_f, 'gy', across)  2.46 us
    ppermute x1, starting transfers between devices, on_device(): message_n = lax.ppermute(message_n, 'gy', inside)  2.07 us
  transfers between devices with their start and end apart: 7, of which 3 were waited for; matrix products, arithmetic and copies ran while one was open for 0% of the time, Pallas kernels for 8%

profile of v10, /device:TPU:8, one launch (start us, length us, event | category | flops | bytes accessed | tf_op | source)
XLA Modules:
  0.0 44.3 jit_solution(6382065832033410950)
XLA Ops:
  0.0 1.7 %shard_map.64 = (bf16[2,4,128,128]{3,2,1,0:T(8,128)(2,1)S(1)}, bf16[2,4,5,128,128]{4,3,2,1,0:T(8,128)(2,1)S(1)}, bf16[2,2,128,128]{3,2,1,0:T(8,128)(2,1)S(1)}, b...) custom-call(s32[2,4,4]{2,1,0:T(4,128)} %a_links.1, ...), custom_call_target="tpu_custom_call" | custom-call | tf_op jit(solution)/shard_map/pallas_call | solution.py:21
  1.7 0.7 %collective-permute-start.2 = (bf16[1808,128]{1,0:T(8,128)(2,1)S(1)}, bf16[1808,128]{1,0:T(8,128)(2,1)S(1)}, u32[]{:S(2)}, u32[]{:S(2)}) collective-permute-start(bf16[1808,128]{1,0:T(8,128)(2,1)S(1)} %get-tuple-element.30), channel_id=1, source_target_pairs={{1,2},{3,4},{5,6},{7,8},{9,10},{11,12},{13,14},{15,16},{17,18},{19... | collective-permute-start | bytes 1388552 | tf_op jit(solution)/shard_map/ppermute | solution.py:366
  2.4 3.5 %collective-permute-start = (bf16[6,128,128]{2,1,0:T(8,128)(2,1)S(1)}, bf16[6,128,128]{2,1,0:T(8,128)(2,1)S(1)}, u32[]{:S(2)}, u32[]{:S(2)}) collective-permute-start(bf16[6,128,128]{2,1,0:T(8,128)(2,1)S(1)} %get-tuple-element.27), channel_id=1, source_target_pairs={{0,64},{64,128},{128,192},{192,256},{256,320},{320,384},{384,448},... | collective-permute-start | bytes 589832 | tf_op jit(solution)/shard_map/ppermute | solution.py:367
  5.9 12.8 %collective-permute-start.1 = (bf16[6,128,128]{2,1,0:T(8,128)(2,1)S(1)}, bf16[6,128,128]{2,1,0:T(8,128)(2,1)S(1)}, u32[]{:S(2)}, u32[]{:S(2)}) collective-permute-start(bf16[6,128,128]{2,1,0:T(8,128)(2,1)S(1)} %get-tuple-element.28), channel_id=1, source_target_pairs={{64,0},{128,64},{192,128},{256,192},{320,256},{384,320},{448,384},... | collective-permute-start | bytes 589832 | tf_op jit(solution)/shard_map/ppermute | solution.py:368
  18.7 2.0 %all-gather = bf16[1056,128]{1,0:T(8,128)(2,1)S(1)} all-gather(bf16[528,128]{1,0:T(8,128)(2,1)S(1)} %get-tuple-element.29), channel_id=2, replica_groups={{0,1},{2,3},{4,5},{6,7},{8,9},{10,11},{12,13},{14,15},{16,17},{18,19},{..., dimensions={0}, use_global_device_ids=true | all-gather | bytes 405504 | tf_op jit(solution)/shard_map/all_gather | solution.py:369
  20.7 0.0 collective-permute-done.2.halo_o
  20.7 1.2 %shard_map.65 = (f32[4,3,128,128]{3,2,1,0:T(8,128)S(1)}, f32[4,2,128,128]{3,2,1,0:T(8,128)S(1)}, bf16[2576,128]{1,0:T(8,128)(2,1)S(1)}) custom-call(bf16[2,4,128,128]{3,2,1,0:T(8,128)(2,1)S(1)} %get-tuple-element.24.own, bf16[2,4,5,128,128]{4,3,2,1,0:T(8,128)(2,1)S(1)} %get-tuple-element.25.a, bf16[2,2,128,128]{3,2,1,0:T(8,128)(2,1)S(1)} %get-tuple-element.26.sides, ...), custom_call_target="tpu_custom_call" | custom-call | tf_op jit(solution)/shard_map/pallas_call | solution.py:21
  21.9 2.1 %collective-permute-start.3 = (bf16[2576,128]{1,0:T(8,128)(2,1)S(1)}, bf16[2576,128]{1,0:T(8,128)(2,1)S(1)}, u32[]{:S(2)}, u32[]{:S(2)}) collective-permute-start(bf16[2576,128]{1,0:T(8,128)(2,1)S(1)} %get-tuple-element.33), channel_id=1, source_target_pairs={{0,1},{2,3},{4,5},{6,7},{8,9},{10,11},{12,13},{14,15},{16,17},{18,... | collective-permute-start | bytes 1978376 | tf_op jit(solution)/shard_map/ppermute | solution.py:373
  24.0 0.0 collective-permute-done.from_west
  24.0 0.0 collective-permute-done.1.from_east
  24.1 0.7 %collective-permute-start.4 = (bf16[4,128,128]{2,1,0:T(8,128)(2,1)S(1)}, bf16[4,128,128]{2,1,0:T(8,128)(2,1)S(1)}, u32[]{:S(2)}, u32[]{:S(2)}) collective-permute-start(bf16[4,128,128]{2,1,0:T(8,128)(2,1)S(1)} %shard_map.66.border), channel_id=1, source_target_pairs={{3,4},{7,8},{11,12},{15,16},{19,20},{23,24},{27,28},{31,32},{35,36... | collective-permute-start | bytes 393224 | tf_op jit(solution)/shard_map/ppermute | solution.py:376
  24.7 1.2 %collective-permute-done.3.message = bf16[2576,128]{1,0:T(8,128)(2,1)S(1)} collective-permute-done((bf16[2576,128]{1,0:T(8,128)(2,1)S(1)}, bf16[2576,128]{1,0:T(8,128)(2,1)S(1)}, u32[]{:S(2)}, u32[]{:S(2)}) %collective-permute-start.3) | collective-permute-done | bytes 659488 | tf_op jit(solution)/shard_map/ppermute | solution.py:373
  25.9 0.2 shard_map.67
  26.1 1.9 %collective-permute-start.6 = (bf16[12,128,128]{2,1,0:T(8,128)(2,1)S(1)}, bf16[12,128,128]{2,1,0:T(8,128)(2,1)S(1)}, u32[]{:S(2)}, u32[]{:S(2)}) collective-permute-start(bf16[12,128,128]{2,1,0:T(8,128)(2,1)S(1)} %get-tuple-element.34.chosen), channel_id=1, source_target_pairs={{0,2},{1,3},{2,0},{3,1},{4,6},{5,7},{6,4},{7,5},{8,10},{9,11},{10,... | collective-permute-start | bytes 1179656 | tf_op jit(solution)/shard_map/ppermute | solution.py:380
  28.1 0.7 %shard_map.68 = (f32[2,3,128,128]{3,2,1,0:T(8,128)S(1)}, f32[2,2,128,128]{3,2,1,0:T(8,128)S(1)}, bf16[4,128,128]{2,1,0:T(8,128)(2,1)S(1)}) custom-call(bf16[2,4,128,128]{3,2,1,0:T(8,128)(2,1)S(1)} %get-tuple-element.24.own, bf16[2,4,5,128,128]{4,3,2,1,0:T(8,128)(2,1)S(1)} %get-tuple-element.25.a, bf16[2,2,128,128]{3,2,1,0:T(8,128)(2,1)S(1)} %get-tuple-element.26.sides, ...), custom_call_target="tpu_custom_call" | custom-call | tf_op jit(solution)/shard_map/pallas_call | solution.py:21
  28.8 0.0 collective-permute-done.4.from_group
  28.8 0.1 shard_map.69
  28.9 2.5 %all-gather.1 = bf16[3584,128]{1,0:T(8,128)(2,1)S(1)} all-gather(bf16[1792,128]{1,0:T(8,128)(2,1)S(1)} %get-tuple-element.39), channel_id=3, replica_groups={{0,1},{2,3},{4,5},{6,7},{8,9},{10,11},{12,13},{14,15},{16,17},{18,19},{..., dimensions={0}, use_global_device_ids=true | all-gather | bytes 1376256 | tf_op jit(solution)/shard_map/all_gather | solution.py:386
  31.4 0.1 shard_map.70
  31.5 3.9 %collective-permute-start.5 = (bf16[6,128,128]{2,1,0:T(8,128)(2,1)S(1)}, bf16[6,128,128]{2,1,0:T(8,128)(2,1)S(1)}, u32[]{:S(2)}, u32[]{:S(2)}) collective-permute-start(bf16[6,128,128]{2,1,0:T(8,128)(2,1)S(1)} %shard_map.70), channel_id=1, source_target_pairs={{0,2},{1,3},{2,0},{3,1},{4,6},{5,7},{6,4},{7,5},{8,10},{9,11},{10,... | collective-permute-start | bytes 589832 | tf_op jit(solution)/shard_map/ppermute | solution.py:388
  35.4 4.6 %collective-permute-done.6.arrived = bf16[12,128,128]{2,1,0:T(8,128)(2,1)S(1)} collective-permute-done((bf16[12,128,128]{2,1,0:T(8,128)(2,1)S(1)}, bf16[12,128,128]{2,1,0:T(8,128)(2,1)S(1)}, u32[]{:S(2)}, u32[]{:S(2)}) %collective-permute-start.6) | collective-permute-done | bytes 393248 | tf_op jit(solution)/shard_map/ppermute | solution.py:380
  40.0 1.0 %shard_map.71.started = f32[2,1,3,3,128,128]{5,4,3,2,1,0:T(8,128)} custom-call(f32[16,128]{1,0:T(8,128)S(1)} %get-tuple-element.23.mine, f32[4,3,128,128]{3,2,1,0:T(8,128)S(1)} %get-tuple-element.31.row, f32[4,2,128,128]{3,2,1,0:T(8,128)S(1)} %get-tuple-element.32.for_e, bf16[2576,128]{1,0:T(8,128)(2,1)S(1)} %collective-permute-done.3.message, ...), custom_call_target="tpu_custom_call" | custom-call | tf_op jit(solution)/shard_map/pallas_call | solution.py:21
  41.0 2.5 %collective-permute-done.5.arrived = bf16[6,128,128]{2,1,0:T(8,128)(2,1)S(1)} collective-permute-done((bf16[6,128,128]{2,1,0:T(8,128)(2,1)S(1)}, bf16[6,128,128]{2,1,0:T(8,128)(2,1)S(1)}, u32[]{:S(2)}, u32[]{:S(2)}) %collective-permute-start.5) | collective-permute-done | bytes 196640 | tf_op jit(solution)/shard_map/ppermute | solution.py:388
  43.4 0.9 %shard_map.72 = f32[2,1,3,3,128,128]{5,4,3,2,1,0:T(8,128)} custom-call(f32[16,128]{1,0:T(8,128)S(1)} %get-tuple-element.23.mine, f32[2,3,128,128]{3,2,1,0:T(8,128)S(1)} %get-tuple-element.38.row, f32[2,2,128,128]{3,2,1,0:T(8,128)S(1)} %get-tuple-element.36.for_e, bf16[2,1792,128]{2,1,0:T(8,128)(2,1)S(1)} %bitcast.4, ...), custom_call_target="tpu_custom_call", output_to_operand_aliasing={{}: (5, {})} | custom-call | tf_op jit(solution)/shard_map/pallas_call | solution.py:21
  (1 shorter events, 0.0 us)
Async XLA Ops:
  1.7 19.0 %collective-permute-start.2 = (bf16[1808,128]{1,0:T(8,128)(2,1)S(1)}, bf16[1808,128]{1,0:T(8,128)(2,1)S(1)}, u32[]{:S(2)}, u32[]{:S(2)}) collective-permute-start(bf16[1808,128]{1,0:T(8,128)(2,1)S(1)} %get-tuple-element.30), channel_id=1, source_target_pairs={{1,2},{3,4},{5,6},{7,8},{9,10},{11,12},{13,14},{15,16},{17,18},{19... | collective-permute-start | bytes 1388552 | tf_op jit(solution)/shard_map/ppermute | solution.py:366
  2.4 21.6 %collective-permute-start = (bf16[6,128,128]{2,1,0:T(8,128)(2,1)S(1)}, bf16[6,128,128]{2,1,0:T(8,128)(2,1)S(1)}, u32[]{:S(2)}, u32[]{:S(2)}) collective-permute-start(bf16[6,128,128]{2,1,0:T(8,128)(2,1)S(1)} %get-tuple-element.27), channel_id=1, source_target_pairs={{0,64},{64,128},{128,192},{192,256},{256,320},{320,384},{384,448},... | collective-permute-start | bytes 589832 | tf_op jit(solution)/shard_map/ppermute | solution.py:367
  5.9 18.1 %collective-permute-start.1 = (bf16[6,128,128]{2,1,0:T(8,128)(2,1)S(1)}, bf16[6,128,128]{2,1,0:T(8,128)(2,1)S(1)}, u32[]{:S(2)}, u32[]{:S(2)}) collective-permute-start(bf16[6,128,128]{2,1,0:T(8,128)(2,1)S(1)} %get-tuple-element.28), channel_id=1, source_target_pairs={{64,0},{128,64},{192,128},{256,192},{320,256},{384,320},{448,384},... | collective-permute-start | bytes 589832 | tf_op jit(solution)/shard_map/ppermute | solution.py:368
  21.9 4.0 %collective-permute-start.3 = (bf16[2576,128]{1,0:T(8,128)(2,1)S(1)}, bf16[2576,128]{1,0:T(8,128)(2,1)S(1)}, u32[]{:S(2)}, u32[]{:S(2)}) collective-permute-start(bf16[2576,128]{1,0:T(8,128)(2,1)S(1)} %get-tuple-element.33), channel_id=1, source_target_pairs={{0,1},{2,3},{4,5},{6,7},{8,9},{10,11},{12,13},{14,15},{16,17},{18,... | collective-permute-start | bytes 1978376 | tf_op jit(solution)/shard_map/ppermute | solution.py:373
  24.1 4.7 %collective-permute-start.4 = (bf16[4,128,128]{2,1,0:T(8,128)(2,1)S(1)}, bf16[4,128,128]{2,1,0:T(8,128)(2,1)S(1)}, u32[]{:S(2)}, u32[]{:S(2)}) collective-permute-start(bf16[4,128,128]{2,1,0:T(8,128)(2,1)S(1)} %shard_map.66.border), channel_id=1, source_target_pairs={{3,4},{7,8},{11,12},{15,16},{19,20},{23,24},{27,28},{31,32},{35,36... | collective-permute-start | bytes 393224 | tf_op jit(solution)/shard_map/ppermute | solution.py:376
  26.1 13.9 %collective-permute-start.6 = (bf16[12,128,128]{2,1,0:T(8,128)(2,1)S(1)}, bf16[12,128,128]{2,1,0:T(8,128)(2,1)S(1)}, u32[]{:S(2)}, u32[]{:S(2)}) collective-permute-start(bf16[12,128,128]{2,1,0:T(8,128)(2,1)S(1)} %get-tuple-element.34.chosen), channel_id=1, source_target_pairs={{0,2},{1,3},{2,0},{3,1},{4,6},{5,7},{6,4},{7,5},{8,10},{9,11},{10,... | collective-permute-start | bytes 1179656 | tf_op jit(solution)/shard_map/ppermute | solution.py:380
  31.5 11.9 %collective-permute-start.5 = (bf16[6,128,128]{2,1,0:T(8,128)(2,1)S(1)}, bf16[6,128,128]{2,1,0:T(8,128)(2,1)S(1)}, u32[]{:S(2)}, u32[]{:S(2)}) collective-permute-start(bf16[6,128,128]{2,1,0:T(8,128)(2,1)S(1)} %shard_map.70), channel_id=1, source_target_pairs={{0,2},{1,3},{2,0},{3,1},{4,6},{5,7},{6,4},{7,5},{8,10},{9,11},{10,... | collective-permute-start | bytes 589832 | tf_op jit(solution)/shard_map/ppermute | solution.py:388

commit v11 on v10

--- a/solution.py
+++ b/solution.py
@@ -47,7 +47,7 @@
 
 
 def begin_kernel(a_links, p_links, picks, own_in, side_in, a_in,
-                 own, a, sides, east, west, msg_o, msg_e, mine,
+                 own, a, sides, east, west, msg_o, mine,
                  s_links, s_side, s_picks, raw, sems):
     copies = [
         pltpu.make_async_copy(src, dst, sems.at[i])
@@ -76,17 +76,11 @@
     codes = jnp.where(rows < PAD // 2, s_picks[0, 0], s_picks[0, 1]).astype(F32)
     mine[...] = codes
     msg_o[pl.ds(14 * B, PAD)] = codes.astype(BF16)
-    msg_e[pl.ds(4 * B, PAD)] = codes.astype(BF16)
     copies[5].wait()
     for u in range(2):
         for j in range(4):
             for k in range(4):
                 a[u, j, k + 1] = a[u, j, k + 1] * s_links[u, j, k].astype(F32).astype(BF16)
-
-    def fill_e(j, k):
-        for u in range(2):
-            msg_e[tile(2 * u)] = own[u, j]
-            msg_e[tile(2 * u + 1)] = sides[u, k]
 
     def fill_o(j_o, k_o):
         for u in range(2):
@@ -112,8 +106,6 @@
             for i in range(5):
                 msg_o[tile(7 * u + 2 + i)] = result[:, i * B:(i + 1) * B]
 
-    pl.when(core == 0)(lambda: fill_e(3, 1))
-    pl.when(core == 1)(lambda: fill_e(0, 0))
     pl.when(jnp.logical_and(core == 0, keep[0]))(lambda: fill_o(0, 0))
     pl.when(jnp.logical_and(core == 1, keep[1]))(lambda: fill_o(3, 1))
 
@@ -135,20 +127,27 @@
     return first[:, :B], [first[:, B:], inner[0], inner[1], last[:, :B]], last[:, B:]
 
 
-def near_kernel(own, a, sides, halo_e, halo_o, row, for_e, message):
+def near_kernel(own, a, sides, halo_o, mine, row, for_e, message):
     core = lax.rem(lax.axis_index("gy"), 2)
     even = core == 0
     zero = jnp.zeros((B, B), BF16)
-    message[pl.ds(20 * B, PAD)] = halo_o[pl.ds(14 * B, PAD)]
+    message[pl.ds(28 * B, PAD)] = halo_o[pl.ds(14 * B, PAD)]
+    message[pl.ds(28 * B + PAD, PAD)] = mine[...].astype(BF16)
     for u in range(2):
         def edge(k):
-            from_e, from_o = halo_e[1 - core, tile(2 * u + k)], halo_o[tile(7 * u + k)]
-            return jnp.where(even, from_o, from_e), jnp.where(even, from_e, from_o)
+            from_o = halo_o[tile(7 * u + k)]
+            return jnp.where(even, from_o, zero), jnp.where(even, zero, from_o)
 
         own_down, own_up = edge(0)
         high_down, low_up = edge(1)
         low, high = sides[u, 0], sides[u, 1]
         o = [own[u, j] for j in range(4)]
+        message[tile(20 + 4 * u)] = jnp.where(even, o[3], low)
+        message[tile(21 + 4 * u)] = jnp.where(even, high, o[0])
+        before = dot_t(jnp.where(even, cat([o[3], high], 1), cat([o[0], low], 1)),
+                       jnp.where(even, a[u, 3, 4], a[u, 0, 3]))
+        message[tile(22 + 4 * u)] = before[:B].astype(BF16)
+        message[tile(23 + 4 * u)] = before[B:].astype(BF16)
         right = [
             [[low, o[0]], [own_down, high_down], [zero, o[1]]],
             [[zero, o[1]], [low, o[0]], [zero, o[2]]],
@@ -253,18 +252,21 @@
     return mine, theirs, inner
 
 
-def complete(core, row, for_e, message, k, t):
+def complete(core, row, for_e, message, joint, k, t):
+    def to_mine(s):
+        value = message[tile(5 * k + 3 + s)].astype(F32)
+        return value + joint[k // 2, 0, s] if k % 2 else value
+
+    def to_theirs(s):
+        return for_e[k, s] + joint[k // 2, 1, s] if k % 2 else for_e[k, s]
+
     mine = row[k, t]
     theirs = message[tile(5 * k + t)].astype(F32)
     if t == 1:
-        mine = mine + message[tile(5 * k + 3 + core)].astype(F32)
-        theirs = theirs + for_e[k, 1 - core]
-    else:
-        gets = (core == 0) == (t == 2)
-        s = 1 if t == 2 else 0
-        mine = mine + jnp.where(gets, message[tile(5 * k + 3 + s)].astype(F32), 0.0)
-        theirs = theirs + jnp.where(gets, 0.0, for_e[k, s])
-    return mine, theirs
+        return mine + to_mine(core), theirs + to_theirs(1 - core)
+    gets = (core == 0) == (t == 2)
+    s = 1 if t == 2 else 0
+    return mine + jnp.where(gets, to_mine(s), 0.0), theirs + jnp.where(gets, 0.0, to_theirs(s))
 
 
 def masks(codes, u, position, core):
@@ -274,19 +276,29 @@
             jnp.broadcast_to(code == other.astype(F32), (B, B)))
 
 
-def choose_near_kernel(mine, row, for_e, message, halo_e, halo_o, border, out, wanted):
+def choose_near_kernel(mine, row, for_e, message, sent, halo_o, border, out, wanted, joint):
     del border
     c = lax.axis_index("gy")
     core, position = lax.rem(c, 2), lax.rem(c, 4)
     outer = jnp.logical_or(position == 0, position == 3)
-    inferred = 6.0 - mine[...] - halo_e[1 - core, pl.ds(4 * B, PAD)].astype(F32)
+    inferred = 6.0 - mine[...] - message[pl.ds(28 * B + PAD, PAD)].astype(F32)
     inferred = inferred - halo_o[pl.ds(14 * B, PAD)].astype(F32)
-    codes = jnp.where(outer, message[pl.ds(20 * B, PAD)].astype(F32), inferred)
+    codes = jnp.where(outer, message[pl.ds(28 * B, PAD)].astype(F32), inferred)
     wanted[...] = codes
+    for u in range(2):
+        def part(ref, i):
+            return ref[tile(20 + 4 * u + i)]
+
+        ours, got = cat([part(sent, 0), part(sent, 1)], 1), cat([part(message, 0), part(message, 1)], 1)
+        to_mine = dot(cat([part(sent, 2), part(message, 3)], 1), cat([got, ours], 0))
+        to_theirs = dot(cat([part(message, 2), part(sent, 3)], 1), cat([ours, got], 0))
+        for s in range(2):
+            joint[u, 0, s] = to_mine[:, s * B:(s + 1) * B]
+            joint[u, 1, s] = to_theirs[:, s * B:(s + 1) * B]
     for k, (u, _) in enumerate(NEAR):
         use_mine, use_theirs = masks(codes, u, position, core)
         for t in range(3):
-            own_row, other_row = complete(core, row, for_e, message, k, t)
+            own_row, other_row = complete(core, row, for_e, message, joint, k, t)
             out[3 * k + t] = jnp.where(use_mine, own_row, jnp.where(use_theirs, other_row, 0.0)).astype(BF16)
 
 
@@ -300,14 +312,14 @@
             out[3 * k + t] = jnp.where(use_mine, mine, jnp.where(use_theirs, theirs, inner)).astype(BF16)
 
 
-def finish_near_kernel(mine, row, for_e, message, arrived, out, buffer, sems):
+def finish_near_kernel(mine, row, for_e, message, joint, arrived, out, buffer, sems):
     c = lax.axis_index("gy")
     core, position = lax.rem(c, 2), lax.rem(c, 4)
     copies = []
     for k, (u, d) in enumerate(NEAR):
         use_mine, use_theirs = masks(mine[...], u, position, core)
         for t in range(3):
-            own_row, other_row = complete(core, row, for_e, message, k, t)
+            own_row, other_row = complete(core, row, for_e, message, joint, k, t)
             got = arrived[3 * k + t].astype(F32)
             buffer[k, t] = jnp.where(use_mine, own_row, jnp.where(use_theirs, other_row, got))
         copies.append(pltpu.make_async_copy(buffer.at[k], out.at[u, 0, d], sems.at[k]))
@@ -354,29 +366,29 @@
     bb = (B, B)
     near, far = len(NEAR), len(FAR)
 
-    own, a, sides, east, west, msg_o, msg_e, mine = call(
+    own, a, sides, east, west, msg_o, mine = call(
         begin_kernel,
         [pltpu.with_memory_space_constraint(x, pltpu.HBM)
          for x in (a_links, p_links, coarse_pick.T, p_own, p_side, a_tiles)],
         [(p_own.shape, BF16), (a_tiles.shape, BF16), ((2, 2) + bb, BF16), ((6,) + bb, BF16), ((6,) + bb, BF16),
-         ((14 * B + PAD, B), BF16), ((4 * B + PAD, B), BF16), ((PAD, B), F32)],
+         ((14 * B + PAD, B), BF16), ((PAD, B), F32)],
         in_specs=[HBM] * 6,
         scratch=[pltpu.SMEM(a_links.shape, jnp.int32), pltpu.SMEM(p_links.shape, jnp.int32),
                  pltpu.SMEM((1, 2), jnp.int32), pltpu.VMEM(p_side.shape, BF16), pltpu.SemaphoreType.DMA((6,))])
     halo_o = lax.ppermute(msg_o, "gy", outside)
     from_west = lax.ppermute(east, "gx", eastward)
     from_east = lax.ppermute(west, "gx", westward)
-    halo_e = lax.all_gather(msg_e, "gy", axis_index_groups=cores)
     row_n, for_e_n, message_n = call(
-        near_kernel, (own, a, sides, halo_e, halo_o),
-        [((near, 3) + bb, F32), ((near, 2) + bb, F32), ((5 * near * B + PAD, B), BF16)])
+        near_kernel, (own, a, sides, halo_o, mine),
+        [((near, 3) + bb, F32), ((near, 2) + bb, F32), ((28 * B + 2 * PAD, B), BF16)])
+    sent_n = message_n
     message_n = lax.ppermute(message_n, "gy", inside)
     (for_group,) = call(
         border_kernel, (a, sides, from_west, from_east), [((2 * far,) + bb, BF16)], cost=20000000000)
     from_group = lax.ppermute(for_group, "gy", between)
-    chosen_n, wanted = call(
-        choose_near_kernel, (mine, row_n, for_e_n, message_n, halo_e, halo_o, for_group),
-        [((3 * near,) + bb, BF16), ((PAD, B), F32)])
+    chosen_n, wanted, joint = call(
+        choose_near_kernel, (mine, row_n, for_e_n, message_n, sent_n, halo_o, for_group),
+        [((3 * near,) + bb, BF16), ((PAD, B), F32), ((2, 2, 2) + bb, F32)])
     arrived_n = lax.ppermute(chosen_n, "gy", across)
     row_f, for_e_f, for_o_f = call(
         far_kernel, (own, a, sides, from_west, from_east, chosen_n),
@@ -388,7 +400,7 @@
     arrived_f = lax.ppermute(chosen_f, "gy", across)
     shape = (2, 1, 3, 3) + bb
     (out,) = call(
-        finish_near_kernel, (mine, row_n, for_e_n, message_n, arrived_n), [(shape, F32)], out_specs=[HBM],
+        finish_near_kernel, (mine, row_n, for_e_n, message_n, joint, arrived_n), [(shape, F32)], out_specs=[HBM],
         scratch=[pltpu.VMEM((near, 3) + bb, F32), pltpu.SemaphoreType.DMA((near,))], cost=0)
     (out,) = call(
         finish_far_kernel, (mine, row_f, for_e_f, message_f, arrived_f, out), [(shape, F32)],

time: 44.6 us -> 43.2 us (0.969)
  blocking collectives: 4.46 us -> 2.46 us
  waiting for transfers between devices: 8.23 us -> 8.72 us
    all_gather x1 -> x0, blocking collectives: 2 us -> none  [on_device(): halo_e = lax.all_gather(msg_e, 'gy', axis_index_groups=cores)]
    ppermute x1, waiting for transfers between devices: 1.19 us -> 1.72 us  [on_device(): message_n = lax.ppermute(message_n, 'gy', inside)]
where the time goes in v11:
time: 43.2 us; the launch traced here: 43 us
  starting transfers between devices  25.4 us (59%)
  waiting for transfers between devices  8.72 us (20%)
  Pallas kernels  6.19 us (14%)
  blocking collectives  2.46 us (6%)
    ppermute x1, starting transfers between devices, on_device(): from_east = lax.ppermute(west, 'gx', westward)  12.8 us
    pallas_call x9, Pallas kernels, call(): pl.pallas_call(kernel, in_specs=in_specs or [VMEM] * len(args), out_specs...  6.19 us
    ppermute x1, waiting for transfers between devices, on_device(): arrived_n = lax.ppermute(chosen_n, 'gy', across)  4.58 us
    ppermute x1, starting transfers between devices, on_device(): arrived_f = lax.ppermute(chosen_f, 'gy', across)  3.92 us
    ppermute x1, starting transfers between devices, on_device(): from_west = lax.ppermute(east, 'gx', eastward)  3.48 us
    all_gather x1, blocking collectives, on_device(): message_f = lax.all_gather(message_f, 'gy', axis_index_groups=cores)  2.46 us
    ppermute x1, waiting for transfers between devices, on_device(): arrived_f = lax.ppermute(chosen_f, 'gy', across)  2.4 us
    ppermute x1, starting transfers between devices, on_device(): message_n = lax.ppermute(message_n, 'gy', inside)  1.92 us
  transfers between devices with their start and end apart: 7, of which 3 were waited for; matrix products, arithmetic and copies ran while one was open for 0% of the time, Pallas kernels for 8%

profile of v11, /device:TPU:8, one launch (start us, length us, event | category | flops | bytes accessed | tf_op | source)
XLA Modules:
  0.0 43.0 jit_solution(15207433094974333805)
XLA Ops:
  0.0 1.7 %shard_map.64 = (bf16[2,4,128,128]{3,2,1,0:T(8,128)(2,1)S(1)}, bf16[2,4,5,128,128]{4,3,2,1,0:T(8,128)(2,1)S(1)}, bf16[2,2,128,128]{3,2,1,0:T(8,128)(2,1)S(1)}, b...) custom-call(s32[2,4,4]{2,1,0:T(4,128)} %a_links.1, ...), custom_call_target="tpu_custom_call" | custom-call | tf_op jit(solution)/shard_map/pallas_call | solution.py:21
  1.7 0.7 %collective-permute-start.2 = (bf16[1808,128]{1,0:T(8,128)(2,1)S(1)}, bf16[1808,128]{1,0:T(8,128)(2,1)S(1)}, u32[]{:S(2)}, u32[]{:S(2)}) collective-permute-start(bf16[1808,128]{1,0:T(8,128)(2,1)S(1)} %get-tuple-element.29), channel_id=1, source_target_pairs={{1,2},{3,4},{5,6},{7,8},{9,10},{11,12},{13,14},{15,16},{17,18},{19... | collective-permute-start | bytes 1388552 | tf_op jit(solution)/shard_map/ppermute | solution.py:378
  2.4 3.5 %collective-permute-start = (bf16[6,128,128]{2,1,0:T(8,128)(2,1)S(1)}, bf16[6,128,128]{2,1,0:T(8,128)(2,1)S(1)}, u32[]{:S(2)}, u32[]{:S(2)}) collective-permute-start(bf16[6,128,128]{2,1,0:T(8,128)(2,1)S(1)} %get-tuple-element.27), channel_id=1, source_target_pairs={{0,64},{64,128},{128,192},{192,256},{256,320},{320,384},{384,448},... | collective-permute-start | bytes 589832 | tf_op jit(solution)/shard_map/ppermute | solution.py:379
  5.9 12.8 %collective-permute-start.1 = (bf16[6,128,128]{2,1,0:T(8,128)(2,1)S(1)}, bf16[6,128,128]{2,1,0:T(8,128)(2,1)S(1)}, u32[]{:S(2)}, u32[]{:S(2)}) collective-permute-start(bf16[6,128,128]{2,1,0:T(8,128)(2,1)S(1)} %get-tuple-element.28), channel_id=1, source_target_pairs={{64,0},{128,64},{192,128},{256,192},{320,256},{384,320},{448,384},... | collective-permute-start | bytes 589832 | tf_op jit(solution)/shard_map/ppermute | solution.py:380
  18.7 0.0 collective-permute-done.2.halo_o
  18.7 1.3 %shard_map.65 = (f32[4,3,128,128]{3,2,1,0:T(8,128)S(1)}, f32[4,2,128,128]{3,2,1,0:T(8,128)S(1)}, bf16[3616,128]{1,0:T(8,128)(2,1)S(1)}) custom-call(bf16[2,4,128,128]{3,2,1,0:T(8,128)(2,1)S(1)} %get-tuple-element.24.own, bf16[2,4,5,128,128]{4,3,2,1,0:T(8,128)(2,1)S(1)} %get-tuple-element.25.a, bf16[2,2,128,128]{3,2,1,0:T(8,128)(2,1)S(1)} %get-tuple-element.26.sides, ...), custom_call_target="tpu_custom_call" | custom-call | tf_op jit(solution)/shard_map/pallas_call | solution.py:21
  20.0 1.9 %collective-permute-start.3 = (bf16[3616,128]{1,0:T(8,128)(2,1)S(1)}, bf16[3616,128]{1,0:T(8,128)(2,1)S(1)}, u32[]{:S(2)}, u32[]{:S(2)}) collective-permute-start(bf16[3616,128]{1,0:T(8,128)(2,1)S(1)} %get-tuple-element.32.sent), channel_id=1, source_target_pairs={{0,1},{2,3},{4,5},{6,7},{8,9},{10,11},{12,13},{14,15},{16,17},{18,... | collective-permute-start | bytes 2777096 | tf_op jit(solution)/shard_map/ppermute | solution.py:385
  21.9 0.0 collective-permute-done.from_west
  21.9 0.0 collective-permute-done.1.from_east
  22.0 0.7 %collective-permute-start.4 = (bf16[4,128,128]{2,1,0:T(8,128)(2,1)S(1)}, bf16[4,128,128]{2,1,0:T(8,128)(2,1)S(1)}, u32[]{:S(2)}, u32[]{:S(2)}) collective-permute-start(bf16[4,128,128]{2,1,0:T(8,128)(2,1)S(1)} %shard_map.66.border), channel_id=1, source_target_pairs={{3,4},{7,8},{11,12},{15,16},{19,20},{23,24},{27,28},{31,32},{35,36... | collective-permute-start | bytes 393224 | tf_op jit(solution)/shard_map/ppermute | solution.py:388
  22.6 1.7 %collective-permute-done.3.message = bf16[3616,128]{1,0:T(8,128)(2,1)S(1)} collective-permute-done((bf16[3616,128]{1,0:T(8,128)(2,1)S(1)}, bf16[3616,128]{1,0:T(8,128)(2,1)S(1)}, u32[]{:S(2)}, u32[]{:S(2)}) %collective-permute-start.3) | collective-permute-done | bytes 925728 | tf_op jit(solution)/shard_map/ppermute | solution.py:385
  24.4 0.4 shard_map.67
  24.8 1.9 %collective-permute-start.6 = (bf16[12,128,128]{2,1,0:T(8,128)(2,1)S(1)}, bf16[12,128,128]{2,1,0:T(8,128)(2,1)S(1)}, u32[]{:S(2)}, u32[]{:S(2)}) collective-permute-start(bf16[12,128,128]{2,1,0:T(8,128)(2,1)S(1)} %get-tuple-element.33.chosen), channel_id=1, source_target_pairs={{0,2},{1,3},{2,0},{3,1},{4,6},{5,7},{6,4},{7,5},{8,10},{9,11},{10,... | collective-permute-start | bytes 1179656 | tf_op jit(solution)/shard_map/ppermute | solution.py:392
  26.7 0.7 %shard_map.68 = (f32[2,3,128,128]{3,2,1,0:T(8,128)S(1)}, f32[2,2,128,128]{3,2,1,0:T(8,128)S(1)}, bf16[4,128,128]{2,1,0:T(8,128)(2,1)S(1)}) custom-call(bf16[2,4,128,128]{3,2,1,0:T(8,128)(2,1)S(1)} %get-tuple-element.24.own, bf16[2,4,5,128,128]{4,3,2,1,0:T(8,128)(2,1)S(1)} %get-tuple-element.25.a, bf16[2,2,128,128]{3,2,1,0:T(8,128)(2,1)S(1)} %get-tuple-element.26.sides, ...), custom_call_target="tpu_custom_call" | custom-call | tf_op jit(solution)/shard_map/pallas_call | solution.py:21
  27.4 0.0 collective-permute-done.4.from_group
  27.5 0.1 shard_map.69
  27.6 2.5 %all-gather = bf16[3584,128]{1,0:T(8,128)(2,1)S(1)} all-gather(bf16[1792,128]{1,0:T(8,128)(2,1)S(1)} %get-tuple-element.38), channel_id=2, replica_groups={{0,1},{2,3},{4,5},{6,7},{8,9},{10,11},{12,13},{14,15},{16,17},{18,19},{..., dimensions={0}, use_global_device_ids=true | all-gather | bytes 1376256 | tf_op jit(solution)/shard_map/all_gather | solution.py:398
  30.0 0.1 shard_map.70
  30.1 3.9 %collective-permute-start.5 = (bf16[6,128,128]{2,1,0:T(8,128)(2,1)S(1)}, bf16[6,128,128]{2,1,0:T(8,128)(2,1)S(1)}, u32[]{:S(2)}, u32[]{:S(2)}) collective-permute-start(bf16[6,128,128]{2,1,0:T(8,128)(2,1)S(1)} %shard_map.70), channel_id=1, source_target_pairs={{0,2},{1,3},{2,0},{3,1},{4,6},{5,7},{6,4},{7,5},{8,10},{9,11},{10,... | collective-permute-start | bytes 589832 | tf_op jit(solution)/shard_map/ppermute | solution.py:400
  34.1 4.6 %collective-permute-done.6.arrived = bf16[12,128,128]{2,1,0:T(8,128)(2,1)S(1)} collective-permute-done((bf16[12,128,128]{2,1,0:T(8,128)(2,1)S(1)}, bf16[12,128,128]{2,1,0:T(8,128)(2,1)S(1)}, u32[]{:S(2)}, u32[]{:S(2)}) %collective-permute-start.6) | collective-permute-done | bytes 393248 | tf_op jit(solution)/shard_map/ppermute | solution.py:392
  38.7 1.0 %shard_map.71.started = f32[2,1,3,3,128,128]{5,4,3,2,1,0:T(8,128)} custom-call(f32[16,128]{1,0:T(8,128)S(1)} %get-tuple-element.23.mine, f32[4,3,128,128]{3,2,1,0:T(8,128)S(1)} %get-tuple-element.30.row, f32[4,2,128,128]{3,2,1,0:T(8,128)S(1)} %get-tuple-element.31.for_e, bf16[3616,128]{1,0:T(8,128)(2,1)S(1)} %collective-permute-done.3.message, ...), custom_call_target="tpu_custom_call" | custom-call | tf_op jit(solution)/shard_map/pallas_call | solution.py:21
  39.7 2.4 %collective-permute-done.5.arrived = bf16[6,128,128]{2,1,0:T(8,128)(2,1)S(1)} collective-permute-done((bf16[6,128,128]{2,1,0:T(8,128)(2,1)S(1)}, bf16[6,128,128]{2,1,0:T(8,128)(2,1)S(1)}, u32[]{:S(2)}, u32[]{:S(2)}) %collective-permute-start.5) | collective-permute-done | bytes 196640 | tf_op jit(solution)/shard_map/ppermute | solution.py:400
  42.1 0.9 %shard_map.72 = f32[2,1,3,3,128,128]{5,4,3,2,1,0:T(8,128)} custom-call(f32[16,128]{1,0:T(8,128)S(1)} %get-tuple-element.23.mine, f32[2,3,128,128]{3,2,1,0:T(8,128)S(1)} %get-tuple-element.37.row, f32[2,2,128,128]{3,2,1,0:T(8,128)S(1)} %get-tuple-element.35.for_e, bf16[2,1792,128]{2,1,0:T(8,128)(2,1)S(1)} %bitcast.3, ...), custom_call_target="tpu_custom_call", output_to_operand_aliasing={{}: (5, {})} | custom-call | tf_op jit(solution)/shard_map/pallas_call | solution.py:21
  (1 shorter events, 0.0 us)
Async XLA Ops:
  1.7 17.0 %collective-permute-start.2 = (bf16[1808,128]{1,0:T(8,128)(2,1)S(1)}, bf16[1808,128]{1,0:T(8,128)(2,1)S(1)}, u32[]{:S(2)}, u32[]{:S(2)}) collective-permute-start(bf16[1808,128]{1,0:T(8,128)(2,1)S(1)} %get-tuple-element.29), channel_id=1, source_target_pairs={{1,2},{3,4},{5,6},{7,8},{9,10},{11,12},{13,14},{15,16},{17,18},{19... | collective-permute-start | bytes 1388552 | tf_op jit(solution)/shard_map/ppermute | solution.py:378
  2.4 19.5 %collective-permute-start = (bf16[6,128,128]{2,1,0:T(8,128)(2,1)S(1)}, bf16[6,128,128]{2,1,0:T(8,128)(2,1)S(1)}, u32[]{:S(2)}, u32[]{:S(2)}) collective-permute-start(bf16[6,128,128]{2,1,0:T(8,128)(2,1)S(1)} %get-tuple-element.27), channel_id=1, source_target_pairs={{0,64},{64,128},{128,192},{192,256},{256,320},{320,384},{384,448},... | collective-permute-start | bytes 589832 | tf_op jit(solution)/shard_map/ppermute | solution.py:379
  5.9 16.1 %collective-permute-start.1 = (bf16[6,128,128]{2,1,0:T(8,128)(2,1)S(1)}, bf16[6,128,128]{2,1,0:T(8,128)(2,1)S(1)}, u32[]{:S(2)}, u32[]{:S(2)}) collective-permute-start(bf16[6,128,128]{2,1,0:T(8,128)(2,1)S(1)} %get-tuple-element.28), channel_id=1, source_target_pairs={{64,0},{128,64},{192,128},{256,192},{320,256},{384,320},{448,384},... | collective-permute-start | bytes 589832 | tf_op jit(solution)/shard_map/ppermute | solution.py:380
  20.0 4.4 %collective-permute-start.3 = (bf16[3616,128]{1,0:T(8,128)(2,1)S(1)}, bf16[3616,128]{1,0:T(8,128)(2,1)S(1)}, u32[]{:S(2)}, u32[]{:S(2)}) collective-permute-start(bf16[3616,128]{1,0:T(8,128)(2,1)S(1)} %get-tuple-element.32.sent), channel_id=1, source_target_pairs={{0,1},{2,3},{4,5},{6,7},{8,9},{10,11},{12,13},{14,15},{16,17},{18,... | collective-permute-start | bytes 2777096 | tf_op jit(solution)/shard_map/ppermute | solution.py:385
  22.0 5.5 %collective-permute-start.4 = (bf16[4,128,128]{2,1,0:T(8,128)(2,1)S(1)}, bf16[4,128,128]{2,1,0:T(8,128)(2,1)S(1)}, u32[]{:S(2)}, u32[]{:S(2)}) collective-permute-start(bf16[4,128,128]{2,1,0:T(8,128)(2,1)S(1)} %shard_map.66.border), channel_id=1, source_target_pairs={{3,4},{7,8},{11,12},{15,16},{19,20},{23,24},{27,28},{31,32},{35,36... | collective-permute-start | bytes 393224 | tf_op jit(solution)/shard_map/ppermute | solution.py:388
  24.8 13.9 %collective-permute-start.6 = (bf16[12,128,128]{2,1,0:T(8,128)(2,1)S(1)}, bf16[12,128,128]{2,1,0:T(8,128)(2,1)S(1)}, u32[]{:S(2)}, u32[]{:S(2)}) collective-permute-start(bf16[12,128,128]{2,1,0:T(8,128)(2,1)S(1)} %get-tuple-element.33.chosen), channel_id=1, source_target_pairs={{0,2},{1,3},{2,0},{3,1},{4,6},{5,7},{6,4},{7,5},{8,10},{9,11},{10,... | collective-permute-start | bytes 1179656 | tf_op jit(solution)/shard_map/ppermute | solution.py:392
  30.1 11.9 %collective-permute-start.5 = (bf16[6,128,128]{2,1,0:T(8,128)(2,1)S(1)}, bf16[6,128,128]{2,1,0:T(8,128)(2,1)S(1)}, u32[]{:S(2)}, u32[]{:S(2)}) collective-permute-start(bf16[6,128,128]{2,1,0:T(8,128)(2,1)S(1)} %shard_map.70), channel_id=1, source_target_pairs={{0,2},{1,3},{2,0},{3,1},{4,6},{5,7},{6,4},{7,5},{8,10},{9,11},{10,... | collective-permute-start | bytes 589832 | tf_op jit(solution)/shard_map/ppermute | solution.py:400

commit v12 on v11

--- a/solution.py
+++ b/solution.py
@@ -312,9 +312,11 @@
             out[3 * k + t] = jnp.where(use_mine, mine, jnp.where(use_theirs, theirs, inner)).astype(BF16)
 
 
-def finish_near_kernel(mine, row, for_e, message, joint, arrived, out, buffer, sems):
+def finish_near_kernel(mine, row, for_e, message, joint, arrived, row_far, for_e_far, message_far,
+                       out, base, buffer, sems):
     c = lax.axis_index("gy")
     core, position = lax.rem(c, 2), lax.rem(c, 4)
+    half = position // 2
     copies = []
     for k, (u, d) in enumerate(NEAR):
         use_mine, use_theirs = masks(mine[...], u, position, core)
@@ -324,27 +326,27 @@
             buffer[k, t] = jnp.where(use_mine, own_row, jnp.where(use_theirs, other_row, got))
         copies.append(pltpu.make_async_copy(buffer.at[k], out.at[u, 0, d], sems.at[k]))
         copies[-1].start()
+    for k, (u, _) in enumerate(FAR):
+        use_mine, use_theirs = masks(mine[...], u, position, core)
+        code = mine[u * PAD // 2:u * PAD // 2 + 1]
+        add_inner = jnp.broadcast_to(code == (2 - half).astype(F32), (B, B))
+        for t in range(3):
+            own_row, other_row, inner = far_tiles(core, half, row_far, for_e_far, message_far, k, t)
+            there = jnp.where(add_inner, inner, 0.0)
+            base[k, t] = jnp.where(use_mine, own_row, jnp.where(use_theirs, other_row, there))
     for copy in copies:
         copy.wait()
 
 
-def finish_far_kernel(mine, row, for_e, message, arrived, started, out, buffer, sems):
+def finish_far_kernel(mine, base, arrived, started, out, buffer, sems):
     del started
-    c = lax.axis_index("gy")
-    core, position = lax.rem(c, 2), lax.rem(c, 4)
-    half = position // 2
+    outer = 3 * (lax.rem(lax.axis_index("gy"), 4) // 2)
     copies = []
     for k, (u, d) in enumerate(FAR):
-        use_mine, use_theirs = masks(mine[...], u, position, core)
         code = mine[u * PAD // 2:u * PAD // 2 + 1]
-        add_arrived = jnp.broadcast_to(code == (1 + half).astype(F32), (B, B))
-        add_inner = jnp.broadcast_to(code == (2 - half).astype(F32), (B, B))
-        for t in range(3):
-            own_row, other_row, inner = far_tiles(core, half, row, for_e, message, k, t)
-            got = arrived[3 * k + t].astype(F32)
-            here = jnp.where(use_mine, own_row, other_row) + jnp.where(add_arrived, got, 0.0)
-            there = got + jnp.where(add_inner, inner, 0.0)
-            buffer[k, t] = jnp.where(jnp.logical_or(use_mine, use_theirs), here, there)
+        add = jnp.broadcast_to(code != outer.astype(F32), (B, B))
+        for t in range(3):
+            buffer[k, t] = base[k, t] + jnp.where(add, arrived[3 * k + t].astype(F32), 0.0)
         copies.append(pltpu.make_async_copy(buffer.at[k], out.at[u, 0, d], sems.at[k]))
         copies[-1].start()
     for copy in copies:
@@ -399,12 +401,14 @@
     (chosen_f,) = call(choose_far_kernel, (wanted, row_f, for_e_f, message_f), [((3 * far,) + bb, BF16)])
     arrived_f = lax.ppermute(chosen_f, "gy", across)
     shape = (2, 1, 3, 3) + bb
+    out, base = call(
+        finish_near_kernel,
+        (mine, row_n, for_e_n, message_n, joint, arrived_n, row_f, for_e_f, message_f),
+        [(shape, F32), ((far, 3) + bb, F32)], out_specs=[HBM, VMEM],
+        scratch=[pltpu.VMEM((near, 3) + bb, F32), pltpu.SemaphoreType.DMA((near,))])
     (out,) = call(
-        finish_near_kernel, (mine, row_n, for_e_n, message_n, joint, arrived_n), [(shape, F32)], out_specs=[HBM],
-        scratch=[pltpu.VMEM((near, 3) + bb, F32), pltpu.SemaphoreType.DMA((near,))], cost=0)
-    (out,) = call(
-        finish_far_kernel, (mine, row_f, for_e_f, message_f, arrived_f, out), [(shape, F32)],
-        in_specs=[VMEM] * 5 + [HBM], out_specs=[HBM], aliases={5: 0},
+        finish_far_kernel, (mine, base, arrived_f, out), [(shape, F32)],
+        in_specs=[VMEM] * 3 + [HBM], out_specs=[HBM], aliases={3: 0},
         scratch=[pltpu.VMEM((far, 3) + bb, F32), pltpu.SemaphoreType.DMA((far,))])
     return out
 

time: 43.2 us -> 43.1 us (level)
  no operation moved by 1% of the time
where the time goes in v12:
time: 43.1 us; the launch traced here: 42.9 us
  starting transfers between devices  25.4 us (59%)
  waiting for transfers between devices  8.72 us (20%)
  Pallas kernels  6.09 us (14%)
  blocking collectives  2.46 us (6%)
    ppermute x1, starting transfers between devices, on_device(): from_east = lax.ppermute(west, 'gx', westward)  12.8 us
    pallas_call x9, Pallas kernels, call(): pl.pallas_call(kernel, in_specs=in_specs or [VMEM] * len(args), out_specs...  6.09 us
    ppermute x1, waiting for transfers between devices, on_device(): arrived_n = lax.ppermute(chosen_n, 'gy', across)  4.58 us
    ppermute x1, starting transfers between devices, on_device(): arrived_f = lax.ppermute(chosen_f, 'gy', across)  3.93 us
    ppermute x1, starting transfers between devices, on_device(): from_west = lax.ppermute(east, 'gx', eastward)  3.48 us
    all_gather x1, blocking collectives, on_device(): message_f = lax.all_gather(message_f, 'gy', axis_index_groups=cores)  2.46 us
    ppermute x1, waiting for transfers between devices, on_device(): arrived_f = lax.ppermute(chosen_f, 'gy', across)  2.4 us
    ppermute x1, starting transfers between devices, on_device(): message_n = lax.ppermute(message_n, 'gy', inside)  1.92 us
  transfers between devices with their start and end apart: 7, of which 3 were waited for; matrix products, arithmetic and copies ran while one was open for 0% of the time, Pallas kernels for 8%

profile of v12, /device:TPU:8, one launch (start us, length us, event | category | flops | bytes accessed | tf_op | source)
XLA Modules:
  0.0 42.9 jit_solution(8546187167066231446)
XLA Ops:
  0.0 1.7 %shard_map.64 = (bf16[2,4,128,128]{3,2,1,0:T(8,128)(2,1)S(1)}, bf16[2,4,5,128,128]{4,3,2,1,0:T(8,128)(2,1)S(1)}, bf16[2,2,128,128]{3,2,1,0:T(8,128)(2,1)S(1)}, b...) custom-call(s32[2,4,4]{2,1,0:T(4,128)} %a_links.1, ...), custom_call_target="tpu_custom_call" | custom-call | tf_op jit(solution)/shard_map/pallas_call | solution.py:21
  1.7 0.7 %collective-permute-start = (bf16[1808,128]{1,0:T(8,128)(2,1)S(1)}, bf16[1808,128]{1,0:T(8,128)(2,1)S(1)}, u32[]{:S(2)}, u32[]{:S(2)}) collective-permute-start(bf16[1808,128]{1,0:T(8,128)(2,1)S(1)} %get-tuple-element.29), channel_id=1, source_target_pairs={{1,2},{3,4},{5,6},{7,8},{9,10},{11,12},{13,14},{15,16},{17,18},{19... | collective-permute-start | bytes 1388552 | tf_op jit(solution)/shard_map/ppermute | solution.py:380
  2.4 3.5 %collective-permute-start.2 = (bf16[6,128,128]{2,1,0:T(8,128)(2,1)S(1)}, bf16[6,128,128]{2,1,0:T(8,128)(2,1)S(1)}, u32[]{:S(2)}, u32[]{:S(2)}) collective-permute-start(bf16[6,128,128]{2,1,0:T(8,128)(2,1)S(1)} %get-tuple-element.33), channel_id=1, source_target_pairs={{0,64},{64,128},{128,192},{192,256},{256,320},{320,384},{384,448},... | collective-permute-start | bytes 589832 | tf_op jit(solution)/shard_map/ppermute | solution.py:381
  5.9 12.8 %collective-permute-start.3 = (bf16[6,128,128]{2,1,0:T(8,128)(2,1)S(1)}, bf16[6,128,128]{2,1,0:T(8,128)(2,1)S(1)}, u32[]{:S(2)}, u32[]{:S(2)}) collective-permute-start(bf16[6,128,128]{2,1,0:T(8,128)(2,1)S(1)} %get-tuple-element.34), channel_id=1, source_target_pairs={{64,0},{128,64},{192,128},{256,192},{320,256},{384,320},{448,384},... | collective-permute-start | bytes 589832 | tf_op jit(solution)/shard_map/ppermute | solution.py:382
  18.7 0.0 collective-permute-done.halo_o
  18.7 1.3 %shard_map.65 = (f32[4,3,128,128]{3,2,1,0:T(8,128)S(1)}, f32[4,2,128,128]{3,2,1,0:T(8,128)S(1)}, bf16[3616,128]{1,0:T(8,128)(2,1)S(1)}) custom-call(bf16[2,4,128,128]{3,2,1,0:T(8,128)(2,1)S(1)} %get-tuple-element.26.own, bf16[2,4,5,128,128]{4,3,2,1,0:T(8,128)(2,1)S(1)} %get-tuple-element.27.a, bf16[2,2,128,128]{3,2,1,0:T(8,128)(2,1)S(1)} %get-tuple-element.28.sides, ...), custom_call_target="tpu_custom_call" | custom-call | tf_op jit(solution)/shard_map/pallas_call | solution.py:21
  20.0 1.9 %collective-permute-start.1 = (bf16[3616,128]{1,0:T(8,128)(2,1)S(1)}, bf16[3616,128]{1,0:T(8,128)(2,1)S(1)}, u32[]{:S(2)}, u32[]{:S(2)}) collective-permute-start(bf16[3616,128]{1,0:T(8,128)(2,1)S(1)} %get-tuple-element.32.sent), channel_id=1, source_target_pairs={{0,1},{2,3},{4,5},{6,7},{8,9},{10,11},{12,13},{14,15},{16,17},{18,... | collective-permute-start | bytes 2777096 | tf_op jit(solution)/shard_map/ppermute | solution.py:387
  21.9 0.0 collective-permute-done.2.from_west
  21.9 0.0 collective-permute-done.3.from_east
  22.0 0.7 %collective-permute-start.5 = (bf16[4,128,128]{2,1,0:T(8,128)(2,1)S(1)}, bf16[4,128,128]{2,1,0:T(8,128)(2,1)S(1)}, u32[]{:S(2)}, u32[]{:S(2)}) collective-permute-start(bf16[4,128,128]{2,1,0:T(8,128)(2,1)S(1)} %shard_map.66.border), channel_id=1, source_target_pairs={{3,4},{7,8},{11,12},{15,16},{19,20},{23,24},{27,28},{31,32},{35,36... | collective-permute-start | bytes 393224 | tf_op jit(solution)/shard_map/ppermute | solution.py:390
  22.6 1.7 %collective-permute-done.1.message = bf16[3616,128]{1,0:T(8,128)(2,1)S(1)} collective-permute-done((bf16[3616,128]{1,0:T(8,128)(2,1)S(1)}, bf16[3616,128]{1,0:T(8,128)(2,1)S(1)}, u32[]{:S(2)}, u32[]{:S(2)}) %collective-permute-start.1) | collective-permute-done | bytes 925728 | tf_op jit(solution)/shard_map/ppermute | solution.py:387
  24.4 0.4 shard_map.67
  24.8 1.9 %collective-permute-start.4 = (bf16[12,128,128]{2,1,0:T(8,128)(2,1)S(1)}, bf16[12,128,128]{2,1,0:T(8,128)(2,1)S(1)}, u32[]{:S(2)}, u32[]{:S(2)}) collective-permute-start(bf16[12,128,128]{2,1,0:T(8,128)(2,1)S(1)} %get-tuple-element.36.chosen), channel_id=1, source_target_pairs={{0,2},{1,3},{2,0},{3,1},{4,6},{5,7},{6,4},{7,5},{8,10},{9,11},{10,... | collective-permute-start | bytes 1179656 | tf_op jit(solution)/shard_map/ppermute | solution.py:394
  26.7 0.7 %shard_map.68 = (f32[2,3,128,128]{3,2,1,0:T(8,128)S(1)}, f32[2,2,128,128]{3,2,1,0:T(8,128)S(1)}, bf16[4,128,128]{2,1,0:T(8,128)(2,1)S(1)}) custom-call(bf16[2,4,128,128]{3,2,1,0:T(8,128)(2,1)S(1)} %get-tuple-element.26.own, bf16[2,4,5,128,128]{4,3,2,1,0:T(8,128)(2,1)S(1)} %get-tuple-element.27.a, bf16[2,2,128,128]{3,2,1,0:T(8,128)(2,1)S(1)} %get-tuple-element.28.sides, ...), custom_call_target="tpu_custom_call" | custom-call | tf_op jit(solution)/shard_map/pallas_call | solution.py:21
  27.4 0.0 collective-permute-done.5.from_group
  27.4 0.1 shard_map.69
  27.5 2.5 %all-gather = bf16[3584,128]{1,0:T(8,128)(2,1)S(1)} all-gather(bf16[1792,128]{1,0:T(8,128)(2,1)S(1)} %get-tuple-element.41), channel_id=2, replica_groups={{0,1},{2,3},{4,5},{6,7},{8,9},{10,11},{12,13},{14,15},{16,17},{18,19},{..., dimensions={0}, use_global_device_ids=true | all-gather | bytes 1376256 | tf_op jit(solution)/shard_map/all_gather | solution.py:400
  30.0 0.1 shard_map.71
  30.1 3.9 %collective-permute-start.6 = (bf16[6,128,128]{2,1,0:T(8,128)(2,1)S(1)}, bf16[6,128,128]{2,1,0:T(8,128)(2,1)S(1)}, u32[]{:S(2)}, u32[]{:S(2)}) collective-permute-start(bf16[6,128,128]{2,1,0:T(8,128)(2,1)S(1)} %shard_map.71), channel_id=1, source_target_pairs={{0,2},{1,3},{2,0},{3,1},{4,6},{5,7},{6,4},{7,5},{8,10},{9,11},{10,... | collective-permute-start | bytes 589832 | tf_op jit(solution)/shard_map/ppermute | solution.py:402
  34.1 4.6 %collective-permute-done.4.arrived = bf16[12,128,128]{2,1,0:T(8,128)(2,1)S(1)} collective-permute-done((bf16[12,128,128]{2,1,0:T(8,128)(2,1)S(1)}, bf16[12,128,128]{2,1,0:T(8,128)(2,1)S(1)}, u32[]{:S(2)}, u32[]{:S(2)}) %collective-permute-start.4) | collective-permute-done | bytes 393248 | tf_op jit(solution)/shard_map/ppermute | solution.py:394
  38.7 1.0 %shard_map.70 = (f32[2,1,3,3,128,128]{5,4,3,2,1,0:T(8,128)}, f32[2,3,128,128]{3,2,1,0:T(8,128)S(1)}) custom-call(f32[16,128]{1,0:T(8,128)S(1)} %get-tuple-element.25.mine, f32[4,3,128,128]{3,2,1,0:T(8,128)S(1)} %get-tuple-element.30.row, f32[4,2,128,128]{3,2,1,0:T(8,128)S(1)} %get-tuple-element.31.for_e, ...), custom_call_target="tpu_custom_call" | custom-call | tf_op jit(solution)/shard_map/pallas_call | solution.py:21
  39.7 2.4 %collective-permute-done.6.arrived = bf16[6,128,128]{2,1,0:T(8,128)(2,1)S(1)} collective-permute-done((bf16[6,128,128]{2,1,0:T(8,128)(2,1)S(1)}, bf16[6,128,128]{2,1,0:T(8,128)(2,1)S(1)}, u32[]{:S(2)}, u32[]{:S(2)}) %collective-permute-start.6) | collective-permute-done | bytes 196640 | tf_op jit(solution)/shard_map/ppermute | solution.py:402
  42.1 0.8 %shard_map.72 = f32[2,1,3,3,128,128]{5,4,3,2,1,0:T(8,128)} custom-call(f32[16,128]{1,0:T(8,128)S(1)} %get-tuple-element.25.mine, f32[2,3,128,128]{3,2,1,0:T(8,128)S(1)} %get-tuple-element.42.base, bf16[6,128,128]{2,1,0:T(8,128)(2,1)S(1)} %collective-permute-done.6.arrived, ...), custom_call_target="tpu_custom_call", output_to_operand_aliasing={{}: (3, {})} | custom-call | tf_op jit(solution)/shard_map/pallas_call | solution.py:21
  (1 shorter events, 0.0 us)
Async XLA Ops:
  1.7 17.0 %collective-permute-start = (bf16[1808,128]{1,0:T(8,128)(2,1)S(1)}, bf16[1808,128]{1,0:T(8,128)(2,1)S(1)}, u32[]{:S(2)}, u32[]{:S(2)}) collective-permute-start(bf16[1808,128]{1,0:T(8,128)(2,1)S(1)} %get-tuple-element.29), channel_id=1, source_target_pairs={{1,2},{3,4},{5,6},{7,8},{9,10},{11,12},{13,14},{15,16},{17,18},{19... | collective-permute-start | bytes 1388552 | tf_op jit(solution)/shard_map/ppermute | solution.py:380
  2.4 19.5 %collective-permute-start.2 = (bf16[6,128,128]{2,1,0:T(8,128)(2,1)S(1)}, bf16[6,128,128]{2,1,0:T(8,128)(2,1)S(1)}, u32[]{:S(2)}, u32[]{:S(2)}) collective-permute-start(bf16[6,128,128]{2,1,0:T(8,128)(2,1)S(1)} %get-tuple-element.33), channel_id=1, source_target_pairs={{0,64},{64,128},{128,192},{192,256},{256,320},{320,384},{384,448},... | collective-permute-start | bytes 589832 | tf_op jit(solution)/shard_map/ppermute | solution.py:381
  5.9 16.1 %collective-permute-start.3 = (bf16[6,128,128]{2,1,0:T(8,128)(2,1)S(1)}, bf16[6,128,128]{2,1,0:T(8,128)(2,1)S(1)}, u32[]{:S(2)}, u32[]{:S(2)}) collective-permute-start(bf16[6,128,128]{2,1,0:T(8,128)(2,1)S(1)} %get-tuple-element.34), channel_id=1, source_target_pairs={{64,0},{128,64},{192,128},{256,192},{320,256},{384,320},{448,384},... | collective-permute-start | bytes 589832 | tf_op jit(solution)/shard_map/ppermute | solution.py:382
  20.0 4.4 %collective-permute-start.1 = (bf16[3616,128]{1,0:T(8,128)(2,1)S(1)}, bf16[3616,128]{1,0:T(8,128)(2,1)S(1)}, u32[]{:S(2)}, u32[]{:S(2)}) collective-permute-start(bf16[3616,128]{1,0:T(8,128)(2,1)S(1)} %get-tuple-element.32.sent), channel_id=1, source_target_pairs={{0,1},{2,3},{4,5},{6,7},{8,9},{10,11},{12,13},{14,15},{16,17},{18,... | collective-permute-start | bytes 2777096 | tf_op jit(solution)/shard_map/ppermute | solution.py:387
  22.0 5.5 %collective-permute-start.5 = (bf16[4,128,128]{2,1,0:T(8,128)(2,1)S(1)}, bf16[4,128,128]{2,1,0:T(8,128)(2,1)S(1)}, u32[]{:S(2)}, u32[]{:S(2)}) collective-permute-start(bf16[4,128,128]{2,1,0:T(8,128)(2,1)S(1)} %shard_map.66.border), channel_id=1, source_target_pairs={{3,4},{7,8},{11,12},{15,16},{19,20},{23,24},{27,28},{31,32},{35,36... | collective-permute-start | bytes 393224 | tf_op jit(solution)/shard_map/ppermute | solution.py:390
  24.8 13.9 %collective-permute-start.4 = (bf16[12,128,128]{2,1,0:T(8,128)(2,1)S(1)}, bf16[12,128,128]{2,1,0:T(8,128)(2,1)S(1)}, u32[]{:S(2)}, u32[]{:S(2)}) collective-permute-start(bf16[12,128,128]{2,1,0:T(8,128)(2,1)S(1)} %get-tuple-element.36.chosen), channel_id=1, source_target_pairs={{0,2},{1,3},{2,0},{3,1},{4,6},{5,7},{6,4},{7,5},{8,10},{9,11},{10,... | collective-permute-start | bytes 1179656 | tf_op jit(solution)/shard_map/ppermute | solution.py:394
  30.1 11.9 %collective-permute-start.6 = (bf16[6,128,128]{2,1,0:T(8,128)(2,1)S(1)}, bf16[6,128,128]{2,1,0:T(8,128)(2,1)S(1)}, u32[]{:S(2)}, u32[]{:S(2)}) collective-permute-start(bf16[6,128,128]{2,1,0:T(8,128)(2,1)S(1)} %shard_map.71), channel_id=1, source_target_pairs={{0,2},{1,3},{2,0},{3,1},{4,6},{5,7},{6,4},{7,5},{8,10},{9,11},{10,... | collective-permute-start | bytes 589832 | tf_op jit(solution)/shard_map/ppermute | solution.py:402
